TPU v7x, 128 devices: a whole 4x4x4 slice. The times are simulated.
128 devices in a mesh: ha: 16 (over x, y), wa: 8 (over z, core).
Axes of the slice: x: 4, y: 4, z: 4, core: 2. Of those that a mesh axis runs over, the one named last changes fastest.
Arguments:
- features: bfloat16 [16, 64, 64, 384], P(None, 'ha', 'wa'), may hold values from -6 to 6
- cache_first: bfloat16 [2, 64, 64, 384], P(None, 'ha', 'wa'), may hold values from -4 to 4
- cache_second: bfloat16 [2, 64, 64, 384], P(None, 'ha', 'wa'), may hold values from -4 to 4
- cache_head: bfloat16 [2, 64, 64, 384], P(None, 'ha', 'wa'), may hold values from -4 to 4
- gain_first: float32 [384], replicated, may hold values from 0.1 to 1.9
- gain_second: float32 [384], replicated, may hold values from 0.1 to 1.9
- gain_head: float32 [384], replicated, may hold values from 0.1 to 1.9
- conv_first: bfloat16 [3, 3, 3, 384, 384], replicated, may hold values from -0.0625 to 0.0625
- conv_second: bfloat16 [3, 3, 3, 384, 384], replicated, may hold values from -0.0625 to 0.0625
- conv_head: bfloat16 [3, 3, 3, 384, 32], replicated, may hold values from -0.0625 to 0.0625
- bias_first: float32 [384], replicated, may hold values from -3 to 3
- bias_second: float32 [384], replicated, may hold values from -3 to 3
- bias_head: float32 [32], replicated, may hold values from -3 to 3
Outputs:
- latent_tokens: bfloat16 [16384, 128], P(('ha', 'wa'))
All inputs are finite; a program needn't handle non-finite values.
Results may differ from a plain program's by a relative error of at most 0.014.
Values may be sent and summed in bfloat16 or wider, within the bound.
No kernel may reach another device: no remote copies, remote signals or barrier semaphores. Data moves between devices by JAX's collectives and lax.ppermute only.
A program may use at most 192 MiB of HBM per device.

v0:
```python
import jax
import jax.numpy as jnp
from jax import lax
from jax.sharding import PartitionSpec as P


def padded_2(block, sides, width):
    for axis, dim in sides:
        count = lax.axis_size(axis)
        forward = [(i, i + 1) for i in range(count - 1)]
        backward = [(target, source) for source, target in forward]
        low = lax.ppermute(
            lax.slice_in_dim(block, block.shape[dim] - width, None, axis=dim), axis, forward
        )
        high = lax.ppermute(lax.slice_in_dim(block, 0, width, axis=dim), axis, backward)
        block = jnp.concatenate([low, block, high], axis=dim)
    return block


def activate(values, gain):
    wide = values.astype(jnp.float32)
    scale = lax.rsqrt(jnp.mean(wide * wide, axis=-1, keepdims=True) + 1e-06)
    return jax.nn.silu(wide * scale * gain).astype(jnp.bfloat16)


def causal_conv(padded, weight, frames, rows, cols):
    width_in = padded.shape[-1]
    out_width = weight.shape[-1]
    stacked = jnp.concatenate([padded[:, :, w_off : w_off + cols] for w_off in range(3)], axis=-1)
    total = jnp.zeros((frames * rows * cols, out_width), jnp.float32)
    for t_off in range(3):
        for h_off in range(3):
            taken = stacked[t_off : t_off + frames, h_off : h_off + rows].reshape(-1, 3 * width_in)
            kernel = weight[t_off, h_off].reshape(3 * width_in, out_width)
            total = total + jnp.dot(taken, kernel, preferred_element_type=jnp.float32)
    return total.reshape(frames, rows, cols, out_width)


def local(
    features,
    cache_first,
    cache_second,
    cache_head,
    gain_first,
    gain_second,
    gain_head,
    conv_first,
    conv_second,
    conv_head,
    bias_first,
    bias_second,
    bias_head,
):
    frames, rows, cols = (features.shape[0], features.shape[1], features.shape[2])
    first_in = jnp.concatenate([cache_first, activate(features, gain_first)], axis=0)
    first_pad = padded_2(first_in, (("ha", 1), ("wa", 2)), 1)
    hidden = (causal_conv(first_pad, conv_first, frames, rows, cols) + bias_first).astype(
        jnp.bfloat16
    )
    second_in = jnp.concatenate([cache_second, activate(hidden, gain_second)], axis=0)
    second_pad = padded_2(second_in, (("ha", 1), ("wa", 2)), 1)
    block_out = (
        causal_conv(second_pad, conv_second, frames, rows, cols)
        + bias_second
        + features.astype(jnp.float32)
    ).astype(jnp.bfloat16)
    head_in = jnp.concatenate([cache_head, activate(block_out, gain_head)], axis=0)
    head_pad = padded_2(head_in, (("ha", 1), ("wa", 2)), 1)
    head = causal_conv(head_pad, conv_head, frames, rows, cols) + bias_head
    moment_count = head.shape[-1]
    moments = head.astype(jnp.bfloat16).reshape(frames, rows // 2, 2, cols // 2, 2, moment_count)
    patches = jnp.transpose(moments, (0, 1, 3, 2, 4, 5)).reshape(
        frames, rows // 2, cols // 2, 4 * moment_count
    )
    frame_block = lax.all_to_all(patches, "ha", split_axis=0, concat_axis=1, tiled=True)
    flat_rows = frame_block.reshape(
        frame_block.shape[0] * frame_block.shape[1], cols // 2, 4 * moment_count
    )
    token_block = lax.all_to_all(flat_rows, "wa", split_axis=0, concat_axis=1, tiled=True)
    return token_block.reshape(token_block.shape[0] * token_block.shape[1], 4 * moment_count)


def solution(mesh):
    placed = (
        P(None, "ha", "wa", None),
        P(None, "ha", "wa", None),
        P(None, "ha", "wa", None),
        P(None, "ha", "wa", None),
        P(),
        P(),
        P(),
        P(),
        P(),
        P(),
        P(),
        P(),
        P(),
    )
    return jax.shard_map(
        local, mesh=mesh, in_specs=placed, out_specs=P(("ha", "wa"), None), check_vma=False
    )
```

profile of v0, /device:TPU:1, one launch (start us, length us, event | category | flops | bytes accessed | tf_op | source)
XLA Modules:
  0.0 120.6 jit_solution(13276235688160866735)
XLA Ops:
  1.2 1.3 %fusion.42 = bf16[16,4,8,384]{3,2,1,0:T(8,128)(2,1)S(1)} fusion(bf16[16,4,8,384]{3,2,1,0:T(8,128)(2,1)} %param.13, f32[384]{0:T(512)} %param.17, f32[16,4,8]{2,1,0:T(4,128)S(1)} %add_rsqrt_fusion.1), kind=kLoop, calls=%fused_computation.74 | loop fusion | flops 1572864 | bytes 790016 | tf_op jit(solution)/shard_map/convert_element_type | solution.py:23
  3.3 4.0 %collective-permute-start = (bf16[18,1,8,384]{3,2,1,0:T(8,128)(2,1)S(1)}, bf16[18,1,8,384]{3,2,1,0:T(8,128)(2,1)S(1)}, u32[]{:S(2)}, u32[]{:S(2)}) collective-permute-start(bf16[18,1,8,384]{3,2,1,0:T(8,128)(2,1)S(1)} %get-tuple-element.71), channel_id=1, source_target_pairs={{0,8},{8,16},{16,24},{24,32},{32,40},{40,48},{48,56},{56,64},{64,7... | collective-permute-start | bytes 331784 | tf_op jit(solution)/shard_map/ppermute | solution.py:12
  7.3 1.3 %collective-permute-start.1 = (bf16[18,1,8,384]{3,2,1,0:T(8,128)(2,1)S(1)}, bf16[18,1,8,384]{3,2,1,0:T(8,128)(2,1)S(1)}, u32[]{:S(2)}, u32[]{:S(2)}) collective-permute-start(bf16[18,1,8,384]{3,2,1,0:T(8,128)(2,1)S(1)} %get-tuple-element.72), channel_id=1, source_target_pairs={{8,0},{16,8},{24,16},{32,24},{40,32},{48,40},{56,48},{64,56},{72,6... | collective-permute-start | bytes 331784 | tf_op jit(solution)/shard_map/ppermute | solution.py:15
  9.0 3.8 %collective-permute-done.1 = bf16[18,1,8,384]{3,2,1,0:T(8,128)(2,1)S(1)} collective-permute-done((bf16[18,1,8,384]{3,2,1,0:T(8,128)(2,1)S(1)}, bf16[18,1,8,384]{3,2,1,0:T(8,128)(2,1)S(1)}, u32[]{:S(2)}, u32[]{:S(2)}) %collective-permute-start.1) | collective-permute-done | bytes 110624 | tf_op jit(solution)/shard_map/ppermute | solution.py:15
  13.1 5.5 %collective-permute-start.2 = (bf16[18,6,1,384]{3,1,2,0:T(8,128)(2,1)S(1)}, bf16[18,6,1,384]{3,1,2,0:T(8,128)(2,1)S(1)}, u32[]{:S(2)}, u32[]{:S(2)}) collective-permute-start(bf16[18,6,1,384]{3,1,2,0:T(8,128)(2,1)S(1)} %copy.61), channel_id=1, source_target_pairs={{0,1},{1,2},{2,3},{3,4},{4,5},{5,6},{6,7},{8,9},{9,10},{10,11},{11... | collective-permute-start | bytes 248840 | tf_op jit(solution)/shard_map/ppermute | solution.py:12
  18.6 1.9 %collective-permute-start.3 = (bf16[18,6,1,384]{3,1,2,0:T(8,128)(2,1)S(1)}, bf16[18,6,1,384]{3,1,2,0:T(8,128)(2,1)S(1)}, u32[]{:S(2)}, u32[]{:S(2)}) collective-permute-start(bf16[18,6,1,384]{3,1,2,0:T(8,128)(2,1)S(1)} %copy.63), channel_id=1, source_target_pairs={{1,0},{2,1},{3,2},{4,3},{5,4},{6,5},{7,6},{9,8},{10,9},{11,10},{12... | collective-permute-start | bytes 248840 | tf_op jit(solution)/shard_map/ppermute | solution.py:15
  20.6 4.0 %fusion.47 = (bf16[1,1,3,384,384]{4,3,2,1,0:T(8,128)(2,1)S(1)}, bf16[1,1,3,384,384]{4,3,2,1,0:T(8,128)(2,1)S(1)}, bf16[1,1,3,384,384]{4,3,2,1,0:T(8,128)(2,1)S(1...) fusion(bf16[3,3,3,384,384]{4,3,2,1,0:T(8,128)(2,1)} %param.20), kind=kLoop, calls=%fused_computation.104 | loop fusion | bytes 15925248 | tf_op jit(solution)/shard_map/slice | solution.py:34
  24.9 1.6 %fusion.4 = bf16[18,6,8,1152]{3,2,1,0:T(8,128)(2,1)S(1)} fusion(bf16[18,6,1,384]{3,2,1,0:T(2,128)(2,1)S(1)} %copy.64, bf16[18,1,8,384]{3,2,1,0:T(8,128)(2,1)S(1)} %collective-permute-done.1, bf16[18,1,8,384]{3,2,1,0:T(8,128)(2,1)S(1)} %collective-permute-done, bf16[16,4,8,384]{3,2,1,0:T(8,128)(2,1)S(1)} %fusion.42, bf16[2,4,8,384]{3,2,1,0:T(8,128)(2,1)S(1)} %copy-done.2, ...), kind=kLoop, calls=%fused_computation.21 | loop fusion | flops 27869184 | bytes 2820096 | tf_op jit(solution)/shard_map/concatenate | solution.py:29
  35.7 3.2 %collective-permute-start.4 = (bf16[18,1,8,384]{3,2,1,0:T(8,128)(2,1)S(1)}, bf16[18,1,8,384]{3,2,1,0:T(8,128)(2,1)S(1)}, u32[]{:S(2)}, u32[]{:S(2)}) collective-permute-start(bf16[18,1,8,384]{3,2,1,0:T(8,128)(2,1)S(1)} %get-tuple-element.69), channel_id=1, source_target_pairs={{0,8},{8,16},{16,24},{24,32},{32,40},{40,48},{48,56},{56,64},{64,7... | collective-permute-start | bytes 331784 | tf_op jit(solution)/shard_map/ppermute | solution.py:12
  38.9 1.3 %collective-permute-start.5 = (bf16[18,1,8,384]{3,2,1,0:T(8,128)(2,1)S(1)}, bf16[18,1,8,384]{3,2,1,0:T(8,128)(2,1)S(1)}, u32[]{:S(2)}, u32[]{:S(2)}) collective-permute-start(bf16[18,1,8,384]{3,2,1,0:T(8,128)(2,1)S(1)} %get-tuple-element.70), channel_id=1, source_target_pairs={{8,0},{16,8},{24,16},{32,24},{40,32},{48,40},{56,48},{64,56},{72,6... | collective-permute-start | bytes 331784 | tf_op jit(solution)/shard_map/ppermute | solution.py:15
  40.6 3.8 %collective-permute-done.5 = bf16[18,1,8,384]{3,2,1,0:T(8,128)(2,1)S(1)} collective-permute-done((bf16[18,1,8,384]{3,2,1,0:T(8,128)(2,1)S(1)}, bf16[18,1,8,384]{3,2,1,0:T(8,128)(2,1)S(1)}, u32[]{:S(2)}, u32[]{:S(2)}) %collective-permute-start.5) | collective-permute-done | bytes 110624 | tf_op jit(solution)/shard_map/ppermute | solution.py:15
  44.6 5.3 %collective-permute-start.6 = (bf16[18,6,1,384]{3,1,2,0:T(8,128)(2,1)S(1)}, bf16[18,6,1,384]{3,1,2,0:T(8,128)(2,1)S(1)}, u32[]{:S(2)}, u32[]{:S(2)}) collective-permute-start(bf16[18,6,1,384]{3,1,2,0:T(8,128)(2,1)S(1)} %copy.65), channel_id=1, source_target_pairs={{0,1},{1,2},{2,3},{3,4},{4,5},{5,6},{6,7},{8,9},{9,10},{10,11},{11... | collective-permute-start | bytes 248840 | tf_op jit(solution)/shard_map/ppermute | solution.py:12
  50.0 2.1 %collective-permute-start.7 = (bf16[18,6,1,384]{3,1,2,0:T(8,128)(2,1)S(1)}, bf16[18,6,1,384]{3,1,2,0:T(8,128)(2,1)S(1)}, u32[]{:S(2)}, u32[]{:S(2)}) collective-permute-start(bf16[18,6,1,384]{3,1,2,0:T(8,128)(2,1)S(1)} %copy.67), channel_id=1, source_target_pairs={{1,0},{2,1},{3,2},{4,3},{5,4},{6,5},{7,6},{9,8},{10,9},{11,10},{12... | collective-permute-start | bytes 248840 | tf_op jit(solution)/shard_map/ppermute | solution.py:15
  52.1 4.0 %fusion.46 = (bf16[1,1,3,384,384]{4,3,2,1,0:T(8,128)(2,1)S(1)}, bf16[1,1,3,384,384]{4,3,2,1,0:T(8,128)(2,1)S(1)}, bf16[1,1,3,384,384]{4,3,2,1,0:T(8,128)(2,1)S(1...) fusion(bf16[3,3,3,384,384]{4,3,2,1,0:T(8,128)(2,1)} %param.21), kind=kLoop, calls=%fused_computation.103 | loop fusion | bytes 15925248 | tf_op jit(solution)/shard_map/slice | solution.py:34
  56.4 1.6 %fusion.2 = bf16[18,6,8,1152]{3,2,1,0:T(8,128)(2,1)S(1)} fusion(bf16[18,6,1,384]{3,2,1,0:T(2,128)(2,1)S(1)} %copy.68, bf16[18,1,8,384]{3,2,1,0:T(8,128)(2,1)S(1)} %collective-permute-done.5, bf16[18,1,8,384]{3,2,1,0:T(8,128)(2,1)S(1)} %collective-permute-done.4, bf16[16,4,8,384]{3,2,1,0:T(8,128)(2,1)S(1)} %multiply_convert_fusion, ...), kind=kLoop, calls=%fused_computation.11 | loop fusion | flops 27869184 | bytes 2820096 | tf_op jit(solution)/shard_map/concatenate | solution.py:29
  67.5 4.4 %collective-permute-start.8 = (bf16[18,1,8,384]{3,2,1,0:T(8,128)(2,1)S(1)}, bf16[18,1,8,384]{3,2,1,0:T(8,128)(2,1)S(1)}, u32[]{:S(2)}, u32[]{:S(2)}) collective-permute-start(bf16[18,1,8,384]{3,2,1,0:T(8,128)(2,1)S(1)} %get-tuple-element.67), channel_id=1, source_target_pairs={{0,8},{8,16},{16,24},{24,32},{32,40},{40,48},{48,56},{56,64},{64,7... | collective-permute-start | bytes 331784 | tf_op jit(solution)/shard_map/ppermute | solution.py:12
  71.9 1.3 %collective-permute-start.9 = (bf16[18,1,8,384]{3,2,1,0:T(8,128)(2,1)S(1)}, bf16[18,1,8,384]{3,2,1,0:T(8,128)(2,1)S(1)}, u32[]{:S(2)}, u32[]{:S(2)}) collective-permute-start(bf16[18,1,8,384]{3,2,1,0:T(8,128)(2,1)S(1)} %get-tuple-element.68), channel_id=1, source_target_pairs={{8,0},{16,8},{24,16},{32,24},{40,32},{48,40},{56,48},{64,56},{72,6... | collective-permute-start | bytes 331784 | tf_op jit(solution)/shard_map/ppermute | solution.py:15
  73.7 3.8 %collective-permute-done.9 = bf16[18,1,8,384]{3,2,1,0:T(8,128)(2,1)S(1)} collective-permute-done((bf16[18,1,8,384]{3,2,1,0:T(8,128)(2,1)S(1)}, bf16[18,1,8,384]{3,2,1,0:T(8,128)(2,1)S(1)}, u32[]{:S(2)}, u32[]{:S(2)}) %collective-permute-start.9) | collective-permute-done | bytes 110624 | tf_op jit(solution)/shard_map/ppermute | solution.py:15
  77.7 5.1 %collective-permute-start.10 = (bf16[18,6,1,384]{3,1,2,0:T(8,128)(2,1)S(1)}, bf16[18,6,1,384]{3,1,2,0:T(8,128)(2,1)S(1)}, u32[]{:S(2)}, u32[]{:S(2)}) collective-permute-start(bf16[18,6,1,384]{3,1,2,0:T(8,128)(2,1)S(1)} %copy.69), channel_id=1, source_target_pairs={{0,1},{1,2},{2,3},{3,4},{4,5},{5,6},{6,7},{8,9},{9,10},{10,11},{11... | collective-permute-start | bytes 248840 | tf_op jit(solution)/shard_map/ppermute | solution.py:12
  82.8 1.9 %collective-permute-start.11 = (bf16[18,6,1,384]{3,1,2,0:T(8,128)(2,1)S(1)}, bf16[18,6,1,384]{3,1,2,0:T(8,128)(2,1)S(1)}, u32[]{:S(2)}, u32[]{:S(2)}) collective-permute-start(bf16[18,6,1,384]{3,1,2,0:T(8,128)(2,1)S(1)} %copy.71), channel_id=1, source_target_pairs={{1,0},{2,1},{3,2},{4,3},{5,4},{6,5},{7,6},{9,8},{10,9},{11,10},{12... | collective-permute-start | bytes 248840 | tf_op jit(solution)/shard_map/ppermute | solution.py:15
  85.7 3.2 %collective-permute-done.11 = bf16[18,6,1,384]{3,1,2,0:T(8,128)(2,1)S(1)} collective-permute-done((bf16[18,6,1,384]{3,1,2,0:T(8,128)(2,1)S(1)}, bf16[18,6,1,384]{3,1,2,0:T(8,128)(2,1)S(1)}, u32[]{:S(2)}, u32[]{:S(2)}) %collective-permute-start.11) | collective-permute-done | bytes 82976 | tf_op jit(solution)/shard_map/ppermute | solution.py:15
  89.0 1.6 %fusion = bf16[18,6,8,1152]{3,2,1,0:T(8,128)(2,1)S(1)} fusion(bf16[18,6,1,384]{3,2,1,0:T(2,128)(2,1)S(1)} %copy.72, bf16[18,1,8,384]{3,2,1,0:T(8,128)(2,1)S(1)} %collective-permute-done.9, bf16[18,1,8,384]{3,2,1,0:T(8,128)(2,1)S(1)} %collective-permute-done.8, bf16[16,4,8,384]{3,2,1,0:T(8,128)(2,1)S(1)} %fusion.34, bf16[2,4,8,384]{3,2,1,0:T(8,128)(2,1)S(1)} %copy-done.4, ...), kind=kLoop, calls=%fused_computation.1 | loop fusion | flops 27869184 | bytes 2820096 | tf_op jit(solution)/shard_map/concatenate | solution.py:29
  96.4 14.6 %all_to_all.24 = bf16[16,2,4,128]{3,2,1,0:T(4,128)(2,1)S(1)} all-to-all(bf16[16,2,4,128]{3,2,1,0:T(4,128)(2,1)S(1)} %reshape.178), channel_id=1, replica_groups=mesh['ha'=16,'wa'=8] {'ha'}, dimensions={0} | all-to-all | bytes 65536 | tf_op jit(solution)/shard_map/all_to_all | solution.py:75
  111.0 8.9 %all_to_all.25 = bf16[32,4,128]{2,1,0:T(4,128)(2,1)S(1)} all-to-all(bf16[32,4,128]{2,1,0:T(4,128)(2,1)S(1)} %bitcast.220), channel_id=1, replica_groups=mesh['ha'=16,'wa'=8] {'wa'}, dimensions={0} | all-to-all | bytes 65536 | tf_op jit(solution)/shard_map/all_to_all | solution.py:79
  (109 shorter events, 30.3 us)
Async XLA Ops:
  0.0 12.8 %copy-start.2 = (bf16[2,4,8,384]{3,2,1,0:T(8,128)(2,1)S(1)}, bf16[2,4,8,384]{3,2,1,0:T(8,128)(2,1)}, u32[]{:S(2)}) copy-start(bf16[2,4,8,384]{3,2,1,0:T(8,128)(2,1)} %param.14) | copy-start | bytes 147460
  3.3 5.8 %collective-permute-start = (bf16[18,1,8,384]{3,2,1,0:T(8,128)(2,1)S(1)}, bf16[18,1,8,384]{3,2,1,0:T(8,128)(2,1)S(1)}, u32[]{:S(2)}, u32[]{:S(2)}) collective-permute-start(bf16[18,1,8,384]{3,2,1,0:T(8,128)(2,1)S(1)} %get-tuple-element.71), channel_id=1, source_target_pairs={{0,8},{8,16},{16,24},{24,32},{32,40},{40,48},{48,56},{56,64},{64,7... | collective-permute-start | bytes 331784 | tf_op jit(solution)/shard_map/ppermute | solution.py:12
  7.3 5.5 %collective-permute-start.1 = (bf16[18,1,8,384]{3,2,1,0:T(8,128)(2,1)S(1)}, bf16[18,1,8,384]{3,2,1,0:T(8,128)(2,1)S(1)}, u32[]{:S(2)}, u32[]{:S(2)}) collective-permute-start(bf16[18,1,8,384]{3,2,1,0:T(8,128)(2,1)S(1)} %get-tuple-element.72), channel_id=1, source_target_pairs={{8,0},{16,8},{24,16},{32,24},{40,32},{48,40},{56,48},{64,56},{72,6... | collective-permute-start | bytes 331784 | tf_op jit(solution)/shard_map/ppermute | solution.py:15
  13.1 11.5 %collective-permute-start.2 = (bf16[18,6,1,384]{3,1,2,0:T(8,128)(2,1)S(1)}, bf16[18,6,1,384]{3,1,2,0:T(8,128)(2,1)S(1)}, u32[]{:S(2)}, u32[]{:S(2)}) collective-permute-start(bf16[18,6,1,384]{3,1,2,0:T(8,128)(2,1)S(1)} %copy.61), channel_id=1, source_target_pairs={{0,1},{1,2},{2,3},{3,4},{4,5},{5,6},{6,7},{8,9},{9,10},{10,11},{11... | collective-permute-start | bytes 248840 | tf_op jit(solution)/shard_map/ppermute | solution.py:12
  18.6 6.1 %collective-permute-start.3 = (bf16[18,6,1,384]{3,1,2,0:T(8,128)(2,1)S(1)}, bf16[18,6,1,384]{3,1,2,0:T(8,128)(2,1)S(1)}, u32[]{:S(2)}, u32[]{:S(2)}) collective-permute-start(bf16[18,6,1,384]{3,1,2,0:T(8,128)(2,1)S(1)} %copy.63), channel_id=1, source_target_pairs={{1,0},{2,1},{3,2},{4,3},{5,4},{6,5},{7,6},{9,8},{10,9},{11,10},{12... | collective-permute-start | bytes 248840 | tf_op jit(solution)/shard_map/ppermute | solution.py:15
  33.2 0.8 copy-start.5
  34.1 1.2 %copy-start.6 = (f32[384]{0:T(512)S(1)}, f32[384]{0:T(512)}, u32[]{:S(2)}) copy-start(f32[384]{0:T(512)} %param.18) | copy-start | bytes 4612
  34.1 1.5 %copy-start.3 = (bf16[2,4,8,384]{3,2,1,0:T(8,128)(2,1)S(1)}, bf16[2,4,8,384]{3,2,1,0:T(8,128)(2,1)}, u32[]{:S(2)}) copy-start(bf16[2,4,8,384]{3,2,1,0:T(8,128)(2,1)} %param.15) | copy-start | bytes 147460
  35.7 4.9 %collective-permute-start.4 = (bf16[18,1,8,384]{3,2,1,0:T(8,128)(2,1)S(1)}, bf16[18,1,8,384]{3,2,1,0:T(8,128)(2,1)S(1)}, u32[]{:S(2)}, u32[]{:S(2)}) collective-permute-start(bf16[18,1,8,384]{3,2,1,0:T(8,128)(2,1)S(1)} %get-tuple-element.69), channel_id=1, source_target_pairs={{0,8},{8,16},{16,24},{24,32},{32,40},{40,48},{48,56},{56,64},{64,7... | collective-permute-start | bytes 331784 | tf_op jit(solution)/shard_map/ppermute | solution.py:12
  38.9 5.5 %collective-permute-start.5 = (bf16[18,1,8,384]{3,2,1,0:T(8,128)(2,1)S(1)}, bf16[18,1,8,384]{3,2,1,0:T(8,128)(2,1)S(1)}, u32[]{:S(2)}, u32[]{:S(2)}) collective-permute-start(bf16[18,1,8,384]{3,2,1,0:T(8,128)(2,1)S(1)} %get-tuple-element.70), channel_id=1, source_target_pairs={{8,0},{16,8},{24,16},{32,24},{40,32},{48,40},{56,48},{64,56},{72,6... | collective-permute-start | bytes 331784 | tf_op jit(solution)/shard_map/ppermute | solution.py:15
  44.6 11.5 %collective-permute-start.6 = (bf16[18,6,1,384]{3,1,2,0:T(8,128)(2,1)S(1)}, bf16[18,6,1,384]{3,1,2,0:T(8,128)(2,1)S(1)}, u32[]{:S(2)}, u32[]{:S(2)}) collective-permute-start(bf16[18,6,1,384]{3,1,2,0:T(8,128)(2,1)S(1)} %copy.65), channel_id=1, source_target_pairs={{0,1},{1,2},{2,3},{3,4},{4,5},{5,6},{6,7},{8,9},{9,10},{10,11},{11... | collective-permute-start | bytes 248840 | tf_op jit(solution)/shard_map/ppermute | solution.py:12
  50.0 6.3 %collective-permute-start.7 = (bf16[18,6,1,384]{3,1,2,0:T(8,128)(2,1)S(1)}, bf16[18,6,1,384]{3,1,2,0:T(8,128)(2,1)S(1)}, u32[]{:S(2)}, u32[]{:S(2)}) collective-permute-start(bf16[18,6,1,384]{3,1,2,0:T(8,128)(2,1)S(1)} %copy.67), channel_id=1, source_target_pairs={{1,0},{2,1},{3,2},{4,3},{5,4},{6,5},{7,6},{9,8},{10,9},{11,10},{12... | collective-permute-start | bytes 248840 | tf_op jit(solution)/shard_map/ppermute | solution.py:15
  65.6 1.1 copy-start
  65.6 1.1 copy-start.7
  65.6 1.4 %copy-start.8 = (f32[384]{0:T(512)S(1)}, f32[384]{0:T(512)}, u32[]{:S(2)}) copy-start(f32[384]{0:T(512)} %param.19) | copy-start | bytes 4612
  66.7 0.8 copy-start.4
  66.7 18.0 %copy-start.1 = (bf16[3,3,3,384,32]{3,4,2,1,0:T(8,128)(2,1)S(1)}, bf16[3,3,3,384,32]{3,4,2,1,0:T(8,128)(2,1)}, u32[]{:S(2)}) copy-start(bf16[3,3,3,384,32]{3,4,2,1,0:T(8,128)(2,1)} %param.22) | copy-start | bytes 1990660
  67.5 6.2 %collective-permute-start.8 = (bf16[18,1,8,384]{3,2,1,0:T(8,128)(2,1)S(1)}, bf16[18,1,8,384]{3,2,1,0:T(8,128)(2,1)S(1)}, u32[]{:S(2)}, u32[]{:S(2)}) collective-permute-start(bf16[18,1,8,384]{3,2,1,0:T(8,128)(2,1)S(1)} %get-tuple-element.67), channel_id=1, source_target_pairs={{0,8},{8,16},{16,24},{24,32},{32,40},{40,48},{48,56},{56,64},{64,7... | collective-permute-start | bytes 331784 | tf_op jit(solution)/shard_map/ppermute | solution.py:12
  71.9 5.5 %collective-permute-start.9 = (bf16[18,1,8,384]{3,2,1,0:T(8,128)(2,1)S(1)}, bf16[18,1,8,384]{3,2,1,0:T(8,128)(2,1)S(1)}, u32[]{:S(2)}, u32[]{:S(2)}) collective-permute-start(bf16[18,1,8,384]{3,2,1,0:T(8,128)(2,1)S(1)} %get-tuple-element.68), channel_id=1, source_target_pairs={{8,0},{16,8},{24,16},{32,24},{40,32},{48,40},{56,48},{64,56},{72,6... | collective-permute-start | bytes 331784 | tf_op jit(solution)/shard_map/ppermute | solution.py:15
  77.7 7.9 %collective-permute-start.10 = (bf16[18,6,1,384]{3,1,2,0:T(8,128)(2,1)S(1)}, bf16[18,6,1,384]{3,1,2,0:T(8,128)(2,1)S(1)}, u32[]{:S(2)}, u32[]{:S(2)}) collective-permute-start(bf16[18,6,1,384]{3,1,2,0:T(8,128)(2,1)S(1)} %copy.69), channel_id=1, source_target_pairs={{0,1},{1,2},{2,3},{3,4},{4,5},{5,6},{6,7},{8,9},{9,10},{10,11},{11... | collective-permute-start | bytes 248840 | tf_op jit(solution)/shard_map/ppermute | solution.py:12
  82.8 6.1 %collective-permute-start.11 = (bf16[18,6,1,384]{3,1,2,0:T(8,128)(2,1)S(1)}, bf16[18,6,1,384]{3,1,2,0:T(8,128)(2,1)S(1)}, u32[]{:S(2)}, u32[]{:S(2)}) collective-permute-start(bf16[18,6,1,384]{3,1,2,0:T(8,128)(2,1)S(1)} %copy.71), channel_id=1, source_target_pairs={{1,0},{2,1},{3,2},{4,3},{5,4},{6,5},{7,6},{9,8},{10,9},{11,10},{12... | collective-permute-start | bytes 248840 | tf_op jit(solution)/shard_map/ppermute | solution.py:15
  95.0 1.1 copy-start.9
where the time goes:
time: 121 us
  starting transfers between devices  37.4 us (31%)
  blocking collectives  23.5 us (19%)
  matrix products  19 us (16%)
  waiting for transfers between devices  15.8 us (13%)
  local copies, waits for them, and re-layouts  14.4 us (12%)
  other arithmetic  9.65 us (8%)
    ppermute x6, starting transfers between devices, padded_2(): lax.ppermute(lax.slice_in_dim(block, block.shape[dim] - width, None, axis...  27.6 us
    dot_general x27, matrix products, causal_conv(): total = total + jnp.dot(taken, kernel, preferred_element_type=jnp.float32)  19 us
    all_to_all x1, blocking collectives, local(): lax.all_to_all(patches, 'ha', split_axis=0, concat_axis=1, tiled=True)  14.6 us
    ppermute x6, waiting for transfers between devices, padded_2(): lax.ppermute(lax.slice_in_dim(block, 0, width, axis=dim), axis, backward)  14.5 us
    ppermute x6, starting transfers between devices, padded_2(): lax.ppermute(lax.slice_in_dim(block, 0, width, axis=dim), axis, backward)  9.82 us
    all_to_all x1, blocking collectives, local(): lax.all_to_all(flat_rows, 'wa', split_axis=0, concat_axis=1, tiled=True)  8.94 us
    slice x12, local copies, waits for them, and re-layouts, causal_conv(): kernel = weight[t_off, h_off].reshape(3 * width_in, out_width)  8.53 us
    concatenate x3, other arithmetic, causal_conv(): jnp.concatenate([padded[:, :, w_off:w_off + cols] for w_off in range(3)],...  4.73 us
  transfers between devices with their start and end apart: 12, of which 7 were waited for; matrix products, arithmetic and copies ran while one was open for 8% of the time, Pallas kernels for 0%

commit v1 on v0

v1 whole, which is shorter than its diff:
```python
import functools

import jax
import jax.numpy as jnp
from jax import lax
from jax.experimental import pallas as pl
from jax.experimental.pallas import tpu as pltpu
from jax.sharding import PartitionSpec as P

BF16 = jnp.bfloat16
F32 = jnp.float32
F, R, Q, C = 16, 4, 8, 384
MSG = 19
VM = pl.BlockSpec(memory_space=pltpu.VMEM)
ANY = pl.BlockSpec(memory_space=pl.ANY)


def act(wide, gain):
    scale = lax.rsqrt(jnp.mean(wide * wide, axis=-1, keepdims=True) + 1e-06)
    u = wide * scale * gain
    return u / (1.0 + jnp.exp(-u))


def stack(now, c0, c1):
    row = lax.broadcasted_iota(jnp.int32, (F, C), 0)
    c0 = jnp.broadcast_to(c0, (F, C))
    c1 = jnp.broadcast_to(c1, (F, C))
    one = jnp.where(row == 0, c1, pltpu.roll(now, 1, 0))
    two = jnp.where(row == 0, c0, jnp.where(row == 1, c1, pltpu.roll(now, 2, 0)))
    return two.astype(BF16), one.astype(BF16), now.astype(BF16)


def put_rows(ref, start, value):
    for n in range(3):
        ref[n, pl.ds(start, value.shape[0])] = value[:, n * 128 : (n + 1) * 128]


def rows_at(ref, start, count, stride):
    where = pl.ds(start, count, stride=stride) if stride > 1 else pl.ds(start, count)
    return jnp.concatenate([ref[n, where, :] for n in range(3)], axis=-1)


def first_kernel(feat, cf, cs, gain, own, raw, lo, hi, wide, plain):
    def frame(f, _):
        x = feat[f].astype(F32).reshape(R * Q, C)
        put_rows(plain, f * R * Q, x)
        put_rows(wide, f * R * Q, act(x, gain[...]))
        return 0

    lax.fori_loop(0, F, frame, 0)
    for k in range(R * Q):
        cell = rows_at(wide, k, F, R * Q).astype(BF16)
        own[k] = cell
        if k < 16:
            lo[k] = cell
        else:
            hi[k - 16] = cell
        raw[k] = rows_at(plain, k, F, R * Q).astype(BF16)

    def cached(ref, h):
        return jnp.concatenate([ref[0, h].astype(F32), ref[1, h].astype(F32)], axis=0).astype(BF16)

    for n in range(2):
        lo[16 + n] = cached(cf, n)
        hi[16 + n] = cached(cf, 2 + n)
    lo[18] = cached(cs, 0)
    hi[18] = cached(cs, 3)


def fill_caches(cf, cs, top, bot, wide_f, wide_s):
    for n in range(2):
        put_rows(wide_f, n * 16, top[16 + n].astype(F32))
        put_rows(wide_f, (6 + n) * 16, bot[16 + n].astype(F32))
    put_rows(wide_s, 0, top[18].astype(F32))
    put_rows(wide_s, 5 * 16, bot[18].astype(F32))
    for h in range(R):
        for f in range(2):
            put_rows(wide_f, (2 + h) * 16 + f * 8, cf[f, h].astype(F32))
            put_rows(wide_s, (1 + h) * 16 + f * 8, cs[f, h].astype(F32))


def second_kernel(own, top, bot, cf, cs, left, right, wide_f, wide_s):
    wide_s[...] = jnp.zeros_like(wide_s)
    fill_caches(cf, cs, top, bot, wide_f, wide_s)
    for out, base, edge in ((left, 0, 0), (right, 6, 7)):
        for c in range(2):
            for h in range(8):
                w = base + c
                if h < 2:
                    cell = top[h * Q + w]
                elif h < 6:
                    cell = own[(h - 2) * Q + w]
                else:
                    cell = bot[(h - 6) * Q + w]
                out[h * 2 + c] = cell
            out[16 + c] = rows_at(wide_f, base + c, 16, 8).astype(BF16)
        out[18] = rows_at(wide_s, edge, 16, 8).astype(BF16)


def main_kernel(
    own, raw, top, bot, left, right, cf, cs, ch, g2, gh, b1, b2, w1, w2, wh, out,
    s1, s2, s3, acc1, acc2, acch, w1v, w2v, whv, wide_f, wide_s, side_f, side_s, wide_h, sems,
):
    copies = []
    for n, (src, dst) in enumerate(((w1, w1v), (w2, w2v))):
        for a in range(3):
            group = []
            for b in range(3):
                for t in range(3):
                    group.append(pltpu.make_async_copy(src.at[t, a, b], dst.at[a, b * 3 + t], sems.at[n * 3 + a]))
            copies.append(group)
    copies.append([pltpu.make_async_copy(wh, whv, sems.at[6])])
    for group in copies:
        for copy in group:
            copy.start()

    ha, wa = lax.axis_index("ha"), lax.axis_index("wa")
    up, down = ha > 0, ha < lax.axis_size("ha") - 1
    west, east = wa > 0, wa < lax.axis_size("wa") - 1

    fill_caches(cf, cs, top, bot, wide_f, wide_s)
    for n, msg in enumerate((left, right)):
        for c in range(2):
            side_f[n, pl.ds(c * 16, 16)] = msg[16 + c].astype(F32)
        side_s[n] = msg[18].astype(F32)
    for h in range(R):
        for f in range(2):
            wide_h[pl.ds(h * 16 + f * 8, 8)] = ch[f, h].astype(F32)

    def put(dst, valid, now, c0, c1):
        if valid is not None:
            keep = jnp.where(valid, 1.0, 0.0).astype(F32)
            now, c0, c1 = now * keep, c0 * keep, c1 * keep
        for n, part in enumerate(stack(now, c0, c1)):
            dst[:, pl.ds(n * C, C)] = part

    def middle(src, h0, count, valid):
        def cell(k, _):
            h, w = k // Q, k % Q
            base = (h0 + h) * 16 + w
            put(
                s1.at[h0 + h, w + 2], valid, src[k].astype(F32),
                rows_at(wide_f, base, 1, 1), rows_at(wide_f, base + 8, 1, 1),
            )
            return 0

        lax.fori_loop(0, count, cell, 0)

    middle(own, 2, 32, None)
    middle(top, 0, 16, up)
    middle(bot, 6, 16, down)
    for n, (msg, side, w0) in enumerate(((left, west, 0), (right, east, 10))):
        def cell(k, _, n=n, msg=msg, side=side, w0=w0):
            h, c = k // 2, k % 2
            valid = side & (up | (h >= 2)) & (down | (h < 6))
            base = c * 16 + h * 2
            put(
                s1.at[h, w0 + c], valid, msg[k].astype(F32),
                side_f[n, pl.ds(base, 1), :], side_f[n, pl.ds(base + 1, 1), :],
            )
            return 0

        lax.fori_loop(0, 16, cell, 0)

    def conv(src, weight, acc, rows, cols, first):
        for a in range(3):
            for copy in copies[first + a]:
                copy.wait()
            taken = jnp.concatenate(
                [src[a : a + rows, b : b + cols].reshape(rows * cols * F, 3 * C) for b in range(3)], axis=-1
            )
            part = jnp.dot(taken, weight[a].reshape(9 * C, C), preferred_element_type=F32)
            part = part.reshape(rows, cols, F, C)
            if a == 0:
                acc[...] = part
            else:
                acc[...] += part

    conv(s1, w1v, acc1, R + 2, Q + 2, 0)

    def hidden(h, w, c0, c1, valid):
        wide = (acc1[h, w] + b1[...]).astype(BF16).astype(F32)
        put(s2.at[h, w], valid, act(wide, g2[...]), c0, c1)

    def row_of(k, _):
        h, w = k // Q, k % Q
        base = h * 16 + w
        hidden(
            h, w + 1, rows_at(wide_s, base, 1, 1), rows_at(wide_s, base + 8, 1, 1),
            (up | (h >= 1)) & (down | (h < 5)),
        )
        return 0

    lax.fori_loop(0, 6 * Q, row_of, 0)
    for n, (side, w) in enumerate(((west, 0), (east, 9))):
        def edge(h, _, n=n, side=side, w=w):
            hidden(
                h, w, side_s[n, pl.ds(h * 2, 1), :], side_s[n, pl.ds(h * 2 + 1, 1), :],
                side & (up | (h >= 1)) & (down | (h < 5)),
            )
            return 0

        lax.fori_loop(0, 6, edge, 0)

    conv(s2, w2v, acc2, R, Q, 3)

    def last(k, _):
        h, w = k // Q, k % Q
        base = h * 16 + w
        wide = (acc2[h, w] + b2[...] + raw[k].astype(F32)).astype(BF16).astype(F32)
        put(
            s3.at[(h % 2) * 2 + w % 2, (h // 2) * 4 + w // 2], None, act(wide, gh[...]),
            wide_h[pl.ds(base, 1), :], wide_h[pl.ds(base + 8, 1), :],
        )
        return 0

    lax.fori_loop(0, R * Q, last, 0)
    for copy in copies[6]:
        copy.wait()
    acch[...] = jnp.zeros_like(acch)
    for rh in range(2):
        for rw in range(2):
            part = jnp.dot(
                s3[rh * 2 + rw].reshape(8 * F, 3 * C), whv[rh * 2 + rw], preferred_element_type=F32
            )
            for p in range(2):
                for q in range(4):
                    for m in range(2):
                        for n in range(2):
                            pp, qq = (p + rh - 1 + m) % 3, (q + rw - 1 + n) % 5
                            slot = pp * 4 + qq if qq < 4 else 12 + pp
                            block = part[(p * 4 + q) * F : (p * 4 + q + 1) * F, (m * 2 + n) * 128 : (m * 2 + n + 1) * 128]
                            acch[pl.ds(slot * F, F)] += block

    def frame(f, _):
        patches = acch[pl.ds(f, 16, stride=F), :].astype(BF16)
        for g in range(8):
            out[f, g] = patches
        return 0

    lax.fori_loop(0, F, frame, 0)


def last_kernel(slots, bias, out, held, sums, sem):
    ha_count = 16
    g = lax.axis_index("wa")
    copies = []
    for k in range(4):
        i = jnp.clip(2 * g - 1 + k, 0, ha_count - 1)
        copies.append(pltpu.make_async_copy(slots.at[pl.ds(i * 8, 8)], held.at[k], sem.at[k]))
        copies[-1].start()
    for copy in copies:
        copy.wait()
    lane = lax.broadcasted_iota(jnp.int32, (4, 128), 1)
    row = lax.broadcasted_iota(jnp.int32, (4, 128), 0)
    for k in range(2):
        for pr in range(2):
            other = k if pr == 0 else k + 2
            there = (2 * g + k > 0) if pr == 0 else (2 * g + k < ha_count - 1)
            upright = ((lane < 64) if pr == 0 else (lane >= 64)) & there

            def edge(j, pr=pr, k=k, other=other, upright=upright):
                mine = jnp.broadcast_to(held[k + 1, j, 12 + pr : 13 + pr].astype(F32), (4, 128))
                theirs = jnp.broadcast_to(held[other, j, 14:15].astype(F32), (4, 128))
                return mine + jnp.where(upright, theirs, 0.0)

            for j in range(8):
                total = held[k + 1, j, pr * 4 : pr * 4 + 4].astype(F32)
                total = total + jnp.where(upright, held[other, j, 8:12].astype(F32), 0.0)
                if j > 0:
                    total = total + jnp.where((row == 0) & (lane % 64 < 32), edge(j - 1), 0.0)
                if j < 7:
                    total = total + jnp.where((row == 3) & (lane % 64 >= 32), edge(j + 1), 0.0)
                sums[pl.ds((2 * k + pr) * 32 + j * 4, 4)] = total + bias[...]
    out[...] = sums[...].astype(BF16)


def shape(*dims, dtype=BF16):
    return jax.ShapeDtypeStruct(dims, dtype)


def params(limit):
    return pltpu.CompilerParams(vmem_limit_bytes=limit * 2**20)


def head_weights(conv_head):
    flat = jnp.transpose(conv_head, (1, 2, 0, 3, 4)).reshape(3, 3, 3 * C, 32)
    none = jnp.zeros((3 * C, 32), BF16)
    sets = []
    for rh in range(2):
        for rw in range(2):
            parts = []
            for m in range(2):
                for n in range(2):
                    for r in range(2):
                        for s in range(2):
                            a = rh - (2 * (rh - 1 + m) + r) + 1
                            b = rw - (2 * (rw - 1 + n) + s) + 1
                            parts.append(flat[a, b] if 0 <= a <= 2 and 0 <= b <= 2 else none)
            sets.append(jnp.concatenate(parts, axis=-1))
    return jnp.stack(sets)


def around(axis, step):
    count = lax.axis_size(axis)
    return [(n, (n + step) % count) for n in range(count)]


def local(
    features, cache_first, cache_second, cache_head, gain_first, gain_second, gain_head,
    conv_first, conv_second, conv_head, bias_first, bias_second, bias_head,
):
    line = lambda v: v.reshape(1, -1)
    own, raw, lo, hi = pl.pallas_call(
        first_kernel,
        out_shape=[shape(32, F, C), shape(32, F, C), shape(MSG, F, C), shape(MSG, F, C)],
        in_specs=[VM] * 4,
        out_specs=[VM] * 4,
        scratch_shapes=[pltpu.VMEM((3, F * R * Q, 128), F32)] * 2,
        compiler_params=params(16),
        name="act_first",
    )(features, cache_first, cache_second, line(gain_first))
    top = lax.ppermute(hi, "ha", around("ha", 1))
    bot = lax.ppermute(lo, "ha", around("ha", -1))
    to_left, to_right = pl.pallas_call(
        second_kernel,
        out_shape=[shape(MSG, F, C)] * 2,
        in_specs=[VM] * 5,
        out_specs=[VM] * 2,
        scratch_shapes=[pltpu.VMEM((3, 128, 128), F32)] * 2,
        compiler_params=params(16),
        name="pack_columns",
    )(own, top, bot, cache_first, cache_second)
    left = lax.ppermute(to_right, "wa", around("wa", 1))
    right = lax.ppermute(to_left, "wa", around("wa", -1))
    slots = pl.pallas_call(
        main_kernel,
        out_shape=shape(F, 8, 16, 128),
        in_specs=[VM] * 13 + [ANY] * 3,
        out_specs=VM,
        scratch_shapes=[
            pltpu.VMEM((R + 4, Q + 4, F, 3 * C), BF16),
            pltpu.VMEM((R + 2, Q + 2, F, 3 * C), BF16),
            pltpu.VMEM((4, 8, F, 3 * C), BF16),
            pltpu.VMEM((R + 2, Q + 2, F, C), F32),
            pltpu.VMEM((R, Q, F, C), F32),
            pltpu.VMEM((16 * F, 128), F32),
            pltpu.VMEM((3, 9, C, C), BF16),
            pltpu.VMEM((3, 9, C, C), BF16),
            pltpu.VMEM((4, 3 * C, 512), BF16),
            pltpu.VMEM((3, 128, 128), F32),
            pltpu.VMEM((3, 128, 128), F32),
            pltpu.VMEM((2, 32, C), F32),
            pltpu.VMEM((2, 16, C), F32),
            pltpu.VMEM((64, C), F32),
            pltpu.SemaphoreType.DMA((7,)),
        ],
        compiler_params=params(56),
        name="block",
    )(
        own, raw, top, bot, left, right, cache_first, cache_second, cache_head,
        line(gain_second), line(gain_head), line(bias_first), line(bias_second),
        conv_first, conv_second, head_weights(conv_head),
    )
    arrived = lax.all_to_all(slots.reshape(F * 8, 16, 128), ("ha", "wa"), 0, 0, tiled=True)
    return pl.pallas_call(
        last_kernel,
        out_shape=shape(128, 128),
        in_specs=[ANY, VM],
        out_specs=VM,
        scratch_shapes=[
            pltpu.VMEM((4, 8, 16, 128), BF16),
            pltpu.VMEM((128, 128), F32),
            pltpu.SemaphoreType.DMA((4,)),
        ],
        compiler_params=params(16),
        name="sum_patches",
    )(arrived, jnp.tile(bias_head, 4).reshape(1, 128))


def solution(mesh):
    tile = P(None, "ha", "wa", None)
    return jax.shard_map(
        local,
        mesh=mesh,
        in_specs=(tile,) * 4 + (P(),) * 9,
        out_specs=P(("ha", "wa"), None),
        check_vma=False,
    )
```

time: 121 us -> 108 us (0.89); the launches traced: 121 us -> 106 us
  Pallas kernels: 0 us -> 37.7 us
  blocking collectives: 23.5 us -> 0 us
  starting transfers between devices: 37.4 us -> 15.3 us
  local copies, waits for them, and re-layouts: 14.4 us -> 35.3 us
  matrix products: 19 us -> 0 us
  other arithmetic: 9.65 us -> 4.09 us
  waiting for transfers between devices: 15.8 us -> 13.6 us
    pallas_call x0 -> x4, Pallas kernels: none -> 37.7 us  [the longest x1 33.8 us: local(): pl.pallas_call(main_kernel, out_shape=shape(F, 8, 16, 128), in_specs=[VM]...]
    ppermute x12 -> x4, starting transfers between devices: 37.4 us -> 8.39 us  [the longest x1 3.64 us: local(): bot = lax.ppermute(lo, 'ha', around('ha', -1))]
    all_to_all x2 -> x0, blocking collectives: 23.5 us -> none  [the longest x1 14.6 us: local(): lax.all_to_all(patches, 'ha', split_axis=0, concat_axis=1, tiled=True)]
    concatenate x0 -> x4, local copies, waits for them, and re-layouts: none -> 20.8 us  [head_weights(): sets.append(jnp.concatenate(parts, axis=-1))]
    dot_general x27 -> x0, matrix products: 19 us -> none  [causal_conv(): total = total + jnp.dot(taken, kernel, preferred_element_type=jnp.float32)]
    ppermute x12 -> x4, waiting for transfers between devices: 15.8 us -> 0.01 us  [the longest x1 0.01 us: local(): bot = lax.ppermute(lo, 'ha', around('ha', -1))]
    all_to_all x0 -> x1, waiting for transfers between devices: none -> 13.6 us  [local(): lax.all_to_all(slots.reshape(F * 8, 16, 128), ('ha', 'wa'), 0, 0, tiled=T...]
    slice x21 -> x0, local copies, waits for them, and re-layouts: 12.2 us -> none  [the longest x12 8.53 us: causal_conv(): kernel = weight[t_off, h_off].reshape(3 * width_in, out_width)]
  transfers between devices with their start and end apart: 12 -> 5, of which waited for: 7 -> 1; matrix products, arithmetic and copies ran while one was open for 8% -> 33% of each run, Pallas kernels for 0% -> 0%
where the time goes in v1:
time: 108 us; the launch traced here: 106 us
  Pallas kernels  37.7 us (35%)
  local copies, waits for them, and re-layouts  35.3 us (33%)
  starting transfers between devices  15.3 us (14%)
  waiting for transfers between devices  13.6 us (13%)
  other arithmetic  4.09 us (4%)
    pallas_call x1, Pallas kernels, local(): pl.pallas_call(main_kernel, out_shape=shape(F, 8, 16, 128), in_specs=[VM]...  33.8 us
    concatenate x4, local copies, waits for them, and re-layouts, head_weights(): sets.append(jnp.concatenate(parts, axis=-1))  20.8 us
    all_to_all x1, waiting for transfers between devices, local(): lax.all_to_all(slots.reshape(F * 8, 16, 128), ('ha', 'wa'), 0, 0, tiled=T...  13.6 us
    all_to_all x1, starting transfers between devices, local(): lax.all_to_all(slots.reshape(F * 8, 16, 128), ('ha', 'wa'), 0, 0, tiled=T...  6.9 us
    unnamed x32, local copies, waits for them, and re-layouts  4.15 us
    another operation x1, other arithmetic, head_weights(): return jnp.stack(sets)  4.09 us
    transpose x1, local copies, waits for them, and re-layouts, head_weights(): flat = jnp.transpose(conv_head, (1, 2, 0, 3, 4)).reshape(3, 3, 3 * C, 32)  3.68 us
    ppermute x1, starting transfers between devices, local(): bot = lax.ppermute(lo, 'ha', around('ha', -1))  3.64 us
  transfers between devices with their start and end apart: 5, of which 1 were waited for; matrix products, arithmetic and copies ran while one was open for 33% of the time, Pallas kernels for 0%

profile of v1, /device:TPU:1, one launch (start us, length us, event | category | flops | bytes accessed | tf_op | source)
XLA Modules:
  0.0 106.1 jit_solution(16099846404444111282)
XLA Ops:
  0.0 0.7 reshape.22.gain
  0.7 0.8 copy-done.3
  1.5 0.8 copy-done.5
  2.3 1.0 copy-done.7
  3.3 2.9 %act_first.1 = (bf16[32,16,384]{2,1,0:T(8,128)(2,1)S(1)}, bf16[32,16,384]{2,1,0:T(8,128)(2,1)S(1)}, bf16[19,16,384]{2,1,0:T(8,128)(2,1)S(1)}, bf16[19,16,384]{2,1,0:T(8,128)(2,1)S(1)}) custom-call(bf16[16,4,8,384]{3,2,1,0:T(8,128)(2,1)S(1)} %copy-done.7, bf16[2,4,8,384]{3,2,1,0:T(8,128)(2,1)S(1)} %copy-done.3, bf16[2,4,8,384]{3,2,1,0:T(8,128)(2,1)S(1)} %copy-done.5, ...), custom_call_target="tpu_custom_call" | custom-call | tf_op jit(solution)/shard_map/act_first/pallas_call | solution.py:314
  6.2 0.7 copy-done.8
  6.9 2.1 %collective-permute-start = (bf16[19,16,384]{2,1,0:T(8,128)(2,1)S(1)}, bf16[19,16,384]{2,1,0:T(8,128)(2,1)S(1)}, u32[]{:S(2)}, u32[]{:S(2)}) collective-permute-start(bf16[19,16,384]{2,1,0:T(8,128)(2,1)S(1)} %get-tuple-element.13), channel_id=1, source_target_pairs={{0,8},{8,16},{16,24},{24,32},{32,40},{40,48},{48,56},{56,64},{64,7... | collective-permute-start | bytes 700424 | tf_op jit(solution)/shard_map/ppermute | solution.py:323
  9.1 3.6 %collective-permute-start.1 = (bf16[19,16,384]{2,1,0:T(8,128)(2,1)S(1)}, bf16[19,16,384]{2,1,0:T(8,128)(2,1)S(1)}, u32[]{:S(2)}, u32[]{:S(2)}) collective-permute-start(bf16[19,16,384]{2,1,0:T(8,128)(2,1)S(1)} %get-tuple-element.14), channel_id=1, source_target_pairs={{0,120},{8,0},{16,8},{24,16},{32,24},{40,32},{48,40},{56,48},{64,5... | collective-permute-start | bytes 700424 | tf_op jit(solution)/shard_map/ppermute | solution.py:324
  12.7 3.7 %copy.14 = bf16[3,3,3,384,32]{4,3,2,1,0:T(8,128)(2,1)} copy(bf16[3,3,3,384,32]{3,4,1,0,2:T(8,128)(2,1)} %bitcast.31) | data formatting | bytes 1327104 | tf_op jit(solution)/shard_map/transpose | solution.py:287
  16.4 2.8 %slice_bitcast_fusion = (bf16[1152,32]{1,0:T(8,128)(2,1)S(1)}, bf16[1152,32]{1,0:T(8,128)(2,1)S(1)}, bf16[1152,32]{1,0:T(8,128)(2,1)S(1)}, bf16[1152,32]{1,0:T(8...) fusion(bf16[3,3,1152,32]{3,2,1,0:T(8,128)(2,1)} %bitcast.25), kind=kLoop, calls=%fused_computation.1 | loop fusion | bytes 1327104 | tf_op jit(solution)/shard_map/squeeze | solution.py:299
  19.3 4.8 %concatenate.13 = bf16[1152,512]{1,0:T(8,128)(2,1)} concatenate(bf16[1152,64]{1,0:T(8,128)(2,1)S(1)} %broadcast.8, bf16[1152,32]{1,0:T(8,128)(2,1)} %get-tuple-element.25, bf16[1152,32]{1,0:T(8,128)(2,1)} %get-tuple-element.24, bf16[1152,64]{1,0:T(8,128)(2,1)S(1)} %broadcast.8, bf16[1152,32]{1,0:T(8,128)(2,1)} %get-tuple-element.23, bf16[1152,32]{1,0:T(8,128)(2,1)S(1)} %broadcast_in_dim.3, ...), dimensions={1} | concatenate | bytes 2359296 | tf_op jit(solution)/shard_map/concatenate | solution.py:300
  24.1 4.9 %concatenate.14 = bf16[1152,512]{1,0:T(8,128)(2,1)} concatenate(bf16[1152,32]{1,0:T(8,128)(2,1)S(1)} %broadcast_in_dim.3, bf16[1152,32]{1,0:T(8,128)(2,1)} %get-tuple-element.25, bf16[1152,32]{1,0:T(8,128)(2,1)S(1)} %broadcast_in_dim.3, bf16[1152,32]{1,0:T(8,128)(2,1)} %get-tuple-element.22, bf16[1152,32]{1,0:T(8,128)(2,1)} %get-tuple-element.24, ...), dimensions={1} | concatenate | bytes 2359296 | tf_op jit(solution)/shard_map/concatenate | solution.py:300
  29.0 0.7 broadcast.7
  29.8 5.1 %concatenate.12 = bf16[1152,512]{1,0:T(8,128)(2,1)} concatenate(bf16[1152,96]{1,0:T(8,128)(2,1)} %broadcast.7, bf16[1152,32]{1,0:T(8,128)(2,1)} %get-tuple-element.25, bf16[1152,64]{1,0:T(8,128)(2,1)S(1)} %broadcast.8, bf16[1152,32]{1,0:T(8,128)(2,1)} %get-tuple-element.24, bf16[1152,32]{1,0:T(8,128)(2,1)} %get-tuple-element.23, bf16[1152,32]{1,0:T(8,128)(2,1)S(1)} %broadcast_in_dim.3, ...), dimensions={1} | concatenate | bytes 2359296 | tf_op jit(solution)/shard_map/concatenate | solution.py:300
  34.9 6.0 %concatenate.15 = bf16[1152,512]{1,0:T(8,128)(2,1)} concatenate(bf16[1152,32]{1,0:T(8,128)(2,1)} %get-tuple-element.25, bf16[1152,32]{1,0:T(8,128)(2,1)} %get-tuple-element.24, bf16[1152,32]{1,0:T(8,128)(2,1)} %get-tuple-element.22, bf16[1152,32]{1,0:T(8,128)(2,1)S(1)} %get-tuple-element.20, bf16[1152,32]{1,0:T(8,128)(2,1)} %get-tuple-element.23, ...), dimensions={1} | concatenate | bytes 2359296 | tf_op jit(solution)/shard_map/concatenate | solution.py:300
  41.0 2.6 %collective-permute-start.2 = (bf16[19,16,384]{2,1,0:T(8,128)(2,1)S(1)}, bf16[19,16,384]{2,1,0:T(8,128)(2,1)S(1)}, u32[]{:S(2)}, u32[]{:S(2)}) collective-permute-start(bf16[19,16,384]{2,1,0:T(8,128)(2,1)S(1)} %get-tuple-element.15), channel_id=1, source_target_pairs={{0,1},{1,2},{2,3},{3,4},{4,5},{5,6},{6,7},{7,0},{8,9},{9,10},{10,1... | collective-permute-start | bytes 700424 | tf_op jit(solution)/shard_map/ppermute | solution.py:334
  43.6 4.1 %pad_maximum_fusion.wh = bf16[4,1152,512]{2,1,0:T(8,128)(2,1)} fusion(bf16[1,1152,512]{2,1,0:T(8,128)(2,1)} %bitcast.27, bf16[1,1152,512]{2,1,0:T(8,128)(2,1)} %bitcast.29, bf16[1,1152,512]{2,1,0:T(8,128)(2,1)} %bitcast.28, bf16[1,1152,512]{2,1,0:T(8,128)(2,1)} %bitcast.26), kind=kLoop, calls=%fused_computation | loop fusion | flops 7077888 | bytes 9437184 | tf_op jit(solution)/shard_map/stack | solution.py:301
  48.3 0.6 reshape.24.gh
  49.4 0.6 reshape.26.b2
  50.0 0.7 copy-done.9
  50.8 33.8 %block.1 = bf16[16,8,16,128]{3,2,1,0:T(8,128)(2,1)} custom-call(bf16[32,16,384]{2,1,0:T(8,128)(2,1)} %copy-done, bf16[32,16,384]{2,1,0:T(8,128)(2,1)} %copy-done.8, bf16[19,16,384]{2,1,0:T(8,128)(2,1)} %copy-done.1, bf16[19,16,384]{2,1,0:T(8,128)(2,1)} %copy-done.2, bf16[19,16,384]{2,1,0:T(8,128)(2,1)} %copy-done.9, bf16[19,16,384]{2,1,0:T(8,128)(2,1)} %copy-done.10, ...), custom_call_target="tpu_custom_call" | custom-call | tf_op jit(solution)/shard_map/block/pallas_call | solution.py:336
  84.7 6.9 %all-to-all-start = ((bf16[128,16,128]{2,1,0:T(8,128)(2,1)}), bf16[128,16,128]{2,1,0:T(8,128)(2,1)S(1)}, u32[]{:S(2)}, u32[]{:S(2)}) async-start(bf16[128,16,128]{2,1,0:T(8,128)(2,1)} %bitcast.30), calls=%async_computation | async-start | bytes 1048576 | tf_op jit(solution)/shard_map/all_to_all | solution.py:365
  91.7 13.6 %all-to-all-done.slots = bf16[128,16,128]{2,1,0:T(8,128)(2,1)S(1)} async-done(((bf16[128,16,128]{2,1,0:T(8,128)(2,1)}), bf16[128,16,128]{2,1,0:T(8,128)(2,1)S(1)}, u32[]{:S(2)}, u32[]{:S(2)}) %all-to-all-start) | async-done | bytes 524320 | tf_op jit(solution)/shard_map/all_to_all | solution.py:365
  105.2 0.9 sum_patches.1
  (39 shorter events, 1.5 us)
Async XLA Ops:
  0.7 0.8 copy-start.3
  1.5 0.8 copy-start.5
  2.3 1.0 copy-start.7
  6.2 0.8 copy-start.8
  6.9 33.9 %copy-start = (bf16[32,16,384]{2,1,0:T(8,128)(2,1)}, bf16[32,16,384]{2,1,0:T(8,128)(2,1)S(1)}, u32[]{:S(2)}) copy-start(bf16[32,16,384]{2,1,0:T(8,128)(2,1)S(1)} %get-tuple-element.11.own) | copy-start | bytes 1179652
  6.9 33.9 %collective-permute-start = (bf16[19,16,384]{2,1,0:T(8,128)(2,1)S(1)}, bf16[19,16,384]{2,1,0:T(8,128)(2,1)S(1)}, u32[]{:S(2)}, u32[]{:S(2)}) collective-permute-start(bf16[19,16,384]{2,1,0:T(8,128)(2,1)S(1)} %get-tuple-element.13), channel_id=1, source_target_pairs={{0,8},{8,16},{16,24},{24,32},{32,40},{40,48},{48,56},{56,64},{64,7... | collective-permute-start | bytes 700424 | tf_op jit(solution)/shard_map/ppermute | solution.py:323
  9.1 31.8 %collective-permute-start.1 = (bf16[19,16,384]{2,1,0:T(8,128)(2,1)S(1)}, bf16[19,16,384]{2,1,0:T(8,128)(2,1)S(1)}, u32[]{:S(2)}, u32[]{:S(2)}) collective-permute-start(bf16[19,16,384]{2,1,0:T(8,128)(2,1)S(1)} %get-tuple-element.14), channel_id=1, source_target_pairs={{0,120},{8,0},{16,8},{24,16},{32,24},{40,32},{48,40},{56,48},{64,5... | collective-permute-start | bytes 700424 | tf_op jit(solution)/shard_map/ppermute | solution.py:324
  29.8 11.1 %copy-start.4 = (bf16[2,4,8,384]{3,2,1,0:T(8,128)(2,1)S(1)}, bf16[2,4,8,384]{3,2,1,0:T(8,128)(2,1)}, u32[]{:S(2)}) copy-start(bf16[2,4,8,384]{3,2,1,0:T(8,128)(2,1)} %cf.5) | copy-start | bytes 147460
  29.8 11.1 %copy-start.6 = (bf16[2,4,8,384]{3,2,1,0:T(8,128)(2,1)S(1)}, bf16[2,4,8,384]{3,2,1,0:T(8,128)(2,1)}, u32[]{:S(2)}) copy-start(bf16[2,4,8,384]{3,2,1,0:T(8,128)(2,1)} %cs.5) | copy-start | bytes 147460
  40.8 6.9 %copy-start.1 = (bf16[19,16,384]{2,1,0:T(8,128)(2,1)}, bf16[19,16,384]{2,1,0:T(8,128)(2,1)S(1)}, u32[]{:S(2)}) copy-start(bf16[19,16,384]{2,1,0:T(8,128)(2,1)S(1)} %collective-permute-done.top) | copy-start | bytes 700420
  40.9 6.9 %copy-start.2 = (bf16[19,16,384]{2,1,0:T(8,128)(2,1)}, bf16[19,16,384]{2,1,0:T(8,128)(2,1)S(1)}, u32[]{:S(2)}) copy-start(bf16[19,16,384]{2,1,0:T(8,128)(2,1)S(1)} %collective-permute-done.1.bot) | copy-start | bytes 700420
  41.0 9.0 %collective-permute-start.2 = (bf16[19,16,384]{2,1,0:T(8,128)(2,1)S(1)}, bf16[19,16,384]{2,1,0:T(8,128)(2,1)S(1)}, u32[]{:S(2)}, u32[]{:S(2)}) collective-permute-start(bf16[19,16,384]{2,1,0:T(8,128)(2,1)S(1)} %get-tuple-element.15), channel_id=1, source_target_pairs={{0,1},{1,2},{2,3},{3,4},{4,5},{5,6},{6,7},{7,0},{8,9},{9,10},{10,1... | collective-permute-start | bytes 700424 | tf_op jit(solution)/shard_map/ppermute | solution.py:334
  43.6 6.4 %collective-permute-start.3 = (bf16[19,16,384]{2,1,0:T(8,128)(2,1)S(1)}, bf16[19,16,384]{2,1,0:T(8,128)(2,1)S(1)}, u32[]{:S(2)}, u32[]{:S(2)}) collective-permute-start(bf16[19,16,384]{2,1,0:T(8,128)(2,1)S(1)} %get-tuple-element.16), channel_id=1, source_target_pairs={{0,7},{1,0},{2,1},{3,2},{4,3},{5,4},{6,5},{7,6},{8,15},{9,8},{10,9... | collective-permute-start | bytes 700424 | tf_op jit(solution)/shard_map/ppermute | solution.py:335
  43.6 4.1 %copy-start.11 = (f32[384]{0:T(512)S(1)}, f32[384]{0:T(512)}, u32[]{:S(2)}) copy-start(f32[384]{0:T(512)} %param.18) | copy-start | bytes 4612
  43.6 4.7 %copy-start.12 = (f32[384]{0:T(512)S(1)}, f32[384]{0:T(512)}, u32[]{:S(2)}) copy-start(f32[384]{0:T(512)} %param.19) | copy-start | bytes 4612
  43.6 5.3 %copy-start.13 = (f32[384]{0:T(512)S(1)}, f32[384]{0:T(512)}, u32[]{:S(2)}) copy-start(f32[384]{0:T(512)} %param.23) | copy-start | bytes 4612
  43.6 5.8 %copy-start.14 = (f32[384]{0:T(512)S(1)}, f32[384]{0:T(512)}, u32[]{:S(2)}) copy-start(f32[384]{0:T(512)} %param.24) | copy-start | bytes 4612
  50.0 0.7 copy-start.9
  50.0 0.8 copy-start.10
  50.8 40.8 %copy-start.15 = (f32[32]{0:T(128)S(1)}, f32[32]{0:T(128)}, u32[]{:S(2)}) copy-start(f32[32]{0:T(128)} %param.25) | copy-start | bytes 388
  84.7 20.6 %all-to-all-start = ((bf16[128,16,128]{2,1,0:T(8,128)(2,1)}), bf16[128,16,128]{2,1,0:T(8,128)(2,1)S(1)}, u32[]{:S(2)}, u32[]{:S(2)}) async-start(bf16[128,16,128]{2,1,0:T(8,128)(2,1)} %bitcast.30), calls=%async_computation | async-start | bytes 1048576 | tf_op jit(solution)/shard_map/all_to_all | solution.py:365

commit v2 on v1

v2 whole, which is shorter than its diff:
```python
import functools

import jax
import jax.numpy as jnp
from jax import lax
from jax.experimental import pallas as pl
from jax.experimental.pallas import tpu as pltpu
from jax.sharding import PartitionSpec as P

BF16 = jnp.bfloat16
F32 = jnp.float32
F, R, Q, C = 16, 4, 8, 384
MSG = 19
VM = pl.BlockSpec(memory_space=pltpu.VMEM)
ANY = pl.BlockSpec(memory_space=pl.ANY)


def act(wide, half_gain):
    scale = lax.rsqrt(jnp.mean(wide * wide, axis=-1, keepdims=True) + 1e-06)
    h = wide * scale * half_gain
    return h + h * jnp.tanh(h)


def line(ref):
    return ref[...].reshape(1, -1)


def put_rows(ref, start, value):
    for n in range(3):
        ref[n, pl.ds(start, value.shape[0])] = value[:, n * 128 : (n + 1) * 128]


def rows_at(ref, start, count, stride):
    where = pl.ds(start, count, stride=stride) if stride > 1 else pl.ds(start, count)
    return jnp.concatenate([ref[n, where, :] for n in range(3)], axis=-1)


def stack(now, c0, c1):
    row = lax.broadcasted_iota(jnp.int32, now.shape, 0) % F
    c0, c1 = (jnp.concatenate([jnp.broadcast_to(c, (F, C)) for c in cs], axis=0) for cs in (c0, c1))
    one = jnp.where(row == 0, c1, pltpu.roll(now, 1, 0))
    two = jnp.where(row == 0, c0, jnp.where(row == 1, c1, pltpu.roll(now, 2, 0)))
    return two.astype(BF16), one.astype(BF16), now.astype(BF16)


def put(dst, where, now, c0, c1, valid=None):
    if valid is not None:
        keep = jnp.where(valid, 1.0, 0.0).astype(F32)
        now, c0, c1 = now * keep, [c * keep for c in c0], [c * keep for c in c1]
    for n, part in enumerate(stack(now, c0, c1)):
        dst[where + (slice(None), pl.ds(n * C, C))] = part.reshape(-1, F, C)


def bring(pairs, sems):
    copies = [pltpu.make_async_copy(src, dst, sems.at[n]) for n, (src, dst) in enumerate(pairs)]
    for copy in copies:
        copy.start()
    return copies


def first_kernel(feat_h, cf_h, cs_h, gain_h, own, raw, lo, hi, feat, cf, cs, gain, wide, plain, sems):
    copies = bring(((gain_h, gain), (feat_h, feat), (cf_h, cf), (cs_h, cs)), sems)
    copies[0].wait()
    copies[1].wait()
    half = 0.5 * line(gain)

    def frame(f, _):
        x = feat[pl.ds(f * 4, 4)].astype(F32).reshape(4 * R * Q, C)
        put_rows(plain, f * 4 * R * Q, x)
        put_rows(wide, f * 4 * R * Q, act(x, half))
        return 0

    lax.fori_loop(0, F // 4, frame, 0)
    for k in range(R * Q):
        cell = rows_at(wide, k, F, R * Q).astype(BF16)
        own[k] = cell
        if k < 16:
            lo[k] = cell
        else:
            hi[k - 16] = cell
        raw[k] = rows_at(plain, k, F, R * Q).astype(BF16)

    def cached(ref, h):
        return jnp.concatenate([ref[0, h].astype(F32), ref[1, h].astype(F32)], axis=0).astype(BF16)

    copies[2].wait()
    copies[3].wait()
    for n in range(2):
        lo[16 + n] = cached(cf, n)
        hi[16 + n] = cached(cf, 2 + n)
    lo[18] = cached(cs, 0)
    hi[18] = cached(cs, 3)


def fill_caches(cf, cs, top, bot, wide_f, wide_s):
    for n in range(2):
        put_rows(wide_f, n * 16, top[16 + n].astype(F32))
        put_rows(wide_f, (6 + n) * 16, bot[16 + n].astype(F32))
    put_rows(wide_s, 0, top[18].astype(F32))
    put_rows(wide_s, 5 * 16, bot[18].astype(F32))
    for h in range(R):
        for f in range(2):
            put_rows(wide_f, (2 + h) * 16 + f * 8, cf[f, h].astype(F32))
            put_rows(wide_s, (1 + h) * 16 + f * 8, cs[f, h].astype(F32))


def second_kernel(own, top, bot, cf_h, cs_h, left, right, cf, cs, wide_f, wide_s, sems):
    copies = bring(((cf_h, cf), (cs_h, cs)), sems)
    wide_s[...] = jnp.zeros_like(wide_s)
    for out, base in ((left, 0), (right, 6)):
        for c in range(2):
            for h in range(8):
                w = base + c
                if h < 2:
                    cell = top[h * Q + w]
                elif h < 6:
                    cell = own[(h - 2) * Q + w]
                else:
                    cell = bot[(h - 6) * Q + w]
                out[h * 2 + c] = cell
    for copy in copies:
        copy.wait()
    fill_caches(cf, cs, top, bot, wide_f, wide_s)
    for out, base, edge in ((left, 0, 0), (right, 6, 7)):
        for c in range(2):
            out[16 + c] = rows_at(wide_f, base + c, 16, 8).astype(BF16)
        out[18] = rows_at(wide_s, edge, 16, 8).astype(BF16)


def main_kernel(
    own, raw, top, bot, left, right, cf_h, cs_h, ch_h, g2_h, gh_h, b1_h, b2_h, w1, w2, wh, out,
    s1, s2, s3, acc1, acc2, acch, w1v, w2v, whv, wy, wide_f, wide_s, side_f, side_s, wide_h,
    cf, cs, ch, g2, gh, b1, b2, sems, wsems,
):
    small = bring(
        ((cf_h, cf), (cs_h, cs), (ch_h, ch), (g2_h, g2), (gh_h, gh), (b1_h, b1), (b2_h, b2)), sems
    )
    copies = []
    for n, (src, dst) in enumerate(((w1, w1v), (w2, w2v))):
        for a in range(3):
            group = []
            for b in range(3):
                for t in range(3):
                    group.append(pltpu.make_async_copy(src.at[t, a, b], dst.at[a, b * 3 + t], wsems.at[n * 3 + a]))
            copies.append(group)
    copies.insert(3, [pltpu.make_async_copy(wh, whv, wsems.at[6])])
    for group in copies:
        for copy in group:
            copy.start()

    ha, wa = lax.axis_index("ha"), lax.axis_index("wa")
    up, down = ha > 0, ha < lax.axis_size("ha") - 1
    west, east = wa > 0, wa < lax.axis_size("wa") - 1

    for copy in small:
        copy.wait()
    fill_caches(cf, cs, top, bot, wide_f, wide_s)
    for n, msg in enumerate((left, right)):
        for c in range(2):
            side_f[n, pl.ds(c * 16, 16)] = msg[16 + c].astype(F32)
        side_s[n] = msg[18].astype(F32)
    for h in range(R):
        for f in range(2):
            wide_h[pl.ds(h * 16 + f * 8, 8)] = ch[f, h].astype(F32)

    def middle(src, h0, count, valid):
        def cells(h, _):
            base = (h0 + h) * 16
            put(
                s1, (h0 + h, pl.ds(2, Q)), src[pl.ds(h * Q, Q)].reshape(Q * F, C).astype(F32),
                [rows_at(wide_f, base + w, 1, 1) for w in range(Q)],
                [rows_at(wide_f, base + 8 + w, 1, 1) for w in range(Q)], valid,
            )
            return 0

        lax.fori_loop(0, count, cells, 0)

    middle(own, 2, 4, None)
    middle(top, 0, 2, up)
    middle(bot, 6, 2, down)
    for n, (msg, side, w0) in enumerate(((left, west, 0), (right, east, 10))):
        def cells(h, _, n=n, msg=msg, side=side, w0=w0):
            put(
                s1, (h, pl.ds(w0, 2)), msg[pl.ds(h * 2, 2)].reshape(2 * F, C).astype(F32),
                [side_f[n, pl.ds(c * 16 + h * 2, 1), :] for c in range(2)],
                [side_f[n, pl.ds(c * 16 + h * 2 + 1, 1), :] for c in range(2)],
                side & (up | (h >= 2)) & (down | (h < 6)),
            )
            return 0

        lax.fori_loop(0, 8, cells, 0)

    def conv(src, weight, acc, rows, cols, first):
        for a in range(3):
            for copy in copies[first + a]:
                copy.wait()
            taken = jnp.concatenate(
                [src[a : a + rows, b : b + cols].reshape(rows * cols * F, 3 * C) for b in range(3)], axis=-1
            )
            part = jnp.dot(taken, weight[a].reshape(9 * C, C), preferred_element_type=F32)
            part = part.reshape(rows, cols, F, C)
            if a == 0:
                acc[...] = part
            else:
                acc[...] += part

    conv(s1, w1v, acc1, R + 2, Q + 2, 0)

    half2 = 0.5 * line(g2)

    def hidden(h, _):
        base = h * 16
        inside = (up | (h >= 1)) & (down | (h < 5))
        for w0, count, valid, c0, c1 in (
            (1, Q, inside, [rows_at(wide_s, base + w, 1, 1) for w in range(Q)],
             [rows_at(wide_s, base + 8 + w, 1, 1) for w in range(Q)]),
            (0, 1, inside & west, [side_s[0, pl.ds(h * 2, 1), :]], [side_s[0, pl.ds(h * 2 + 1, 1), :]]),
            (9, 1, inside & east, [side_s[1, pl.ds(h * 2, 1), :]], [side_s[1, pl.ds(h * 2 + 1, 1), :]]),
        ):
            wide = (acc1[h, pl.ds(w0, count)].reshape(count * F, C) + line(b1)).astype(BF16).astype(F32)
            put(s2, (h, pl.ds(w0, count)), act(wide, half2), c0, c1, valid)
        return 0

    lax.fori_loop(0, 6, hidden, 0)

    for copy in copies[3]:
        copy.wait()
    none = jnp.zeros((C, 32), BF16)
    for t in range(3):
        for a in range(3):
            wy[pl.ds(t * C, C), pl.ds(a * 128, 128)] = jnp.concatenate(
                [whv[t, a, 0], whv[t, a, 1], whv[t, a, 2], none], axis=-1
            )

    conv(s2, w2v, acc2, R, Q, 4)

    halfh = 0.5 * line(gh)

    def last(h, _):
        base = h * 16
        wide = acc2[h].reshape(Q * F, C) + line(b2) + raw[pl.ds(h * Q, Q)].reshape(Q * F, C).astype(F32)
        put(
            s3, (pl.ds(h * Q, Q),), act(wide.astype(BF16).astype(F32), halfh),
            [wide_h[pl.ds(base + w, 1), :] for w in range(Q)],
            [wide_h[pl.ds(base + 8 + w, 1), :] for w in range(Q)],
        )
        return 0

    lax.fori_loop(0, R, last, 0)
    part = jnp.dot(s3[...].reshape(R * Q * F, 3 * C), wy[...], preferred_element_type=F32)
    lane = lax.broadcasted_iota(jnp.int32, (F, 128), 1)
    sums = {}
    for h in range(R):
        for w in range(Q):
            k = h * Q + w
            for a in range(3):
                block = part[k * F : (k + 1) * F, a * 128 : (a + 1) * 128]
                for b in range(3):
                    row, col = h + 1 - a, w + 1 - b
                    pp, qq = (row // 2) % 3, (col // 2) % 5
                    slot = pp * 4 + qq if qq < 4 else 12 + pp
                    low = (2 * (row % 2) + col % 2) * 32
                    shift = (low - 32 * b) % 128
                    moved = pltpu.roll(block, shift, 1) if shift else block
                    term = jnp.where((lane >= low) & (lane < low + 32), moved, 0.0)
                    sums[slot] = sums[slot] + term if slot in sums else term
    for slot, total in sums.items():
        acch[pl.ds(slot * F, F)] = total
    acch[pl.ds(15 * F, F)] = jnp.zeros((F, 128), F32)

    for f in range(F):
        patches = acch[pl.ds(f, 16, stride=F), :].astype(BF16)
        for g in range(8):
            out[f, g] = patches


def last_kernel(slots, bias, out, held, sums, sem):
    ha_count = 16
    g = lax.axis_index("wa")
    copies = []
    for k in range(4):
        i = jnp.clip(2 * g - 1 + k, 0, ha_count - 1)
        copies.append(pltpu.make_async_copy(slots.at[pl.ds(i * 8, 8)], held.at[k], sem.at[k]))
        copies[-1].start()
    for copy in copies:
        copy.wait()
    lane = lax.broadcasted_iota(jnp.int32, (4, 128), 1)
    row = lax.broadcasted_iota(jnp.int32, (4, 128), 0)
    for k in range(2):
        for pr in range(2):
            other = k if pr == 0 else k + 2
            there = (2 * g + k > 0) if pr == 0 else (2 * g + k < ha_count - 1)
            upright = ((lane < 64) if pr == 0 else (lane >= 64)) & there

            def edge(j, pr=pr, k=k, other=other, upright=upright):
                mine = jnp.broadcast_to(held[k + 1, j, 12 + pr : 13 + pr].astype(F32), (4, 128))
                theirs = jnp.broadcast_to(held[other, j, 14:15].astype(F32), (4, 128))
                return mine + jnp.where(upright, theirs, 0.0)

            for j in range(8):
                total = held[k + 1, j, pr * 4 : pr * 4 + 4].astype(F32)
                total = total + jnp.where(upright, held[other, j, 8:12].astype(F32), 0.0)
                if j > 0:
                    total = total + jnp.where((row == 0) & (lane % 64 < 32), edge(j - 1), 0.0)
                if j < 7:
                    total = total + jnp.where((row == 3) & (lane % 64 >= 32), edge(j + 1), 0.0)
                sums[pl.ds((2 * k + pr) * 32 + j * 4, 4)] = total + bias[...]
    out[...] = sums[...].astype(BF16)


def shape(*dims, dtype=BF16):
    return jax.ShapeDtypeStruct(dims, dtype)


def params(limit):
    return pltpu.CompilerParams(vmem_limit_bytes=limit * 2**20)


def around(axis, step):
    count = lax.axis_size(axis)
    return [(n, (n + step) % count) for n in range(count)]


def local(
    features, cache_first, cache_second, cache_head, gain_first, gain_second, gain_head,
    conv_first, conv_second, conv_head, bias_first, bias_second, bias_head,
):
    own, raw, lo, hi = pl.pallas_call(
        first_kernel,
        out_shape=[shape(32, F, C), shape(32, F, C), shape(MSG, F, C), shape(MSG, F, C)],
        in_specs=[ANY] * 4,
        out_specs=[VM] * 4,
        scratch_shapes=[
            pltpu.VMEM((F, R, Q, C), BF16),
            pltpu.VMEM((2, R, Q, C), BF16),
            pltpu.VMEM((2, R, Q, C), BF16),
            pltpu.VMEM((C,), F32),
            pltpu.VMEM((3, F * R * Q, 128), F32),
            pltpu.VMEM((3, F * R * Q, 128), F32),
            pltpu.SemaphoreType.DMA((4,)),
        ],
        compiler_params=params(16),
        name="act_first",
    )(features, cache_first, cache_second, gain_first)
    top = lax.ppermute(hi, "ha", around("ha", 1))
    bot = lax.ppermute(lo, "ha", around("ha", -1))
    to_left, to_right = pl.pallas_call(
        second_kernel,
        out_shape=[shape(MSG, F, C)] * 2,
        in_specs=[VM] * 3 + [ANY] * 2,
        out_specs=[VM] * 2,
        scratch_shapes=[
            pltpu.VMEM((2, R, Q, C), BF16),
            pltpu.VMEM((2, R, Q, C), BF16),
            pltpu.VMEM((3, 128, 128), F32),
            pltpu.VMEM((3, 128, 128), F32),
            pltpu.SemaphoreType.DMA((2,)),
        ],
        compiler_params=params(16),
        name="pack_columns",
    )(own, top, bot, cache_first, cache_second)
    left = lax.ppermute(to_right, "wa", around("wa", 1))
    right = lax.ppermute(to_left, "wa", around("wa", -1))
    slots = pl.pallas_call(
        main_kernel,
        out_shape=shape(F, 8, 16, 128),
        in_specs=[VM] * 6 + [ANY] * 10,
        out_specs=VM,
        scratch_shapes=[
            pltpu.VMEM((R + 4, Q + 4, F, 3 * C), BF16),
            pltpu.VMEM((R + 2, Q + 2, F, 3 * C), BF16),
            pltpu.VMEM((R * Q, F, 3 * C), BF16),
            pltpu.VMEM((R + 2, Q + 2, F, C), F32),
            pltpu.VMEM((R, Q, F, C), F32),
            pltpu.VMEM((16 * F, 128), F32),
            pltpu.VMEM((3, 9, C, C), BF16),
            pltpu.VMEM((3, 9, C, C), BF16),
            pltpu.VMEM((3, 3, 3, C, 32), BF16),
            pltpu.VMEM((3 * C, 3 * 128), BF16),
            pltpu.VMEM((3, 128, 128), F32),
            pltpu.VMEM((3, 128, 128), F32),
            pltpu.VMEM((2, 32, C), F32),
            pltpu.VMEM((2, 16, C), F32),
            pltpu.VMEM((64, C), F32),
            pltpu.VMEM((2, R, Q, C), BF16),
            pltpu.VMEM((2, R, Q, C), BF16),
            pltpu.VMEM((2, R, Q, C), BF16),
            pltpu.VMEM((C,), F32),
            pltpu.VMEM((C,), F32),
            pltpu.VMEM((C,), F32),
            pltpu.VMEM((C,), F32),
            pltpu.SemaphoreType.DMA((7,)),
            pltpu.SemaphoreType.DMA((7,)),
        ],
        compiler_params=params(56),
        name="block",
    )(
        own, raw, top, bot, left, right, cache_first, cache_second, cache_head,
        gain_second, gain_head, bias_first, bias_second, conv_first, conv_second, conv_head,
    )
    arrived = lax.all_to_all(slots.reshape(F * 8, 16, 128), ("ha", "wa"), 0, 0, tiled=True)
    return pl.pallas_call(
        last_kernel,
        out_shape=shape(128, 128),
        in_specs=[ANY, VM],
        out_specs=VM,
        scratch_shapes=[
            pltpu.VMEM((4, 8, 16, 128), BF16),
            pltpu.VMEM((128, 128), F32),
            pltpu.SemaphoreType.DMA((4,)),
        ],
        compiler_params=params(16),
        name="sum_patches",
    )(arrived, jnp.tile(bias_head, 4).reshape(1, 128))


def solution(mesh):
    tile = P(None, "ha", "wa", None)
    return jax.shard_map(
        local,
        mesh=mesh,
        in_specs=(tile,) * 4 + (P(),) * 9,
        out_specs=P(("ha", "wa"), None),
        check_vma=False,
    )
```

time: 108 us -> 80.4 us (0.74); the launches traced: 106 us -> 80 us
  local copies, waits for them, and re-layouts: 35.3 us -> 7.73 us
  waiting for transfers between devices: 13.6 us -> 20.7 us
  other arithmetic: 4.09 us -> 0 us
  Pallas kernels: 37.7 us -> 33.7 us
  starting transfers between devices: 15.3 us -> 17.8 us
    concatenate x4 -> x0, local copies, waits for them, and re-layouts: 20.8 us -> none  [head_weights(): sets.append(jnp.concatenate(parts, axis=-1))]
    ppermute x1, waiting for transfers between devices: 0.01 us -> 5.28 us  [local(): top = lax.ppermute(hi, 'ha', around('ha', 1))]
    another operation x1 -> x0, other arithmetic: 4.09 us -> none  [head_weights(): return jnp.stack(sets)]
    transpose x1 -> x0, local copies, waits for them, and re-layouts: 3.68 us -> none  [head_weights(): flat = jnp.transpose(conv_head, (1, 2, 0, 3, 4)).reshape(3, 3, 3 * C, 32)]
    unnamed x32 -> x23, local copies, waits for them, and re-layouts: 4.15 us -> 7.65 us
    pallas_call x1, Pallas kernels: 33.8 us -> 30.6 us  [local(): pl.pallas_call(main_kernel, out_shape=shape(F, 8, 16, 128), in_specs=[VM]...]
    reshape x5 -> x0, local copies, waits for them, and re-layouts: 2.92 us -> none  [local(): line = lambda v: v.reshape(1, -1)]
    squeeze x1 -> x0, local copies, waits for them, and re-layouts: 2.85 us -> none  [head_weights(): parts.append(flat[a, b] if 0 <= a <= 2 and 0 <= b <= 2 else none)]
  transfers between devices with their start and end apart: 5 -> 5, of which waited for: 1 -> 3; matrix products, arithmetic and copies ran while one was open for 33% -> 5% of each run, Pallas kernels for 0% -> 0%
where the time goes in v2:
time: 80.4 us; the launch traced here: 80 us
  Pallas kernels  33.7 us (42%)
  waiting for transfers between devices  20.7 us (26%)
  starting transfers between devices  17.8 us (22%)
  local copies, waits for them, and re-layouts  7.73 us (10%)
    pallas_call x1, Pallas kernels, local(): pl.pallas_call(main_kernel, out_shape=shape(F, 8, 16, 128), in_specs=[VM]...  30.6 us
    all_to_all x1, waiting for transfers between devices, local(): lax.all_to_all(slots.reshape(F * 8, 16, 128), ('ha', 'wa'), 0, 0, tiled=T...  13.6 us
    all_to_all x1, starting transfers between devices, local(): lax.all_to_all(slots.reshape(F * 8, 16, 128), ('ha', 'wa'), 0, 0, tiled=T...  9.11 us
    unnamed x23, local copies, waits for them, and re-layouts  7.65 us
    ppermute x1, waiting for transfers between devices, local(): top = lax.ppermute(hi, 'ha', around('ha', 1))  5.28 us
    ppermute x1, starting transfers between devices, local(): bot = lax.ppermute(lo, 'ha', around('ha', -1))  3.71 us
    ppermute x1, starting transfers between devices, local(): left = lax.ppermute(to_right, 'wa', around('wa', 1))  2.82 us
    ppermute x1, starting transfers between devices, local(): top = lax.ppermute(hi, 'ha', around('ha', 1))  2.19 us
  transfers between devices with their start and end apart: 5, of which 3 were waited for; matrix products, arithmetic and copies ran while one was open for 5% of the time, Pallas kernels for 0%

profile of v2, /device:TPU:1, one launch (start us, length us, event | category | flops | bytes accessed | tf_op | source)
XLA Modules:
  0.0 80.0 jit_solution(16615565238226663787)
XLA Ops:
  0.0 0.8 copy-done.3
  0.8 0.8 copy-done.4
  1.6 1.0 %copy-done.5 = bf16[16,4,8,384]{3,2,1,0:T(8,128)(2,1)S(1)} copy-done((bf16[16,4,8,384]{3,2,1,0:T(8,128)(2,1)S(1)}, bf16[16,4,8,384]{3,2,1,0:T(8,128)(2,1)}, u32[]{:S(2)}) %copy-start.5) | copy-done | bytes 393240
  2.6 0.7 copy-done.7
  3.3 2.0 %act_first.1 = (bf16[32,16,384]{2,1,0:T(8,128)(2,1)S(1)}, bf16[32,16,384]{2,1,0:T(8,128)(2,1)S(1)}, bf16[19,16,384]{2,1,0:T(8,128)(2,1)S(1)}, bf16[19,16,384]{2,1,0:T(8,128)(2,1)S(1)}) custom-call(bf16[16,4,8,384]{3,2,1,0:T(8,128)(2,1)S(1)} %copy-done.5, bf16[2,4,8,384]{3,2,1,0:T(8,128)(2,1)S(1)} %copy-done.3, bf16[2,4,8,384]{3,2,1,0:T(8,128)(2,1)S(1)} %copy-done.4, ...), custom_call_target="tpu_custom_call" | custom-call | tf_op jit(solution)/shard_map/act_first/pallas_call | solution.py:328
  5.3 0.0 copy-start.6
  5.3 2.2 %collective-permute-start = (bf16[19,16,384]{2,1,0:T(8,128)(2,1)S(1)}, bf16[19,16,384]{2,1,0:T(8,128)(2,1)S(1)}, u32[]{:S(2)}, u32[]{:S(2)}) collective-permute-start(bf16[19,16,384]{2,1,0:T(8,128)(2,1)S(1)} %get-tuple-element.13), channel_id=1, source_target_pairs={{0,8},{8,16},{16,24},{24,32},{32,40},{40,48},{48,56},{56,64},{64,7... | collective-permute-start | bytes 700424 | tf_op jit(solution)/shard_map/ppermute | solution.py:345
  7.5 3.7 %collective-permute-start.1 = (bf16[19,16,384]{2,1,0:T(8,128)(2,1)S(1)}, bf16[19,16,384]{2,1,0:T(8,128)(2,1)S(1)}, u32[]{:S(2)}, u32[]{:S(2)}) collective-permute-start(bf16[19,16,384]{2,1,0:T(8,128)(2,1)S(1)} %get-tuple-element.14), channel_id=1, source_target_pairs={{0,120},{8,0},{16,8},{24,16},{32,24},{40,32},{48,40},{56,48},{64,5... | collective-permute-start | bytes 700424 | tf_op jit(solution)/shard_map/ppermute | solution.py:346
  11.2 5.3 %collective-permute-done.top = bf16[19,16,384]{2,1,0:T(8,128)(2,1)S(1)} collective-permute-done((bf16[19,16,384]{2,1,0:T(8,128)(2,1)S(1)}, bf16[19,16,384]{2,1,0:T(8,128)(2,1)S(1)}, u32[]{:S(2)}, u32[]{:S(2)}) %collective-permute-start) | collective-permute-done | bytes 233504 | tf_op jit(solution)/shard_map/ppermute | solution.py:345
  16.5 0.0 collective-permute-done.1.bot
  16.5 0.2 pack_columns.1
  16.7 2.8 %collective-permute-start.2 = (bf16[19,16,384]{2,1,0:T(8,128)(2,1)S(1)}, bf16[19,16,384]{2,1,0:T(8,128)(2,1)S(1)}, u32[]{:S(2)}, u32[]{:S(2)}) collective-permute-start(bf16[19,16,384]{2,1,0:T(8,128)(2,1)S(1)} %get-tuple-element.15), channel_id=1, source_target_pairs={{0,1},{1,2},{2,3},{3,4},{4,5},{5,6},{6,7},{7,0},{8,9},{9,10},{10,1... | collective-permute-start | bytes 700424 | tf_op jit(solution)/shard_map/ppermute | solution.py:362
  19.6 0.0 collective-permute-start.3
  19.6 3.7 %copy.14.wh = bf16[3,3,3,384,32]{4,3,2,1,0:T(8,128)(2,1)} copy(bf16[3,3,3,384,32]{3,4,2,1,0:T(8,128)(2,1)} %param.22) | data formatting | bytes 1327104 | tf_op args[9]
  23.2 0.0 collective-permute-done.2.left
  23.2 1.8 %collective-permute-done.3.right = bf16[19,16,384]{2,1,0:T(8,128)(2,1)S(1)} collective-permute-done((bf16[19,16,384]{2,1,0:T(8,128)(2,1)S(1)}, bf16[19,16,384]{2,1,0:T(8,128)(2,1)S(1)}, u32[]{:S(2)}, u32[]{:S(2)}) %collective-permute-start.3) | collective-permute-done | bytes 233504 | tf_op jit(solution)/shard_map/ppermute | solution.py:363
  25.1 0.0 copy-done.1
  25.1 0.0 copy-done.8
  25.1 0.7 copy-done.9
  25.8 30.6 %block.1 = bf16[16,8,16,128]{3,2,1,0:T(8,128)(2,1)} custom-call(bf16[32,16,384]{2,1,0:T(8,128)(2,1)} %copy-done, bf16[32,16,384]{2,1,0:T(8,128)(2,1)} %copy-done.6, bf16[19,16,384]{2,1,0:T(8,128)(2,1)} %copy-done.1, bf16[19,16,384]{2,1,0:T(8,128)(2,1)} %copy-done.2, bf16[19,16,384]{2,1,0:T(8,128)(2,1)} %copy-done.8, bf16[19,16,384]{2,1,0:T(8,128)(2,1)} %copy-done.9, ...), custom_call_target="tpu_custom_call" | custom-call | tf_op jit(solution)/shard_map/block/pallas_call | solution.py:364
  56.4 9.1 %all-to-all-start = ((bf16[128,16,128]{2,1,0:T(8,128)(2,1)}), bf16[128,16,128]{2,1,0:T(8,128)(2,1)S(1)}, u32[]{:S(2)}, u32[]{:S(2)}) async-start(bf16[128,16,128]{2,1,0:T(8,128)(2,1)} %bitcast.1), calls=%async_computation | async-start | bytes 1048576 | tf_op jit(solution)/shard_map/all_to_all | solution.py:401
  65.5 0.1 reshape_tile.3.bias
  65.6 13.6 %all-to-all-done.slots = bf16[128,16,128]{2,1,0:T(8,128)(2,1)S(1)} async-done(((bf16[128,16,128]{2,1,0:T(8,128)(2,1)}), bf16[128,16,128]{2,1,0:T(8,128)(2,1)S(1)}, u32[]{:S(2)}, u32[]{:S(2)}) %all-to-all-start) | async-done | bytes 524320 | tf_op jit(solution)/shard_map/all_to_all | solution.py:401
  79.2 0.9 %sum_patches.1 = bf16[128,128]{1,0:T(8,128)(2,1)} custom-call(bf16[128,16,128]{2,1,0:T(8,128)(2,1)S(1)} %all-to-all-done.slots, f32[1,128]{1,0:T(1,128)S(1)} %reshape_tile.3.bias), custom_call_target="tpu_custom_call" | custom-call | tf_op jit(solution)/shard_map/sum_patches/pallas_call | solution.py:402
  (15 shorter events, 0.0 us)
Async XLA Ops:
  0.0 0.8 copy-start.3
  0.8 0.8 copy-start.4
  1.6 1.0 %copy-start.5 = (bf16[16,4,8,384]{3,2,1,0:T(8,128)(2,1)S(1)}, bf16[16,4,8,384]{3,2,1,0:T(8,128)(2,1)}, u32[]{:S(2)}) copy-start(bf16[16,4,8,384]{3,2,1,0:T(8,128)(2,1)} %feat_h.1) | copy-start | bytes 1179652
  2.6 0.7 copy-start.7
  5.3 11.5 %copy-start.6 = (bf16[32,16,384]{2,1,0:T(8,128)(2,1)}, bf16[32,16,384]{2,1,0:T(8,128)(2,1)S(1)}, u32[]{:S(2)}) copy-start(bf16[32,16,384]{2,1,0:T(8,128)(2,1)S(1)} %get-tuple-element.12.raw) | copy-start | bytes 1179652
  5.3 19.8 %copy-start = (bf16[32,16,384]{2,1,0:T(8,128)(2,1)}, bf16[32,16,384]{2,1,0:T(8,128)(2,1)S(1)}, u32[]{:S(2)}) copy-start(bf16[32,16,384]{2,1,0:T(8,128)(2,1)S(1)} %get-tuple-element.11.own) | copy-start | bytes 1179652
  5.3 11.2 %collective-permute-start = (bf16[19,16,384]{2,1,0:T(8,128)(2,1)S(1)}, bf16[19,16,384]{2,1,0:T(8,128)(2,1)S(1)}, u32[]{:S(2)}, u32[]{:S(2)}) collective-permute-start(bf16[19,16,384]{2,1,0:T(8,128)(2,1)S(1)} %get-tuple-element.13), channel_id=1, source_target_pairs={{0,8},{8,16},{16,24},{24,32},{32,40},{40,48},{48,56},{56,64},{64,7... | collective-permute-start | bytes 700424 | tf_op jit(solution)/shard_map/ppermute | solution.py:345
  7.5 9.0 %collective-permute-start.1 = (bf16[19,16,384]{2,1,0:T(8,128)(2,1)S(1)}, bf16[19,16,384]{2,1,0:T(8,128)(2,1)S(1)}, u32[]{:S(2)}, u32[]{:S(2)}) collective-permute-start(bf16[19,16,384]{2,1,0:T(8,128)(2,1)S(1)} %get-tuple-element.14), channel_id=1, source_target_pairs={{0,120},{8,0},{16,8},{24,16},{32,24},{40,32},{48,40},{56,48},{64,5... | collective-permute-start | bytes 700424 | tf_op jit(solution)/shard_map/ppermute | solution.py:346
  16.5 8.6 %copy-start.1 = (bf16[19,16,384]{2,1,0:T(8,128)(2,1)}, bf16[19,16,384]{2,1,0:T(8,128)(2,1)S(1)}, u32[]{:S(2)}) copy-start(bf16[19,16,384]{2,1,0:T(8,128)(2,1)S(1)} %collective-permute-done.top) | copy-start | bytes 700420
  16.5 8.6 %copy-start.2 = (bf16[19,16,384]{2,1,0:T(8,128)(2,1)}, bf16[19,16,384]{2,1,0:T(8,128)(2,1)S(1)}, u32[]{:S(2)}) copy-start(bf16[19,16,384]{2,1,0:T(8,128)(2,1)S(1)} %collective-permute-done.1.bot) | copy-start | bytes 700420
  16.7 6.5 %collective-permute-start.2 = (bf16[19,16,384]{2,1,0:T(8,128)(2,1)S(1)}, bf16[19,16,384]{2,1,0:T(8,128)(2,1)S(1)}, u32[]{:S(2)}, u32[]{:S(2)}) collective-permute-start(bf16[19,16,384]{2,1,0:T(8,128)(2,1)S(1)} %get-tuple-element.15), channel_id=1, source_target_pairs={{0,1},{1,2},{2,3},{3,4},{4,5},{5,6},{6,7},{7,0},{8,9},{9,10},{10,1... | collective-permute-start | bytes 700424 | tf_op jit(solution)/shard_map/ppermute | solution.py:362
  19.6 5.5 %collective-permute-start.3 = (bf16[19,16,384]{2,1,0:T(8,128)(2,1)S(1)}, bf16[19,16,384]{2,1,0:T(8,128)(2,1)S(1)}, u32[]{:S(2)}, u32[]{:S(2)}) collective-permute-start(bf16[19,16,384]{2,1,0:T(8,128)(2,1)S(1)} %get-tuple-element.16), channel_id=1, source_target_pairs={{0,7},{1,0},{2,1},{3,2},{4,3},{5,4},{6,5},{7,6},{8,15},{9,8},{10,9... | collective-permute-start | bytes 700424 | tf_op jit(solution)/shard_map/ppermute | solution.py:363
  23.2 1.8 %copy-start.8 = (bf16[19,16,384]{2,1,0:T(8,128)(2,1)}, bf16[19,16,384]{2,1,0:T(8,128)(2,1)S(1)}, u32[]{:S(2)}) copy-start(bf16[19,16,384]{2,1,0:T(8,128)(2,1)S(1)} %collective-permute-done.2.left) | copy-start | bytes 700420
  25.1 0.7 copy-start.9
  25.8 39.7 %copy-start.10 = (f32[32]{0:T(128)S(1)}, f32[32]{0:T(128)}, u32[]{:S(2)}) copy-start(f32[32]{0:T(128)} %param.25) | copy-start | bytes 388
  56.4 22.8 %all-to-all-start = ((bf16[128,16,128]{2,1,0:T(8,128)(2,1)}), bf16[128,16,128]{2,1,0:T(8,128)(2,1)S(1)}, u32[]{:S(2)}, u32[]{:S(2)}) async-start(bf16[128,16,128]{2,1,0:T(8,128)(2,1)} %bitcast.1), calls=%async_computation | async-start | bytes 1048576 | tf_op jit(solution)/shard_map/all_to_all | solution.py:401

commit v3 on v2

v3 whole, which is shorter than its diff:
```python
import jax
import jax.numpy as jnp
from jax import lax
from jax.experimental import pallas as pl
from jax.experimental.pallas import tpu as pltpu
from jax.sharding import PartitionSpec as P

BF16 = jnp.bfloat16
F32 = jnp.float32
F, R, Q, C = 16, 4, 8, 384
MSG = 19
VM = pl.BlockSpec(memory_space=pltpu.VMEM)
ANY = pl.BlockSpec(memory_space=pl.ANY)


def act(wide, half_gain):
    scale = lax.rsqrt(jnp.mean(wide * wide, axis=-1, keepdims=True) + 1e-06)
    h = wide * scale * half_gain
    return h + h * jnp.tanh(h)


def line(ref):
    return ref[...].reshape(1, -1)


def put_rows(ref, start, value):
    for n in range(3):
        ref[n, pl.ds(start, value.shape[0])] = value[:, n * 128 : (n + 1) * 128]


def rows_at(ref, start, count, stride):
    where = pl.ds(start, count, stride=stride) if stride > 1 else pl.ds(start, count)
    return jnp.concatenate([ref[n, where, :] for n in range(3)], axis=-1)


def stack(now, c0, c1):
    row = lax.broadcasted_iota(jnp.int32, now.shape, 0) % F
    c0, c1 = (jnp.concatenate([jnp.broadcast_to(c, (F, C)) for c in cs], axis=0) for cs in (c0, c1))
    one = jnp.where(row == 0, c1, pltpu.roll(now, 1, 0))
    two = jnp.where(row == 0, c0, jnp.where(row == 1, c1, pltpu.roll(now, 2, 0)))
    return two.astype(BF16), one.astype(BF16), now.astype(BF16)


def put(dst, where, now, c0, c1, valid=None):
    if valid is not None:
        keep = jnp.where(valid, 1.0, 0.0).astype(F32)
        now, c0, c1 = now * keep, [c * keep for c in c0], [c * keep for c in c1]
    for n, part in enumerate(stack(now, c0, c1)):
        dst[where + (slice(None), pl.ds(n * C, C))] = part.reshape(-1, F, C)


def bring(pairs, sems):
    copies = [pltpu.make_async_copy(src, dst, sems.at[n]) for n, (src, dst) in enumerate(pairs)]
    for copy in copies:
        copy.start()
    return copies


def first_kernel(
    feat_h, cf_h, cs_h, ch_h, g1_h, g2_h, gh_h, b1_h, b2_h, own, raw, lo, hi, cfw, csw, chw, vec,
    feat, caches, g1, g2, gh, b1, b2, wide, plain, sems,
):
    copies = bring(
        ((g1_h, g1), (feat_h, feat), (cf_h, caches.at[0]), (cs_h, caches.at[1]), (ch_h, caches.at[2]),
         (g2_h, g2), (gh_h, gh), (b1_h, b1), (b2_h, b2)), sems
    )
    copies[0].wait()
    copies[1].wait()
    half = 0.5 * line(g1)

    def frame(f, _):
        x = feat[pl.ds(f * 4, 4)].astype(F32).reshape(4 * R * Q, C)
        put_rows(plain, f * 4 * R * Q, x)
        put_rows(wide, f * 4 * R * Q, act(x, half))
        return 0

    lax.fori_loop(0, F // 4, frame, 0)
    for k in range(R * Q):
        cell = rows_at(wide, k, F, R * Q).astype(BF16)
        own[k] = cell
        if k < 16:
            lo[k] = cell
        else:
            hi[k - 16] = cell
        raw[k] = rows_at(plain, k, F, R * Q).astype(BF16)
    for copy in copies[2:]:
        copy.wait()
    for n, value in enumerate((0.5 * line(g2), 0.5 * line(gh), line(b1), line(b2))):
        vec[pl.ds(n, 1)] = value
    for n, out in enumerate((cfw, csw, chw)):
        for h in range(R):
            for f in range(2):
                put_rows(out, h * 16 + f * 8, caches[n, f, h].astype(F32))
    for n in range(2):
        lo[16 + n] = rows_at(cfw, n * 16, 16, 1).astype(BF16)
        hi[16 + n] = rows_at(cfw, (2 + n) * 16, 16, 1).astype(BF16)
    lo[18] = rows_at(csw, 0, 16, 1).astype(BF16)
    hi[18] = rows_at(csw, 48, 16, 1).astype(BF16)


def pack_kernel(own, top, bot, cfw, csw, left, right, wide_f, wide_s):
    for n in range(2):
        put_rows(wide_f, n * 16, top[16 + n].astype(F32))
        put_rows(wide_f, (6 + n) * 16, bot[16 + n].astype(F32))
    put_rows(wide_s, 0, top[18].astype(F32))
    put_rows(wide_s, 5 * 16, bot[18].astype(F32))
    for n in range(3):
        wide_f[n, pl.ds(32, 64)] = cfw[n]
        wide_s[n, pl.ds(16, 64)] = csw[n]
        wide_s[n, pl.ds(96, 32)] = jnp.zeros((32, 128), F32)
    for out, base, edge in ((left, 0, 0), (right, 6, 7)):
        for c in range(2):
            for h in range(8):
                w = base + c
                if h < 2:
                    cell = top[h * Q + w]
                elif h < 6:
                    cell = own[(h - 2) * Q + w]
                else:
                    cell = bot[(h - 6) * Q + w]
                out[h * 2 + c] = cell
            out[16 + c] = rows_at(wide_f, base + c, 16, 8).astype(BF16)
        out[18] = rows_at(wide_s, edge, 16, 8).astype(BF16)


def cached_row(ref, base, w0, count):
    return [[rows_at(ref, base + 8 * f + w0 + w, 1, 1) for w in range(count)] for f in range(2)]


def cached_msg(block, count=Q):
    block = block.astype(F32)
    return [[block[8 * f + w : 8 * f + w + 1] for w in range(count)] for f in range(2)]


def taps(src, weight, a):
    return jnp.dot(src, weight[a].reshape(9 * C, C), preferred_element_type=F32)


def hidden(dst, where, total, vec, cached, valid=None):
    wide = (total + vec[pl.ds(2, 1), :]).astype(BF16).astype(F32)
    put(dst, where, act(wide, vec[pl.ds(0, 1), :]), cached[0], cached[1], valid)


def place():
    ha, wa = lax.axis_index("ha"), lax.axis_index("wa")
    return ha > 0, ha < lax.axis_size("ha") - 1, wa > 0, wa < lax.axis_size("wa") - 1


def inner_kernel(own, cfw, csw, vec, w1, w2, wh, s1, s2, w1v, w2v, wy, acc, sems):
    def group(src, dst, a, sem):
        return [
            pltpu.make_async_copy(src.at[t, a, b], dst.at[a, b * 3 + t], sem) for b in range(3) for t in range(3)
        ]

    first = [group(w1, w1v, a, sems.at[a]) for a in range(3)]
    later = [copy for a in range(3) for copy in group(w2, w2v, a, sems.at[3 + a])]
    for t in range(3):
        for a in range(3):
            for b in range(3):
                later.append(
                    pltpu.make_async_copy(
                        wh.at[t, a, b], wy.at[pl.ds(a * 128 + b * 32, 32), pl.ds(t * C, C)], sems.at[6]
                    )
                )
    for copies in first[:2]:
        for copy in copies:
            copy.start()
    for a in range(3):
        wy[pl.ds(a * 128 + 96, 32)] = jnp.zeros((32, 3 * C), BF16)

    def cells(h, _):
        c0, c1 = cached_row(cfw, h * 16, 0, Q)
        put(s1, (h, pl.ds(0, Q)), own[pl.ds(h * Q, Q)].reshape(Q * F, C).astype(F32), c0, c1)
        return 0

    lax.fori_loop(0, R, cells, 0)
    for a in range(3):
        for copy in first[a]:
            copy.wait()
        for copy in (first[2], later, ())[a]:
            copy.start()
        taken = jnp.concatenate([s1[a : a + 2, b : b + 6].reshape(12 * F, 3 * C) for b in range(3)], axis=-1)
        if a == 0:
            acc[...] = taps(taken, w1v, a)
        else:
            acc[...] += taps(taken, w1v, a)
    for h in range(2):
        hidden(s2, (h, pl.ds(0, 6)), acc[pl.ds(h * 6 * F, 6 * F)], vec, cached_row(csw, (1 + h) * 16, 1, 6))
    for copy in later:
        copy.wait()


def rows_kernel(top, bot, own1, csw, vec, w1v, s1, s2, acc):
    up, down, _, _ = place()
    for msg, h0, valid in ((top, 0, up), (bot, 6, down)):
        for h in range(2):
            c0, c1 = cached_msg(msg[16 + h])
            put(s1, (h0 + h, pl.ds(0, Q)), msg[pl.ds(h * Q, Q)].reshape(Q * F, C).astype(F32), c0, c1, valid)
    s1[2:6] = own1[...]
    for a in range(3):
        taken = jnp.concatenate(
            [
                jnp.concatenate(
                    [s1[4 * n + a : 4 * n + a + 2, b : b + 6].reshape(12 * F, 3 * C) for n in range(2)], axis=0
                )
                for b in range(3)
            ],
            axis=-1,
        )
        if a == 0:
            acc[...] = taps(taken, w1v, a)
        else:
            acc[...] += taps(taken, w1v, a)
    for n, cached, valid in (
        (0, [c[1:7] for c in cached_msg(top[18])], up),
        (1, cached_row(csw, 0, 1, 6), None),
        (2, cached_row(csw, 48, 1, 6), None),
        (3, [c[1:7] for c in cached_msg(bot[18])], down),
    ):
        hidden(s2, (n, pl.ds(0, 6)), acc[pl.ds(n * 6 * F, 6 * F)], vec, cached, valid)


def finish_kernel(
    left, right, top, bot, s1, inner2, rows2, raw, csw, chw, vec, w1v, w2v, wy, out,
    sides, s2, s3, acc1, acc2, acch, side_f, side_s,
):
    up, down, west, east = place()
    for n, msg in enumerate((left, right)):
        for c in range(2):
            side_f[n, pl.ds(c * 16, 16)] = msg[16 + c].astype(F32)
        side_s[n] = msg[18].astype(F32)
    sides[:, 0, 2:4] = s1[:, 0:2]
    sides[:, 1, 0:2] = s1[:, 6:8]
    for n, (msg, side, w0) in enumerate(((left, west, 0), (right, east, 2))):
        def cells(h, _, n=n, msg=msg, side=side, w0=w0):
            for k in range(2):
                hh = h * 2 + k
                put(
                    sides, (hh, n, pl.ds(w0, 2)), msg[pl.ds(hh * 2, 2)].reshape(2 * F, C).astype(F32),
                    [side_f[n, pl.ds(c * 16 + hh * 2, 1), :] for c in range(2)],
                    [side_f[n, pl.ds(c * 16 + hh * 2 + 1, 1), :] for c in range(2)],
                    side & (up | (hh >= 2)) & (down | (hh < 6)),
                )
            return 0

        lax.fori_loop(0, 4, cells, 0)

    for a in range(3):
        taken = jnp.concatenate(
            [sides[a : a + 6, :, b : b + 2].reshape(24 * F, 3 * C) for b in range(3)], axis=-1
        )
        if a == 0:
            acc1[...] = taps(taken, w1v, a)
        else:
            acc1[...] += taps(taken, w1v, a)
    s2[2:4, 2:8] = inner2[...]
    s2[0:2, 2:8] = rows2[0:2]
    s2[4:6, 2:8] = rows2[2:4]
    for h in range(6):
        inside = up if h == 0 else down if h == 5 else True
        if h == 0:
            c0, c1 = cached_msg(top[18])
        elif h == 5:
            c0, c1 = cached_msg(bot[18])
        else:
            c0, c1 = cached_row(csw, (h - 1) * 16, 0, Q)
        for n, side in enumerate((west, east)):
            first = [side_s[n, pl.ds(h * 2 + f, 1), :] for f in range(2)]
            keep = jnp.where(side, 1.0, 0.0).astype(F32)
            total = acc1[pl.ds((h * 2 + n) * 2 * F, 2 * F)]
            wide = (total + vec[pl.ds(2, 1), :]).astype(BF16).astype(F32)
            now = act(wide, vec[pl.ds(0, 1), :])
            own_w = 0 if n == 0 else Q - 1
            pair = [now[:F], now[F:]]
            pair[n] = pair[n] * keep
            now = jnp.concatenate(pair, axis=0)
            olds = []
            for f, c in enumerate((c0, c1)):
                two = [first[f] * keep, c[own_w]]
                olds.append(two if n == 0 else two[::-1])
            put(s2, (h, pl.ds(8 * n, 2)), now, olds[0], olds[1], None if inside is True else inside)

    for a in range(3):
        taken = jnp.concatenate([s2[a : a + R, b : b + Q].reshape(R * Q * F, 3 * C) for b in range(3)], axis=-1)
        if a == 0:
            acc2[...] = taps(taken, w2v, a)
        else:
            acc2[...] += taps(taken, w2v, a)

    def last(h, _):
        wide = acc2[pl.ds(h * Q * F, Q * F)] + vec[pl.ds(3, 1), :]
        wide = wide + raw[pl.ds(h * Q, Q)].reshape(Q * F, C).astype(F32)
        c0, c1 = cached_row(chw, h * 16, 0, Q)
        put(s3, (pl.ds(h * Q, Q),), act(wide.astype(BF16).astype(F32), vec[pl.ds(1, 1), :]), c0, c1)
        return 0

    lax.fori_loop(0, R, last, 0)
    part = lax.dot_general(
        s3[...].reshape(R * Q * F, 3 * C), wy[...], (((1,), (1,)), ((), ())), preferred_element_type=F32
    )
    lane = lax.broadcasted_iota(jnp.int32, (F, 128), 1)
    sums = {}
    for h in range(R):
        for w in range(Q):
            k = h * Q + w
            for a in range(3):
                block = part[k * F : (k + 1) * F, a * 128 : (a + 1) * 128]
                for b in range(3):
                    row, col = h + 1 - a, w + 1 - b
                    pp, qq = (row // 2) % 3, (col // 2) % 5
                    slot = pp * 4 + qq if qq < 4 else 12 + pp
                    low = (2 * (row % 2) + col % 2) * 32
                    shift = (low - 32 * b) % 128
                    moved = pltpu.roll(block, shift, 1) if shift else block
                    term = jnp.where((lane >= low) & (lane < low + 32), moved, 0.0)
                    sums[slot] = sums[slot] + term if slot in sums else term
    for slot, total in sums.items():
        acch[pl.ds(slot * F, F)] = total
    acch[pl.ds(15 * F, F)] = jnp.zeros((F, 128), F32)

    for f in range(F):
        patches = acch[pl.ds(f, 16, stride=F), :].astype(BF16)
        for g in range(8):
            out[f, g] = patches


def last_kernel(slots, bias, out, held, sums, sem):
    ha_count = 16
    g = lax.axis_index("wa")
    copies = []
    for k in range(4):
        i = jnp.clip(2 * g - 1 + k, 0, ha_count - 1)
        copies.append(pltpu.make_async_copy(slots.at[pl.ds(i * 8, 8)], held.at[k], sem.at[k]))
        copies[-1].start()
    for copy in copies:
        copy.wait()
    lane = lax.broadcasted_iota(jnp.int32, (4, 128), 1)
    row = lax.broadcasted_iota(jnp.int32, (4, 128), 0)
    for k in range(2):
        for pr in range(2):
            other = k if pr == 0 else k + 2
            there = (2 * g + k > 0) if pr == 0 else (2 * g + k < ha_count - 1)
            upright = ((lane < 64) if pr == 0 else (lane >= 64)) & there

            def edge(j, pr=pr, k=k, other=other, upright=upright):
                mine = jnp.broadcast_to(held[k + 1, j, 12 + pr : 13 + pr].astype(F32), (4, 128))
                theirs = jnp.broadcast_to(held[other, j, 14:15].astype(F32), (4, 128))
                return mine + jnp.where(upright, theirs, 0.0)

            for j in range(8):
                total = held[k + 1, j, pr * 4 : pr * 4 + 4].astype(F32)
                total = total + jnp.where(upright, held[other, j, 8:12].astype(F32), 0.0)
                if j > 0:
                    total = total + jnp.where((row == 0) & (lane % 64 < 32), edge(j - 1), 0.0)
                if j < 7:
                    total = total + jnp.where((row == 3) & (lane % 64 >= 32), edge(j + 1), 0.0)
                sums[pl.ds((2 * k + pr) * 32 + j * 4, 4)] = total + bias[...]
    out[...] = sums[...].astype(BF16)


def shape(*dims, dtype=BF16):
    return jax.ShapeDtypeStruct(dims, dtype)


def near(*dims, dtype=BF16):
    return pltpu.VMEM(dims, dtype)


def far(array):
    return pltpu.with_memory_space_constraint(array, pltpu.HBM)


def kernel(body, outs, ins, scratch, limit, name, flops=0, moved=0):
    return pl.pallas_call(
        body,
        out_shape=outs,
        in_specs=ins,
        out_specs=[VM] * len(outs),
        scratch_shapes=scratch,
        compiler_params=pltpu.CompilerParams(vmem_limit_bytes=limit * 2**20),
        cost_estimate=pl.CostEstimate(flops=flops, bytes_accessed=moved, transcendentals=0),
        name=name,
    )


def around(axis, step):
    count = lax.axis_size(axis)
    return [(n, (n + step) % count) for n in range(count)]


def local(
    features, cache_first, cache_second, cache_head, gain_first, gain_second, gain_head,
    conv_first, conv_second, conv_head, bias_first, bias_second, bias_head,
):
    own, raw, lo, hi, cfw, csw, chw, vec = kernel(
        first_kernel,
        [near(32, F, C), near(32, F, C), near(MSG, F, C), near(MSG, F, C)]
        + [near(3, 64, 128, dtype=F32)] * 3 + [near(8, C, dtype=F32)],
        [ANY] * 9,
        [
            pltpu.VMEM((F, R, Q, C), BF16),
            pltpu.VMEM((3, 2, R, Q, C), BF16),
        ]
        + [pltpu.VMEM((C,), F32)] * 5
        + [
            pltpu.VMEM((3, F * R * Q, 128), F32),
            pltpu.VMEM((3, F * R * Q, 128), F32),
            pltpu.SemaphoreType.DMA((9,)),
        ],
        12, "act_first",
    )(*[far(v) for v in (features, cache_first, cache_second, cache_head, gain_first, gain_second, gain_head,
                         bias_first, bias_second)])
    top = lax.ppermute(hi, "ha", around("ha", 1))
    bot = lax.ppermute(lo, "ha", around("ha", -1))
    cell_flops = 2 * F * 27 * C * C
    own1, inner2, w1v, w2v, wy = kernel(
        inner_kernel,
        [near(R, Q, F, 3 * C), near(2, 6, F, 3 * C), near(3, 9, C, C), near(3, 9, C, C), near(3 * 128, 3 * C)],
        [VM] * 4 + [ANY] * 3,
        [pltpu.VMEM((12 * F, C), F32), pltpu.SemaphoreType.DMA((7,))],
        8, "inner", 12 * cell_flops, 17 * 2**20,
    )(own, cfw, csw, vec, far(conv_first), far(conv_second), far(jnp.swapaxes(conv_head, 3, 4)))
    to_left, to_right = kernel(
        pack_kernel,
        [near(MSG, F, C)] * 2,
        [VM] * 5,
        [pltpu.VMEM((3, 128, 128), F32)] * 2,
        4, "pack_columns",
    )(own, top, bot, cfw, csw)
    left = lax.ppermute(to_right, "wa", around("wa", 1))
    right = lax.ppermute(to_left, "wa", around("wa", -1))
    s1, rows2 = kernel(
        rows_kernel,
        [near(8, Q, F, 3 * C), near(4, 6, F, 3 * C)],
        [VM] * 6,
        [pltpu.VMEM((24 * F, C), F32)],
        8, "rows", 24 * cell_flops, 10 * 2**20,
    )(top, bot, own1, csw, vec, w1v)
    (slots,) = kernel(
        finish_kernel,
        [shape(F, 8, 16, 128)],
        [VM] * 14,
        [
            pltpu.VMEM((8, 2, 4, F, 3 * C), BF16),
            pltpu.VMEM((R + 2, Q + 2, F, 3 * C), BF16),
            pltpu.VMEM((R * Q, F, 3 * C), BF16),
            pltpu.VMEM((24 * F, C), F32),
            pltpu.VMEM((R * Q * F, C), F32),
            pltpu.VMEM((16 * F, 128), F32),
            pltpu.VMEM((2, 32, C), F32),
            pltpu.VMEM((2, 16, C), F32),
        ],
        20, "finish", 60 * cell_flops, 20 * 2**20,
    )(left, right, top, bot, s1, inner2, rows2, raw, csw, chw, vec, w1v, w2v, wy)
    arrived = lax.all_to_all(slots.reshape(F * 8, 16, 128), ("ha", "wa"), 0, 0, tiled=True)
    return pl.pallas_call(
        last_kernel,
        out_shape=shape(128, 128),
        in_specs=[ANY, VM],
        out_specs=VM,
        scratch_shapes=[
            pltpu.VMEM((4, 8, 16, 128), BF16),
            pltpu.VMEM((128, 128), F32),
            pltpu.SemaphoreType.DMA((4,)),
        ],
        compiler_params=pltpu.CompilerParams(vmem_limit_bytes=8 * 2**20),
        name="sum_patches",
    )(arrived, jnp.tile(bias_head, 4).reshape(1, 128))


def solution(mesh):
    tile = P(None, "ha", "wa", None)
    return jax.shard_map(
        local,
        mesh=mesh,
        in_specs=(tile,) * 4 + (P(),) * 9,
        out_specs=P(("ha", "wa"), None),
        check_vma=False,
    )
```

time: 80.4 us -> 60.3 us (0.75)
  local copies, waits for them, and re-layouts: 7.73 us -> 0.09 us
  waiting for transfers between devices: 20.7 us -> 14.3 us
  Pallas kernels: 33.7 us -> 28.3 us
    unnamed x23 -> x2, local copies, waits for them, and re-layouts: 7.65 us -> 0.01 us
    pallas_call x3 -> x5, Pallas kernels: 32.8 us -> 27.5 us  [the longest x1 13.9 us: local(): kernel(finish_kernel, [shape(F, 8, 16, 128)], [VM] * 14, [pltpu.VMEM((8,...]
    ppermute x1, waiting for transfers between devices: 5.28 us -> 0.01 us  [local(): top = lax.ppermute(hi, 'ha', around('ha', 1))]
    ppermute x1, waiting for transfers between devices: 1.81 us -> 0.73 us  [local(): right = lax.ppermute(to_left, 'wa', around('wa', -1))]
  transfers between devices with their start and end apart: 5 -> 5, of which waited for: 3 -> 2; matrix products, arithmetic and copies ran while one was open for 5% -> 0% of each run, Pallas kernels for 0% -> 18%
where the time goes in v3:
time: 60.3 us; the launch traced here: 60.1 us
  Pallas kernels  28.3 us (47%)
  starting transfers between devices  17.2 us (29%)
  waiting for transfers between devices  14.3 us (24%)
    pallas_call x1, Pallas kernels, local(): kernel(finish_kernel, [shape(F, 8, 16, 128)], [VM] * 14, [pltpu.VMEM((8,...  13.9 us
    all_to_all x1, waiting for transfers between devices, local(): lax.all_to_all(slots.reshape(F * 8, 16, 128), ('ha', 'wa'), 0, 0, tiled=T...  13.6 us
    all_to_all x1, starting transfers between devices, local(): lax.all_to_all(slots.reshape(F * 8, 16, 128), ('ha', 'wa'), 0, 0, tiled=T...  8.7 us
    pallas_call x1, Pallas kernels, local(): kernel(inner_kernel, [near(R, Q, F, 3 * C), near(2, 6, F, 3 * C), near(3,...  5.95 us
    pallas_call x1, Pallas kernels, local(): kernel(rows_kernel, [near(8, Q, F, 3 * C), near(4, 6, F, 3 * C)], [VM] *...  4.74 us
    ppermute x1, starting transfers between devices, local(): bot = lax.ppermute(lo, 'ha', around('ha', -1))  3.71 us
    pallas_call x1, Pallas kernels, local(): kernel(first_kernel, [near(32, F, C), near(32, F, C), near(MSG, F, C), ne...  2.75 us
    ppermute x1, starting transfers between devices, local(): left = lax.ppermute(to_right, 'wa', around('wa', 1))  2.55 us
  transfers between devices with their start and end apart: 5, of which 2 were waited for; matrix products, arithmetic and copies ran while one was open for 0% of the time, Pallas kernels for 18%

profile of v3, /device:TPU:1, one launch (start us, length us, event | category | flops | bytes accessed | tf_op | source)
XLA Modules:
  0.0 60.1 jit_solution(13611697694140226943)
XLA Ops:
  0.0 2.8 %act_first.1 = (bf16[32,16,384]{2,1,0:T(8,128)(2,1)S(1)}, bf16[32,16,384]{2,1,0:T(8,128)(2,1)S(1)}, bf16[19,16,384]{2,1,0:T(8,128)(2,1)S(1)}, bf16[19,16,384]{2,...) custom-call(bf16[16,4,8,384]{3,2,1,0:T(8,128)(2,1)} %feat_h.1, ...), custom_call_target="tpu_custom_call" | custom-call | tf_op jit(solution)/shard_map/act_first/pallas_call | solution.py:395
  2.8 2.2 %collective-permute-start = (bf16[19,16,384]{2,1,0:T(8,128)(2,1)S(1)}, bf16[19,16,384]{2,1,0:T(8,128)(2,1)S(1)}, u32[]{:S(2)}, u32[]{:S(2)}) collective-permute-start(bf16[19,16,384]{2,1,0:T(8,128)(2,1)S(1)} %get-tuple-element.23), channel_id=1, source_target_pairs={{0,8},{8,16},{16,24},{24,32},{32,40},{40,48},{48,56},{56,64},{64,7... | collective-permute-start | bytes 700424 | tf_op jit(solution)/shard_map/ppermute | solution.py:413
  5.0 3.7 %collective-permute-start.1 = (bf16[19,16,384]{2,1,0:T(8,128)(2,1)S(1)}, bf16[19,16,384]{2,1,0:T(8,128)(2,1)S(1)}, u32[]{:S(2)}, u32[]{:S(2)}) collective-permute-start(bf16[19,16,384]{2,1,0:T(8,128)(2,1)S(1)} %get-tuple-element.24), channel_id=1, source_target_pairs={{0,120},{8,0},{16,8},{24,16},{32,24},{40,32},{48,40},{56,48},{64,5... | collective-permute-start | bytes 700424 | tf_op jit(solution)/shard_map/ppermute | solution.py:414
  8.7 6.0 %inner.1 = (bf16[4,8,16,1152]{3,2,1,0:T(8,128)(2,1)S(1)}, bf16[2,6,16,1152]{3,2,1,0:T(8,128)(2,1)S(1)}, bf16[3,9,384,384]{3,2,1,0:T(8,128)(2,1)S(1)}, bf16[3,9,3...) custom-call(bf16[32,16,384]{2,1,0:T(8,128)(2,1)S(1)} %get-tuple-element.22.own, f32[3,64,128]{2,1,0:T(8,128)S(1)} %get-tuple-element.25.cfw, ...), custom_call_target="tpu_custom_call" | custom-call | flops 1528823808 | bytes 17825792 | tf_op jit(solution)/shard_map/inner/pallas_call | solution.py:416
  14.6 0.0 collective-permute-done.top
  14.6 0.0 collective-permute-done.1.bot
  14.7 0.1 pack_columns.1
  14.7 2.5 %collective-permute-start.2 = (bf16[19,16,384]{2,1,0:T(8,128)(2,1)S(1)}, bf16[19,16,384]{2,1,0:T(8,128)(2,1)S(1)}, u32[]{:S(2)}, u32[]{:S(2)}) collective-permute-start(bf16[19,16,384]{2,1,0:T(8,128)(2,1)S(1)} %get-tuple-element.27), channel_id=1, source_target_pairs={{0,1},{1,2},{2,3},{3,4},{4,5},{5,6},{6,7},{7,0},{8,9},{9,10},{10,1... | collective-permute-start | bytes 700424 | tf_op jit(solution)/shard_map/ppermute | solution.py:430
  17.3 0.0 collective-permute-start.3
  17.3 4.7 %rows.1 = (bf16[8,8,16,1152]{3,2,1,0:T(8,128)(2,1)S(1)}, bf16[4,6,16,1152]{3,2,1,0:T(8,128)(2,1)S(1)}) custom-call(bf16[19,16,384]{2,1,0:T(8,128)(2,1)S(1)} %collective-permute-done.top, bf16[19,16,384]{2,1,0:T(8,128)(2,1)S(1)} %collective-permute-done.1.bot, bf16[4,8,16,1152]{3,2,1,0:T(8,128)(2,1)S(1)} %get-tuple-element.30.own1, ...), custom_call_target="tpu_custom_call" | custom-call | flops 3057647616 | bytes 10485760 | tf_op jit(solution)/shard_map/rows/pallas_call | solution.py:432
  22.0 0.0 collective-permute-done.2.left
  22.1 0.7 %collective-permute-done.3.right = bf16[19,16,384]{2,1,0:T(8,128)(2,1)S(1)} collective-permute-done((bf16[19,16,384]{2,1,0:T(8,128)(2,1)S(1)}, bf16[19,16,384]{2,1,0:T(8,128)(2,1)S(1)}, u32[]{:S(2)}, u32[]{:S(2)}) %collective-permute-start.3) | collective-permute-done | bytes 233504 | tf_op jit(solution)/shard_map/ppermute | solution.py:431
  22.8 0.0 copy-start
  22.8 13.9 %finish.1 = bf16[16,8,16,128]{3,2,1,0:T(8,128)(2,1)} custom-call(bf16[19,16,384]{2,1,0:T(8,128)(2,1)S(1)} %collective-permute-done.2.left, bf16[19,16,384]{2,1,0:T(8,128)(2,1)S(1)} %collective-permute-done.3.right, bf16[19,16,384]{2,1,0:T(8,128)(2,1)S(1)} %collective-permute-done.top, bf16[19,16,384]{2,1,0:T(8,128)(2,1)S(1)} %collective-permute-done.1.bot, ...), custom_call_target="tpu_custom_call" | custom-call | flops 7644119040 | bytes 20971520 | tf_op jit(solution)/shard_map/finish/pallas_call | solution.py:439
  36.7 8.7 %all-to-all-start = ((bf16[128,16,128]{2,1,0:T(8,128)(2,1)}), bf16[128,16,128]{2,1,0:T(8,128)(2,1)S(1)}, u32[]{:S(2)}, u32[]{:S(2)}) async-start(bf16[128,16,128]{2,1,0:T(8,128)(2,1)} %bitcast.1), calls=%async_computation | async-start | bytes 1048576 | tf_op jit(solution)/shard_map/all_to_all | solution.py:455
  45.4 0.0 copy-done
  45.4 0.1 reshape_tile.3.bias
  45.5 13.6 %all-to-all-done.slots = bf16[128,16,128]{2,1,0:T(8,128)(2,1)S(1)} async-done(((bf16[128,16,128]{2,1,0:T(8,128)(2,1)}), bf16[128,16,128]{2,1,0:T(8,128)(2,1)S(1)}, u32[]{:S(2)}, u32[]{:S(2)}) %all-to-all-start) | async-done | bytes 524320 | tf_op jit(solution)/shard_map/all_to_all | solution.py:455
  59.1 0.9 %sum_patches.1 = bf16[128,128]{1,0:T(8,128)(2,1)} custom-call(bf16[128,16,128]{2,1,0:T(8,128)(2,1)S(1)} %all-to-all-done.slots, f32[1,128]{1,0:T(1,128)S(1)} %reshape_tile.3.bias), custom_call_target="tpu_custom_call" | custom-call | tf_op jit(solution)/shard_map/sum_patches/pallas_call | solution.py:456
  (1 shorter events, 0.0 us)
Async XLA Ops:
  2.8 11.9 %collective-permute-start = (bf16[19,16,384]{2,1,0:T(8,128)(2,1)S(1)}, bf16[19,16,384]{2,1,0:T(8,128)(2,1)S(1)}, u32[]{:S(2)}, u32[]{:S(2)}) collective-permute-start(bf16[19,16,384]{2,1,0:T(8,128)(2,1)S(1)} %get-tuple-element.23), channel_id=1, source_target_pairs={{0,8},{8,16},{16,24},{24,32},{32,40},{40,48},{48,56},{56,64},{64,7... | collective-permute-start | bytes 700424 | tf_op jit(solution)/shard_map/ppermute | solution.py:413
  5.0 9.7 %collective-permute-start.1 = (bf16[19,16,384]{2,1,0:T(8,128)(2,1)S(1)}, bf16[19,16,384]{2,1,0:T(8,128)(2,1)S(1)}, u32[]{:S(2)}, u32[]{:S(2)}) collective-permute-start(bf16[19,16,384]{2,1,0:T(8,128)(2,1)S(1)} %get-tuple-element.24), channel_id=1, source_target_pairs={{0,120},{8,0},{16,8},{24,16},{32,24},{40,32},{48,40},{56,48},{64,5... | collective-permute-start | bytes 700424 | tf_op jit(solution)/shard_map/ppermute | solution.py:414
  14.7 7.3 %collective-permute-start.2 = (bf16[19,16,384]{2,1,0:T(8,128)(2,1)S(1)}, bf16[19,16,384]{2,1,0:T(8,128)(2,1)S(1)}, u32[]{:S(2)}, u32[]{:S(2)}) collective-permute-start(bf16[19,16,384]{2,1,0:T(8,128)(2,1)S(1)} %get-tuple-element.27), channel_id=1, source_target_pairs={{0,1},{1,2},{2,3},{3,4},{4,5},{5,6},{6,7},{7,0},{8,9},{9,10},{10,1... | collective-permute-start | bytes 700424 | tf_op jit(solution)/shard_map/ppermute | solution.py:430
  17.3 5.5 %collective-permute-start.3 = (bf16[19,16,384]{2,1,0:T(8,128)(2,1)S(1)}, bf16[19,16,384]{2,1,0:T(8,128)(2,1)S(1)}, u32[]{:S(2)}, u32[]{:S(2)}) collective-permute-start(bf16[19,16,384]{2,1,0:T(8,128)(2,1)S(1)} %get-tuple-element.28), channel_id=1, source_target_pairs={{0,7},{1,0},{2,1},{3,2},{4,3},{5,4},{6,5},{7,6},{8,15},{9,8},{10,9... | collective-permute-start | bytes 700424 | tf_op jit(solution)/shard_map/ppermute | solution.py:431
  22.8 22.6 %copy-start = (f32[32]{0:T(128)S(1)}, f32[32]{0:T(128)}, u32[]{:S(2)}) copy-start(f32[32]{0:T(128)} %param.25) | copy-start | bytes 388
  36.7 22.4 %all-to-all-start = ((bf16[128,16,128]{2,1,0:T(8,128)(2,1)}), bf16[128,16,128]{2,1,0:T(8,128)(2,1)S(1)}, u32[]{:S(2)}, u32[]{:S(2)}) async-start(bf16[128,16,128]{2,1,0:T(8,128)(2,1)} %bitcast.1), calls=%async_computation | async-start | bytes 1048576 | tf_op jit(solution)/shard_map/all_to_all | solution.py:455

commit v4 on v3

--- a/solution.py
+++ b/solution.py
@@ -57,24 +57,22 @@
 
 
 def first_kernel(
-    feat_h, cf_h, cs_h, ch_h, g1_h, g2_h, gh_h, b1_h, b2_h, own, raw, lo, hi, cfw, csw, chw, vec,
-    feat, caches, g1, g2, gh, b1, b2, wide, plain, sems,
+    feat_h, cf_h, cs_h, ch_h, g1_h, g2_h, gh_h, b1_h, b2_h, b3_h, own, plain, lo, hi, cfw, csw, chw, vec, bias,
+    feat, caches, g1, g2, gh, b1, b2, b3, wide, sems,
 ):
+    parts = [pl.ds(4 * n, 4) for n in range(4)]
     copies = bring(
-        ((g1_h, g1), (feat_h, feat), (cf_h, caches.at[0]), (cs_h, caches.at[1]), (ch_h, caches.at[2]),
-         (g2_h, g2), (gh_h, gh), (b1_h, b1), (b2_h, b2)), sems
+        [(g1_h, g1)] + [(feat_h.at[part], feat.at[part]) for part in parts]
+        + [(cf_h, caches.at[0]), (cs_h, caches.at[1]), (ch_h, caches.at[2]),
+           (g2_h, g2), (gh_h, gh), (b1_h, b1), (b2_h, b2), (b3_h, b3)], sems
     )
     copies[0].wait()
-    copies[1].wait()
     half = 0.5 * line(g1)
-
-    def frame(f, _):
-        x = feat[pl.ds(f * 4, 4)].astype(F32).reshape(4 * R * Q, C)
-        put_rows(plain, f * 4 * R * Q, x)
-        put_rows(wide, f * 4 * R * Q, act(x, half))
-        return 0
-
-    lax.fori_loop(0, F // 4, frame, 0)
+    for n, part in enumerate(parts):
+        copies[1 + n].wait()
+        x = feat[part].astype(F32).reshape(4 * R * Q, C)
+        put_rows(plain, n * 4 * R * Q, x)
+        put_rows(wide, n * 4 * R * Q, act(x, half))
     for k in range(R * Q):
         cell = rows_at(wide, k, F, R * Q).astype(BF16)
         own[k] = cell
@@ -82,11 +80,11 @@
             lo[k] = cell
         else:
             hi[k - 16] = cell
-        raw[k] = rows_at(plain, k, F, R * Q).astype(BF16)
-    for copy in copies[2:]:
+    for copy in copies[5:]:
         copy.wait()
     for n, value in enumerate((0.5 * line(g2), 0.5 * line(gh), line(b1), line(b2))):
         vec[pl.ds(n, 1)] = value
+    bias[pl.ds(0, 1)] = jnp.concatenate([line(b3)] * 4, axis=-1)
     for n, out in enumerate((cfw, csw, chw)):
         for h in range(R):
             for f in range(2):
@@ -146,7 +144,7 @@
     return ha > 0, ha < lax.axis_size("ha") - 1, wa > 0, wa < lax.axis_size("wa") - 1
 
 
-def inner_kernel(own, cfw, csw, vec, w1, w2, wh, s1, s2, w1v, w2v, wy, acc, sems):
+def inner_kernel(own, plain, cfw, csw, vec, w1, w2, wh, s1, s2, w1v, w2v, wy, raw, acc, sems):
     def group(src, dst, a, sem):
         return [
             pltpu.make_async_copy(src.at[t, a, b], dst.at[a, b * 3 + t], sem) for b in range(3) for t in range(3)
@@ -186,6 +184,8 @@
             acc[...] += taps(taken, w1v, a)
     for h in range(2):
         hidden(s2, (h, pl.ds(0, 6)), acc[pl.ds(h * 6 * F, 6 * F)], vec, cached_row(csw, (1 + h) * 16, 1, 6))
+    for k in range(R * Q):
+        raw[k] = rows_at(plain, k, F, R * Q).astype(BF16)
     for copy in later:
         copy.wait()
 
@@ -280,12 +280,21 @@
                 olds.append(two if n == 0 else two[::-1])
             put(s2, (h, pl.ds(8 * n, 2)), now, olds[0], olds[1], None if inside is True else inside)
 
+    def window(a, rows):
+        return jnp.concatenate([s2[a : a + rows, b : b + Q].reshape(rows * Q * F, 3 * C) for b in range(3)], axis=-1)
+
     for a in range(3):
-        taken = jnp.concatenate([s2[a : a + R, b : b + Q].reshape(R * Q * F, 3 * C) for b in range(3)], axis=-1)
+        part = jnp.dot(window(a, R), w2v[a, :, :, 0:256].reshape(9 * C, 256), preferred_element_type=F32)
         if a == 0:
-            acc2[...] = taps(taken, w2v, a)
-        else:
-            acc2[...] += taps(taken, w2v, a)
+            acc2[:, 0:256] = part
+        else:
+            acc2[:, 0:256] += part
+    side = [w2v[a, :, :, 256:384].reshape(9 * C, 128) for a in range(3)]
+    pair = jnp.dot(window(0, R + 1), jnp.concatenate(side[:2], axis=-1), preferred_element_type=F32)
+    acc2[:, 256:384] = (
+        pair[: R * Q * F, :128] + pair[Q * F :, 128:]
+        + jnp.dot(window(2, R), side[2], preferred_element_type=F32)
+    )
 
     def last(h, _):
         wide = acc2[pl.ds(h * Q * F, Q * F)] + vec[pl.ds(3, 1), :]
@@ -324,16 +333,14 @@
             out[f, g] = patches
 
 
-def last_kernel(slots, bias, out, held, sums, sem):
+def last_kernel(slots, bias, out, sums):
     ha_count = 16
     g = lax.axis_index("wa")
-    copies = []
-    for k in range(4):
-        i = jnp.clip(2 * g - 1 + k, 0, ha_count - 1)
-        copies.append(pltpu.make_async_copy(slots.at[pl.ds(i * 8, 8)], held.at[k], sem.at[k]))
-        copies[-1].start()
-    for copy in copies:
-        copy.wait()
+    first = [jnp.clip(2 * g - 1 + k, 0, ha_count - 1) * 8 for k in range(4)]
+
+    def held(k, j, low, count):
+        return slots[first[k] + j, pl.ds(low, count)].astype(F32)
+
     lane = lax.broadcasted_iota(jnp.int32, (4, 128), 1)
     row = lax.broadcasted_iota(jnp.int32, (4, 128), 0)
     for k in range(2):
@@ -343,18 +350,18 @@
             upright = ((lane < 64) if pr == 0 else (lane >= 64)) & there
 
             def edge(j, pr=pr, k=k, other=other, upright=upright):
-                mine = jnp.broadcast_to(held[k + 1, j, 12 + pr : 13 + pr].astype(F32), (4, 128))
-                theirs = jnp.broadcast_to(held[other, j, 14:15].astype(F32), (4, 128))
+                mine = jnp.broadcast_to(held(k + 1, j, 12 + pr, 1), (4, 128))
+                theirs = jnp.broadcast_to(held(other, j, 14, 1), (4, 128))
                 return mine + jnp.where(upright, theirs, 0.0)
 
             for j in range(8):
-                total = held[k + 1, j, pr * 4 : pr * 4 + 4].astype(F32)
-                total = total + jnp.where(upright, held[other, j, 8:12].astype(F32), 0.0)
+                total = held(k + 1, j, pr * 4, 4)
+                total = total + jnp.where(upright, held(other, j, 8, 4), 0.0)
                 if j > 0:
                     total = total + jnp.where((row == 0) & (lane % 64 < 32), edge(j - 1), 0.0)
                 if j < 7:
                     total = total + jnp.where((row == 3) & (lane % 64 >= 32), edge(j + 1), 0.0)
-                sums[pl.ds((2 * k + pr) * 32 + j * 4, 4)] = total + bias[...]
+                sums[pl.ds((2 * k + pr) * 32 + j * 4, 4)] = total + bias[pl.ds(0, 1), :]
     out[...] = sums[...].astype(BF16)
 
 
@@ -392,34 +399,35 @@
     features, cache_first, cache_second, cache_head, gain_first, gain_second, gain_head,
     conv_first, conv_second, conv_head, bias_first, bias_second, bias_head,
 ):
-    own, raw, lo, hi, cfw, csw, chw, vec = kernel(
+    own, plain, lo, hi, cfw, csw, chw, vec, bias = kernel(
         first_kernel,
-        [near(32, F, C), near(32, F, C), near(MSG, F, C), near(MSG, F, C)]
-        + [near(3, 64, 128, dtype=F32)] * 3 + [near(8, C, dtype=F32)],
-        [ANY] * 9,
+        [near(32, F, C), near(3, F * R * Q, 128, dtype=F32), near(MSG, F, C), near(MSG, F, C)]
+        + [near(3, 64, 128, dtype=F32)] * 3 + [near(8, C, dtype=F32), near(8, 128, dtype=F32)],
+        [ANY] * 10,
         [
             pltpu.VMEM((F, R, Q, C), BF16),
             pltpu.VMEM((3, 2, R, Q, C), BF16),
         ]
         + [pltpu.VMEM((C,), F32)] * 5
         + [
+            pltpu.VMEM((32,), F32),
             pltpu.VMEM((3, F * R * Q, 128), F32),
-            pltpu.VMEM((3, F * R * Q, 128), F32),
-            pltpu.SemaphoreType.DMA((9,)),
+            pltpu.SemaphoreType.DMA((13,)),
         ],
         12, "act_first",
     )(*[far(v) for v in (features, cache_first, cache_second, cache_head, gain_first, gain_second, gain_head,
-                         bias_first, bias_second)])
+                         bias_first, bias_second, bias_head)])
     top = lax.ppermute(hi, "ha", around("ha", 1))
     bot = lax.ppermute(lo, "ha", around("ha", -1))
     cell_flops = 2 * F * 27 * C * C
-    own1, inner2, w1v, w2v, wy = kernel(
+    own1, inner2, w1v, w2v, wy, raw = kernel(
         inner_kernel,
-        [near(R, Q, F, 3 * C), near(2, 6, F, 3 * C), near(3, 9, C, C), near(3, 9, C, C), near(3 * 128, 3 * C)],
-        [VM] * 4 + [ANY] * 3,
+        [near(R, Q, F, 3 * C), near(2, 6, F, 3 * C), near(3, 9, C, C), near(3, 9, C, C), near(3 * 128, 3 * C),
+         near(32, F, C)],
+        [VM] * 5 + [ANY] * 3,
         [pltpu.VMEM((12 * F, C), F32), pltpu.SemaphoreType.DMA((7,))],
         8, "inner", 12 * cell_flops, 17 * 2**20,
-    )(own, cfw, csw, vec, far(conv_first), far(conv_second), far(jnp.swapaxes(conv_head, 3, 4)))
+    )(own, plain, cfw, csw, vec, far(conv_first), far(conv_second), far(jnp.swapaxes(conv_head, 3, 4)))
     to_left, to_right = kernel(
         pack_kernel,
         [near(MSG, F, C)] * 2,
@@ -456,16 +464,12 @@
     return pl.pallas_call(
         last_kernel,
         out_shape=shape(128, 128),
-        in_specs=[ANY, VM],
+        in_specs=[VM] * 2,
         out_specs=VM,
-        scratch_shapes=[
-            pltpu.VMEM((4, 8, 16, 128), BF16),
-            pltpu.VMEM((128, 128), F32),
-            pltpu.SemaphoreType.DMA((4,)),
-        ],
-        compiler_params=pltpu.CompilerParams(vmem_limit_bytes=8 * 2**20),
+        scratch_shapes=[pltpu.VMEM((128, 128), F32)],
+        compiler_params=pltpu.CompilerParams(vmem_limit_bytes=4 * 2**20),
         name="sum_patches",
-    )(arrived, jnp.tile(bias_head, 4).reshape(1, 128))
+    )(arrived, bias)
 
 
 def solution(mesh):

time: 60.3 us -> 58.7 us (0.973)
  blocking collectives: 0 us -> 22.2 us
  waiting for transfers between devices: 14.3 us -> 0.64 us
  starting transfers between devices: 17.2 us -> 8.45 us
  Pallas kernels: 28.3 us -> 27.2 us
    all_to_all x0 -> x1, blocking collectives: none -> 22.2 us  [local(): lax.all_to_all(slots.reshape(F * 8, 16, 128), ('ha', 'wa'), 0, 0, tiled=T...]
    all_to_all x1 -> x0, waiting for transfers between devices: 13.6 us -> none  [local(): lax.all_to_all(slots.reshape(F * 8, 16, 128), ('ha', 'wa'), 0, 0, tiled=T...]
    all_to_all x1 -> x0, starting transfers between devices: 8.7 us -> none  [local(): lax.all_to_all(slots.reshape(F * 8, 16, 128), ('ha', 'wa'), 0, 0, tiled=T...]
    pallas_call x2, Pallas kernels: 3.63 us -> 2.78 us  [the longest x1 2.08 us: local(): kernel(first_kernel, [near(32, F, C), near(3, F * R * Q, 128, dtype=F32),...]
  transfers between devices with their start and end apart: 5 -> 4, of which waited for: 2 -> 1; matrix products, arithmetic and copies ran while one was open for 0% -> 0% of each run, Pallas kernels for 18% -> 18%
where the time goes in v4:
time: 58.7 us; the launch traced here: 58.6 us
  Pallas kernels  27.2 us (46%)
  blocking collectives  22.2 us (38%)
  starting transfers between devices  8.45 us (14%)
  waiting for transfers between devices  0.64 us (1%)
    all_to_all x1, blocking collectives, local(): lax.all_to_all(slots.reshape(F * 8, 16, 128), ('ha', 'wa'), 0, 0, tiled=T...  22.2 us
    pallas_call x1, Pallas kernels, local(): kernel(finish_kernel, [shape(F, 8, 16, 128)], [VM] * 14, [pltpu.VMEM((8,...  13.6 us
    pallas_call x1, Pallas kernels, local(): kernel(inner_kernel, [near(R, Q, F, 3 * C), near(2, 6, F, 3 * C), near(3,...  5.97 us
    pallas_call x1, Pallas kernels, local(): kernel(rows_kernel, [near(8, Q, F, 3 * C), near(4, 6, F, 3 * C)], [VM] *...  4.83 us
    ppermute x1, starting transfers between devices, local(): bot = lax.ppermute(lo, 'ha', around('ha', -1))  3.71 us
    ppermute x1, starting transfers between devices, local(): left = lax.ppermute(to_right, 'wa', around('wa', 1))  2.54 us
    ppermute x1, starting transfers between devices, local(): top = lax.ppermute(hi, 'ha', around('ha', 1))  2.19 us
    pallas_call x1, Pallas kernels, local(): kernel(first_kernel, [near(32, F, C), near(3, F * R * Q, 128, dtype=F32),...  2.08 us
  transfers between devices with their start and end apart: 4, of which 1 were waited for; matrix products, arithmetic and copies ran while one was open for 0% of the time, Pallas kernels for 18%

profile of v4, /device:TPU:1, one launch (start us, length us, event | category | flops | bytes accessed | tf_op | source)
XLA Modules:
  0.0 58.6 jit_solution(10763787400968741708)
XLA Ops:
  0.0 2.1 %act_first.1 = (bf16[32,16,384]{2,1,0:T(8,128)(2,1)S(1)}, f32[3,512,128]{2,1,0:T(8,128)S(1)}, bf16[19,16,384]{2,1,0:T(8,128)(2,1)S(1)}, bf16[19,16,384]{2,1,0:T(...) custom-call(bf16[16,4,8,384]{3,2,1,0:T(8,128)(2,1)} %feat_h.1, ...), custom_call_target="tpu_custom_call" | custom-call | tf_op jit(solution)/shard_map/act_first/pallas_call | solution.py:402
  2.1 2.2 %collective-permute-start = (bf16[19,16,384]{2,1,0:T(8,128)(2,1)S(1)}, bf16[19,16,384]{2,1,0:T(8,128)(2,1)S(1)}, u32[]{:S(2)}, u32[]{:S(2)}) collective-permute-start(bf16[19,16,384]{2,1,0:T(8,128)(2,1)S(1)} %get-tuple-element.25), channel_id=1, source_target_pairs={{0,8},{8,16},{16,24},{24,32},{32,40},{40,48},{48,56},{56,64},{64,7... | collective-permute-start | bytes 700424 | tf_op jit(solution)/shard_map/ppermute | solution.py:420
  4.3 3.7 %collective-permute-start.1 = (bf16[19,16,384]{2,1,0:T(8,128)(2,1)S(1)}, bf16[19,16,384]{2,1,0:T(8,128)(2,1)S(1)}, u32[]{:S(2)}, u32[]{:S(2)}) collective-permute-start(bf16[19,16,384]{2,1,0:T(8,128)(2,1)S(1)} %get-tuple-element.26), channel_id=1, source_target_pairs={{0,120},{8,0},{16,8},{24,16},{32,24},{40,32},{48,40},{56,48},{64,5... | collective-permute-start | bytes 700424 | tf_op jit(solution)/shard_map/ppermute | solution.py:421
  8.0 6.0 %inner.1 = (bf16[4,8,16,1152]{3,2,1,0:T(8,128)(2,1)S(1)}, bf16[2,6,16,1152]{3,2,1,0:T(8,128)(2,1)S(1)}, bf16[3,9,384,384]{3,2,1,0:T(8,128)(2,1)S(1)}, bf16[3,9,3...) custom-call(bf16[32,16,384]{2,1,0:T(8,128)(2,1)S(1)} %get-tuple-element.24.own, ...), custom_call_target="tpu_custom_call" | custom-call | flops 1528823808 | bytes 17825792 | tf_op jit(solution)/shard_map/inner/pallas_call | solution.py:423
  14.0 0.0 collective-permute-done.top
  14.0 0.0 collective-permute-done.1.bot
  14.0 0.1 pack_columns.1
  14.1 2.5 %collective-permute-start.2 = (bf16[19,16,384]{2,1,0:T(8,128)(2,1)S(1)}, bf16[19,16,384]{2,1,0:T(8,128)(2,1)S(1)}, u32[]{:S(2)}, u32[]{:S(2)}) collective-permute-start(bf16[19,16,384]{2,1,0:T(8,128)(2,1)S(1)} %get-tuple-element.29), channel_id=1, source_target_pairs={{0,1},{1,2},{2,3},{3,4},{4,5},{5,6},{6,7},{7,0},{8,9},{9,10},{10,1... | collective-permute-start | bytes 700424 | tf_op jit(solution)/shard_map/ppermute | solution.py:438
  16.6 0.0 collective-permute-start.3
  16.6 4.8 %rows.1 = (bf16[8,8,16,1152]{3,2,1,0:T(8,128)(2,1)S(1)}, bf16[4,6,16,1152]{3,2,1,0:T(8,128)(2,1)S(1)}) custom-call(bf16[19,16,384]{2,1,0:T(8,128)(2,1)S(1)} %collective-permute-done.top, bf16[19,16,384]{2,1,0:T(8,128)(2,1)S(1)} %collective-permute-done.1.bot, bf16[4,8,16,1152]{3,2,1,0:T(8,128)(2,1)S(1)} %get-tuple-element.33.own1, ...), custom_call_target="tpu_custom_call" | custom-call | flops 3057647616 | bytes 10485760 | tf_op jit(solution)/shard_map/rows/pallas_call | solution.py:440
  21.5 0.0 collective-permute-done.2.left
  21.5 0.6 %collective-permute-done.3.right = bf16[19,16,384]{2,1,0:T(8,128)(2,1)S(1)} collective-permute-done((bf16[19,16,384]{2,1,0:T(8,128)(2,1)S(1)}, bf16[19,16,384]{2,1,0:T(8,128)(2,1)S(1)}, u32[]{:S(2)}, u32[]{:S(2)}) %collective-permute-start.3) | collective-permute-done | bytes 233504 | tf_op jit(solution)/shard_map/ppermute | solution.py:439
  22.1 13.6 %finish.1 = bf16[16,8,16,128]{3,2,1,0:T(8,128)(2,1)S(1)} custom-call(bf16[19,16,384]{2,1,0:T(8,128)(2,1)S(1)} %collective-permute-done.2.left, bf16[19,16,384]{2,1,0:T(8,128)(2,1)S(1)} %collective-permute-done.3.right, bf16[19,16,384]{2,1,0:T(8,128)(2,1)S(1)} %collective-permute-done.top, bf16[19,16,384]{2,1,0:T(8,128)(2,1)S(1)} %collective-permute-done.1.bot, ...), custom_call_target="tpu_custom_call" | custom-call | flops 7644119040 | bytes 20971520 | tf_op jit(solution)/shard_map/finish/pallas_call | solution.py:447
  35.7 22.2 %all_to_all.5.slots = bf16[128,16,128]{2,1,0:T(8,128)(2,1)S(1)} all-to-all(bf16[128,16,128]{2,1,0:T(8,128)(2,1)S(1)} %bitcast.2), channel_id=1, replica_groups=mesh['ha'=16,'wa'=8] {'ha','wa'}, dimensions={0} | all-to-all | bytes 1048576 | tf_op jit(solution)/shard_map/all_to_all | solution.py:463
  57.9 0.7 %sum_patches.1 = bf16[128,128]{1,0:T(8,128)(2,1)} custom-call(bf16[128,16,128]{2,1,0:T(8,128)(2,1)S(1)} %all_to_all.5.slots, f32[8,128]{1,0:T(8,128)S(1)} %get-tuple-element.42.bias), custom_call_target="tpu_custom_call" | custom-call | tf_op jit(solution)/shard_map/sum_patches/pallas_call | solution.py:464
Async XLA Ops:
  2.1 11.9 %collective-permute-start = (bf16[19,16,384]{2,1,0:T(8,128)(2,1)S(1)}, bf16[19,16,384]{2,1,0:T(8,128)(2,1)S(1)}, u32[]{:S(2)}, u32[]{:S(2)}) collective-permute-start(bf16[19,16,384]{2,1,0:T(8,128)(2,1)S(1)} %get-tuple-element.25), channel_id=1, source_target_pairs={{0,8},{8,16},{16,24},{24,32},{32,40},{40,48},{48,56},{56,64},{64,7... | collective-permute-start | bytes 700424 | tf_op jit(solution)/shard_map/ppermute | solution.py:420
  4.3 9.7 %collective-permute-start.1 = (bf16[19,16,384]{2,1,0:T(8,128)(2,1)S(1)}, bf16[19,16,384]{2,1,0:T(8,128)(2,1)S(1)}, u32[]{:S(2)}, u32[]{:S(2)}) collective-permute-start(bf16[19,16,384]{2,1,0:T(8,128)(2,1)S(1)} %get-tuple-element.26), channel_id=1, source_target_pairs={{0,120},{8,0},{16,8},{24,16},{32,24},{40,32},{48,40},{56,48},{64,5... | collective-permute-start | bytes 700424 | tf_op jit(solution)/shard_map/ppermute | solution.py:421
  14.1 7.4 %collective-permute-start.2 = (bf16[19,16,384]{2,1,0:T(8,128)(2,1)S(1)}, bf16[19,16,384]{2,1,0:T(8,128)(2,1)S(1)}, u32[]{:S(2)}, u32[]{:S(2)}) collective-permute-start(bf16[19,16,384]{2,1,0:T(8,128)(2,1)S(1)} %get-tuple-element.29), channel_id=1, source_target_pairs={{0,1},{1,2},{2,3},{3,4},{4,5},{5,6},{6,7},{7,0},{8,9},{9,10},{10,1... | collective-permute-start | bytes 700424 | tf_op jit(solution)/shard_map/ppermute | solution.py:438
  16.6 5.5 %collective-permute-start.3 = (bf16[19,16,384]{2,1,0:T(8,128)(2,1)S(1)}, bf16[19,16,384]{2,1,0:T(8,128)(2,1)S(1)}, u32[]{:S(2)}, u32[]{:S(2)}) collective-permute-start(bf16[19,16,384]{2,1,0:T(8,128)(2,1)S(1)} %get-tuple-element.30), channel_id=1, source_target_pairs={{0,7},{1,0},{2,1},{3,2},{4,3},{5,4},{6,5},{7,6},{8,15},{9,8},{10,9... | collective-permute-start | bytes 700424 | tf_op jit(solution)/shard_map/ppermute | solution.py:439

commit v5 on v4

--- a/solution.py
+++ b/solution.py
@@ -96,7 +96,8 @@
     hi[18] = rows_at(csw, 48, 16, 1).astype(BF16)
 
 
-def pack_kernel(own, top, bot, cfw, csw, left, right, wide_f, wide_s):
+def pack_kernel(own, top, bot, cfw, csw, after, left, right, wide_f, wide_s):
+    del after
     for n in range(2):
         put_rows(wide_f, n * 16, top[16 + n].astype(F32))
         put_rows(wide_f, (6 + n) * 16, bot[16 + n].astype(F32))
@@ -130,8 +131,8 @@
     return [[block[8 * f + w : 8 * f + w + 1] for w in range(count)] for f in range(2)]
 
 
-def taps(src, weight, a):
-    return jnp.dot(src, weight[a].reshape(9 * C, C), preferred_element_type=F32)
+def three(weight, a):
+    return jnp.concatenate([weight[a, 3 * b : 3 * b + 3].reshape(3 * C, C) for b in range(3)], axis=-1)
 
 
 def hidden(dst, where, total, vec, cached, valid=None):
@@ -144,7 +145,7 @@
     return ha > 0, ha < lax.axis_size("ha") - 1, wa > 0, wa < lax.axis_size("wa") - 1
 
 
-def inner_kernel(own, plain, cfw, csw, vec, w1, w2, wh, s1, s2, w1v, w2v, wy, raw, acc, sems):
+def inner_kernel(own, plain, cfw, csw, vec, w1, w2, wh, acc, s2, w1v, w2v, wy, raw, s1, sems):
     def group(src, dst, a, sem):
         return [
             pltpu.make_async_copy(src.at[t, a, b], dst.at[a, b * 3 + t], sem) for b in range(3) for t in range(3)
@@ -165,10 +166,11 @@
             copy.start()
     for a in range(3):
         wy[pl.ds(a * 128 + 96, 32)] = jnp.zeros((32, 3 * C), BF16)
+    acc[...] = jnp.zeros_like(acc)
 
     def cells(h, _):
         c0, c1 = cached_row(cfw, h * 16, 0, Q)
-        put(s1, (h, pl.ds(0, Q)), own[pl.ds(h * Q, Q)].reshape(Q * F, C).astype(F32), c0, c1)
+        put(s1, (pl.ds(h * Q, Q),), own[pl.ds(h * Q, Q)].reshape(Q * F, C).astype(F32), c0, c1)
         return 0
 
     lax.fori_loop(0, R, cells, 0)
@@ -177,66 +179,59 @@
             copy.wait()
         for copy in (first[2], later, ())[a]:
             copy.start()
-        taken = jnp.concatenate([s1[a : a + 2, b : b + 6].reshape(12 * F, 3 * C) for b in range(3)], axis=-1)
-        if a == 0:
-            acc[...] = taps(taken, w1v, a)
-        else:
-            acc[...] += taps(taken, w1v, a)
+        part = jnp.dot(s1[...].reshape(R * Q * F, 3 * C), three(w1v, a), preferred_element_type=F32)
+        for b in range(3):
+            acc[2 - a : 2 - a + R, 2 - b : 2 - b + Q] += part[:, b * C : (b + 1) * C].reshape(R, Q, F, C)
     for h in range(2):
-        hidden(s2, (h, pl.ds(0, 6)), acc[pl.ds(h * 6 * F, 6 * F)], vec, cached_row(csw, (1 + h) * 16, 1, 6))
+        hidden(s2, (h, pl.ds(0, 6)), acc[2 + h, 2:8].reshape(6 * F, C), vec, cached_row(csw, (1 + h) * 16, 1, 6))
     for k in range(R * Q):
         raw[k] = rows_at(plain, k, F, R * Q).astype(BF16)
     for copy in later:
         copy.wait()
 
 
-def rows_kernel(top, bot, own1, csw, vec, w1v, s1, s2, acc):
+def rows_kernel(top, bot, acc, csw, vec, w1v, sides, s2, s1, add):
     up, down, _, _ = place()
-    for msg, h0, valid in ((top, 0, up), (bot, 6, down)):
+    for msg, h0, valid in ((top, 0, up), (bot, 2, down)):
         for h in range(2):
             c0, c1 = cached_msg(msg[16 + h])
             put(s1, (h0 + h, pl.ds(0, Q)), msg[pl.ds(h * Q, Q)].reshape(Q * F, C).astype(F32), c0, c1, valid)
-    s1[2:6] = own1[...]
-    for a in range(3):
-        taken = jnp.concatenate(
-            [
-                jnp.concatenate(
-                    [s1[4 * n + a : 4 * n + a + 2, b : b + 6].reshape(12 * F, 3 * C) for n in range(2)], axis=0
-                )
-                for b in range(3)
-            ],
-            axis=-1,
-        )
-        if a == 0:
-            acc[...] = taps(taken, w1v, a)
-        else:
-            acc[...] += taps(taken, w1v, a)
+    add[0:2] = acc[0:2]
+    add[2:4] = acc[4:6]
+    for a, (low, targets) in enumerate(((0, (0, 1)), (1, (0, 3)), (2, (2, 3)))):
+        part = jnp.dot(s1[low : low + 2].reshape(2 * Q * F, 3 * C), three(w1v, a), preferred_element_type=F32)
+        for n, row in enumerate(targets):
+            for b in range(3):
+                block = part[n * Q * F : (n + 1) * Q * F, b * C : (b + 1) * C]
+                add[row, 2 - b : 2 - b + Q] += block.reshape(Q, F, C)
     for n, cached, valid in (
         (0, [c[1:7] for c in cached_msg(top[18])], up),
         (1, cached_row(csw, 0, 1, 6), None),
         (2, cached_row(csw, 48, 1, 6), None),
         (3, [c[1:7] for c in cached_msg(bot[18])], down),
     ):
-        hidden(s2, (n, pl.ds(0, 6)), acc[pl.ds(n * 6 * F, 6 * F)], vec, cached, valid)
+        hidden(s2, (n, pl.ds(0, 6)), add[n, 2:8].reshape(6 * F, C), vec, cached, valid)
+    for n, col in enumerate((0, 8)):
+        sides[0:2, 2 * n : 2 * n + 2] = add[0:2, col : col + 2]
+        sides[2:4, 2 * n : 2 * n + 2] = acc[2:4, col : col + 2]
+        sides[4:6, 2 * n : 2 * n + 2] = add[2:4, col : col + 2]
 
 
 def finish_kernel(
-    left, right, top, bot, s1, inner2, rows2, raw, csw, chw, vec, w1v, w2v, wy, out,
-    sides, s2, s3, acc1, acc2, acch, side_f, side_s,
+    left, right, top, bot, sides, inner2, rows2, raw, csw, chw, vec, w1v, w2v, wy, out,
+    s1, acc1, s2, s3, acc2, acch, side_f, side_s,
 ):
     up, down, west, east = place()
     for n, msg in enumerate((left, right)):
         for c in range(2):
             side_f[n, pl.ds(c * 16, 16)] = msg[16 + c].astype(F32)
         side_s[n] = msg[18].astype(F32)
-    sides[:, 0, 2:4] = s1[:, 0:2]
-    sides[:, 1, 0:2] = s1[:, 6:8]
-    for n, (msg, side, w0) in enumerate(((left, west, 0), (right, east, 2))):
-        def cells(h, _, n=n, msg=msg, side=side, w0=w0):
+    for n, (msg, side) in enumerate(((left, west), (right, east))):
+        def cells(h, _, n=n, msg=msg, side=side):
             for k in range(2):
                 hh = h * 2 + k
                 put(
-                    sides, (hh, n, pl.ds(w0, 2)), msg[pl.ds(hh * 2, 2)].reshape(2 * F, C).astype(F32),
+                    s1, (hh, pl.ds(2 * n, 2)), msg[pl.ds(hh * 2, 2)].reshape(2 * F, C).astype(F32),
                     [side_f[n, pl.ds(c * 16 + hh * 2, 1), :] for c in range(2)],
                     [side_f[n, pl.ds(c * 16 + hh * 2 + 1, 1), :] for c in range(2)],
                     side & (up | (hh >= 2)) & (down | (hh < 6)),
@@ -245,14 +240,13 @@
 
         lax.fori_loop(0, 4, cells, 0)
 
-    for a in range(3):
-        taken = jnp.concatenate(
-            [sides[a : a + 6, :, b : b + 2].reshape(24 * F, 3 * C) for b in range(3)], axis=-1
-        )
-        if a == 0:
-            acc1[...] = taps(taken, w1v, a)
-        else:
-            acc1[...] += taps(taken, w1v, a)
+    acc1[...] = sides[...]
+    for b, targets in enumerate(((0, 1), (0, 3), (2, 3))):
+        taken = jnp.concatenate([s1[a : a + 6, b : b + 2].reshape(12 * F, 3 * C) for a in range(3)], axis=-1)
+        weight = jnp.concatenate([w1v[a, 3 * b : 3 * b + 3].reshape(3 * C, C) for a in range(3)], axis=0)
+        part = jnp.dot(taken, weight, preferred_element_type=F32).reshape(6, 2, F, C)
+        for n, col in enumerate(targets):
+            acc1[:, col] += part[:, n]
     s2[2:4, 2:8] = inner2[...]
     s2[0:2, 2:8] = rows2[0:2]
     s2[4:6, 2:8] = rows2[2:4]
@@ -267,7 +261,7 @@
         for n, side in enumerate((west, east)):
             first = [side_s[n, pl.ds(h * 2 + f, 1), :] for f in range(2)]
             keep = jnp.where(side, 1.0, 0.0).astype(F32)
-            total = acc1[pl.ds((h * 2 + n) * 2 * F, 2 * F)]
+            total = acc1[h, 2 * n : 2 * n + 2].reshape(2 * F, C)
             wide = (total + vec[pl.ds(2, 1), :]).astype(BF16).astype(F32)
             now = act(wide, vec[pl.ds(0, 1), :])
             own_w = 0 if n == 0 else Q - 1
@@ -420,46 +414,46 @@
     top = lax.ppermute(hi, "ha", around("ha", 1))
     bot = lax.ppermute(lo, "ha", around("ha", -1))
     cell_flops = 2 * F * 27 * C * C
-    own1, inner2, w1v, w2v, wy, raw = kernel(
+    sums1, inner2, w1v, w2v, wy, raw = kernel(
         inner_kernel,
-        [near(R, Q, F, 3 * C), near(2, 6, F, 3 * C), near(3, 9, C, C), near(3, 9, C, C), near(3 * 128, 3 * C),
+        [near(R + 2, Q + 2, F, C, dtype=F32), near(2, 6, F, 3 * C), near(3, 9, C, C), near(3, 9, C, C), near(3 * 128, 3 * C),
          near(32, F, C)],
         [VM] * 5 + [ANY] * 3,
-        [pltpu.VMEM((12 * F, C), F32), pltpu.SemaphoreType.DMA((7,))],
-        8, "inner", 12 * cell_flops, 17 * 2**20,
+        [pltpu.VMEM((R * Q, F, 3 * C), BF16), pltpu.SemaphoreType.DMA((7,))],
+        12, "inner", 32 * cell_flops, 17 * 2**20,
     )(own, plain, cfw, csw, vec, far(conv_first), far(conv_second), far(jnp.swapaxes(conv_head, 3, 4)))
     to_left, to_right = kernel(
         pack_kernel,
         [near(MSG, F, C)] * 2,
-        [VM] * 5,
+        [VM] * 6,
         [pltpu.VMEM((3, 128, 128), F32)] * 2,
         4, "pack_columns",
-    )(own, top, bot, cfw, csw)
+    )(own, top, bot, cfw, csw, inner2)
     left = lax.ppermute(to_right, "wa", around("wa", 1))
     right = lax.ppermute(to_left, "wa", around("wa", -1))
-    s1, rows2 = kernel(
+    sides, rows2 = kernel(
         rows_kernel,
-        [near(8, Q, F, 3 * C), near(4, 6, F, 3 * C)],
+        [near(R + 2, 4, F, C, dtype=F32), near(4, 6, F, 3 * C)],
         [VM] * 6,
-        [pltpu.VMEM((24 * F, C), F32)],
-        8, "rows", 24 * cell_flops, 10 * 2**20,
-    )(top, bot, own1, csw, vec, w1v)
+        [pltpu.VMEM((4, Q, F, 3 * C), BF16), pltpu.VMEM((4, Q + 2, F, C), F32)],
+        10, "rows", 16 * cell_flops, 10 * 2**20,
+    )(top, bot, sums1, csw, vec, w1v)
     (slots,) = kernel(
         finish_kernel,
         [shape(F, 8, 16, 128)],
         [VM] * 14,
         [
-            pltpu.VMEM((8, 2, 4, F, 3 * C), BF16),
+            pltpu.VMEM((8, 4, F, 3 * C), BF16),
+            pltpu.VMEM((R + 2, 4, F, C), F32),
             pltpu.VMEM((R + 2, Q + 2, F, 3 * C), BF16),
             pltpu.VMEM((R * Q, F, 3 * C), BF16),
-            pltpu.VMEM((24 * F, C), F32),
             pltpu.VMEM((R * Q * F, C), F32),
             pltpu.VMEM((16 * F, 128), F32),
             pltpu.VMEM((2, 32, C), F32),
             pltpu.VMEM((2, 16, C), F32),
         ],
-        20, "finish", 60 * cell_flops, 20 * 2**20,
-    )(left, right, top, bot, s1, inner2, rows2, raw, csw, chw, vec, w1v, w2v, wy)
+        20, "finish", 48 * cell_flops, 20 * 2**20,
+    )(left, right, top, bot, sides, inner2, rows2, raw, csw, chw, vec, w1v, w2v, wy)
     arrived = lax.all_to_all(slots.reshape(F * 8, 16, 128), ("ha", "wa"), 0, 0, tiled=True)
     return pl.pallas_call(
         last_kernel,

time: 58.7 us -> 56.7 us (0.966)
  blocking collectives: 22.2 us -> 19.8 us
  waiting for transfers between devices: 0.64 us -> 2.36 us
  Pallas kernels: 27.2 us -> 25.8 us
    pallas_call x1, Pallas kernels: 13.6 us -> 11.1 us  [local(): kernel(finish_kernel, [shape(F, 8, 16, 128)], [VM] * 14, [pltpu.VMEM((8,...]
    all_to_all x1, blocking collectives: 22.2 us -> 19.8 us  [local(): lax.all_to_all(slots.reshape(F * 8, 16, 128), ('ha', 'wa'), 0, 0, tiled=T...]
    ppermute x1, waiting for transfers between devices: 0.63 us -> 2.35 us  [local(): right = lax.ppermute(to_left, 'wa', around('wa', -1))]
    pallas_call x3, Pallas kernels: 10.9 us -> 11.9 us  [the longest x1 8.74 us: local(): kernel(inner_kernel, [near(R + 2, Q + 2, F, C, dtype=F32), near(2, 6, F,...]
  transfers between devices with their start and end apart: 4 -> 4, of which waited for: 1 -> 1; matrix products, arithmetic and copies ran while one was open for 0% -> 0% of each run, Pallas kernels for 18% -> 21%
where the time goes in v5:
time: 56.7 us; the launch traced here: 56.5 us
  Pallas kernels  25.8 us (46%)
  blocking collectives  19.8 us (35%)
  starting transfers between devices  8.45 us (15%)
  waiting for transfers between devices  2.36 us (4%)
    all_to_all x1, blocking collectives, local(): lax.all_to_all(slots.reshape(F * 8, 16, 128), ('ha', 'wa'), 0, 0, tiled=T...  19.8 us
    pallas_call x1, Pallas kernels, local(): kernel(finish_kernel, [shape(F, 8, 16, 128)], [VM] * 14, [pltpu.VMEM((8,...  11.1 us
    pallas_call x1, Pallas kernels, local(): kernel(inner_kernel, [near(R + 2, Q + 2, F, C, dtype=F32), near(2, 6, F,...  8.74 us
    ppermute x1, starting transfers between devices, local(): bot = lax.ppermute(lo, 'ha', around('ha', -1))  3.71 us
    pallas_call x1, Pallas kernels, local(): kernel(rows_kernel, [near(R + 2, 4, F, C, dtype=F32), near(4, 6, F, 3 * C...  3.12 us
    ppermute x1, starting transfers between devices, local(): left = lax.ppermute(to_right, 'wa', around('wa', 1))  2.54 us
    ppermute x1, waiting for transfers between devices, local(): right = lax.ppermute(to_left, 'wa', around('wa', -1))  2.35 us
    ppermute x1, starting transfers between devices, local(): top = lax.ppermute(hi, 'ha', around('ha', 1))  2.19 us
  transfers between devices with their start and end apart: 4, of which 1 were waited for; matrix products, arithmetic and copies ran while one was open for 0% of the time, Pallas kernels for 21%

profile of v5, /device:TPU:1, one launch (start us, length us, event | category | flops | bytes accessed | tf_op | source)
XLA Modules:
  0.0 56.5 jit_solution(2511219845087198701)
XLA Ops:
  0.0 2.1 %act_first.1 = (bf16[32,16,384]{2,1,0:T(8,128)(2,1)S(1)}, f32[3,512,128]{2,1,0:T(8,128)S(1)}, bf16[19,16,384]{2,1,0:T(8,128)(2,1)S(1)}, bf16[19,16,384]{2,1,0:T(...) custom-call(bf16[16,4,8,384]{3,2,1,0:T(8,128)(2,1)} %feat_h.1, ...), custom_call_target="tpu_custom_call" | custom-call | tf_op jit(solution)/shard_map/act_first/pallas_call | solution.py:396
  2.1 2.2 %collective-permute-start = (bf16[19,16,384]{2,1,0:T(8,128)(2,1)S(1)}, bf16[19,16,384]{2,1,0:T(8,128)(2,1)S(1)}, u32[]{:S(2)}, u32[]{:S(2)}) collective-permute-start(bf16[19,16,384]{2,1,0:T(8,128)(2,1)S(1)} %get-tuple-element.25), channel_id=1, source_target_pairs={{0,8},{8,16},{16,24},{24,32},{32,40},{40,48},{48,56},{56,64},{64,7... | collective-permute-start | bytes 700424 | tf_op jit(solution)/shard_map/ppermute | solution.py:414
  4.3 3.7 %collective-permute-start.1 = (bf16[19,16,384]{2,1,0:T(8,128)(2,1)S(1)}, bf16[19,16,384]{2,1,0:T(8,128)(2,1)S(1)}, u32[]{:S(2)}, u32[]{:S(2)}) collective-permute-start(bf16[19,16,384]{2,1,0:T(8,128)(2,1)S(1)} %get-tuple-element.26), channel_id=1, source_target_pairs={{0,120},{8,0},{16,8},{24,16},{32,24},{40,32},{48,40},{56,48},{64,5... | collective-permute-start | bytes 700424 | tf_op jit(solution)/shard_map/ppermute | solution.py:415
  8.0 8.7 %inner.1 = (f32[6,10,16,384]{3,2,1,0:T(8,128)S(1)}, bf16[2,6,16,1152]{3,2,1,0:T(8,128)(2,1)S(1)}, bf16[3,9,384,384]{3,2,1,0:T(8,128)(2,1)S(1)}, bf16[3,9,384,384...) custom-call(bf16[32,16,384]{2,1,0:T(8,128)(2,1)S(1)} %get-tuple-element.24.own, ...), custom_call_target="tpu_custom_call" | custom-call | flops 4076863488 | bytes 17825792 | tf_op jit(solution)/shard_map/inner/pallas_call | solution.py:417
  16.7 0.0 collective-permute-done.top
  16.8 0.0 collective-permute-done.1.bot
  16.8 0.1 pack_columns.1
  16.9 2.5 %collective-permute-start.2 = (bf16[19,16,384]{2,1,0:T(8,128)(2,1)S(1)}, bf16[19,16,384]{2,1,0:T(8,128)(2,1)S(1)}, u32[]{:S(2)}, u32[]{:S(2)}) collective-permute-start(bf16[19,16,384]{2,1,0:T(8,128)(2,1)S(1)} %get-tuple-element.32), channel_id=1, source_target_pairs={{0,1},{1,2},{2,3},{3,4},{4,5},{5,6},{6,7},{7,0},{8,9},{9,10},{10,1... | collective-permute-start | bytes 700424 | tf_op jit(solution)/shard_map/ppermute | solution.py:432
  19.4 0.0 collective-permute-start.3
  19.4 3.1 %rows.1 = (f32[6,4,16,384]{3,2,1,0:T(8,128)S(1)}, bf16[4,6,16,1152]{3,2,1,0:T(8,128)(2,1)S(1)}) custom-call(bf16[19,16,384]{2,1,0:T(8,128)(2,1)S(1)} %collective-permute-done.top, bf16[19,16,384]{2,1,0:T(8,128)(2,1)S(1)} %collective-permute-done.1.bot, f32[6,10,16,384]{3,2,1,0:T(8,128)S(1)} %get-tuple-element.34.acc, ...), custom_call_target="tpu_custom_call" | custom-call | flops 2038431744 | bytes 10485760 | tf_op jit(solution)/shard_map/rows/pallas_call | solution.py:434
  22.5 0.0 collective-permute-done.2.left
  22.5 2.4 %collective-permute-done.3.right = bf16[19,16,384]{2,1,0:T(8,128)(2,1)S(1)} collective-permute-done((bf16[19,16,384]{2,1,0:T(8,128)(2,1)S(1)}, bf16[19,16,384]{2,1,0:T(8,128)(2,1)S(1)}, u32[]{:S(2)}, u32[]{:S(2)}) %collective-permute-start.3) | collective-permute-done | bytes 233504 | tf_op jit(solution)/shard_map/ppermute | solution.py:433
  24.9 11.1 %finish.1 = bf16[16,8,16,128]{3,2,1,0:T(8,128)(2,1)S(1)} custom-call(bf16[19,16,384]{2,1,0:T(8,128)(2,1)S(1)} %collective-permute-done.2.left, bf16[19,16,384]{2,1,0:T(8,128)(2,1)S(1)} %collective-permute-done.3.right, bf16[19,16,384]{2,1,0:T(8,128)(2,1)S(1)} %collective-permute-done.top, bf16[19,16,384]{2,1,0:T(8,128)(2,1)S(1)} %collective-permute-done.1.bot, ...), custom_call_target="tpu_custom_call" | custom-call | flops 6115295232 | bytes 20971520 | tf_op jit(solution)/shard_map/finish/pallas_call | solution.py:441
  36.0 19.8 %all_to_all.5.slots = bf16[128,16,128]{2,1,0:T(8,128)(2,1)S(1)} all-to-all(bf16[128,16,128]{2,1,0:T(8,128)(2,1)S(1)} %bitcast.2), channel_id=1, replica_groups=mesh['ha'=16,'wa'=8] {'ha','wa'}, dimensions={0} | all-to-all | bytes 1048576 | tf_op jit(solution)/shard_map/all_to_all | solution.py:457
  55.8 0.7 %sum_patches.1 = bf16[128,128]{1,0:T(8,128)(2,1)} custom-call(bf16[128,16,128]{2,1,0:T(8,128)(2,1)S(1)} %all_to_all.5.slots, f32[8,128]{1,0:T(8,128)S(1)} %get-tuple-element.42.bias), custom_call_target="tpu_custom_call" | custom-call | tf_op jit(solution)/shard_map/sum_patches/pallas_call | solution.py:458
Async XLA Ops:
  2.1 14.7 %collective-permute-start = (bf16[19,16,384]{2,1,0:T(8,128)(2,1)S(1)}, bf16[19,16,384]{2,1,0:T(8,128)(2,1)S(1)}, u32[]{:S(2)}, u32[]{:S(2)}) collective-permute-start(bf16[19,16,384]{2,1,0:T(8,128)(2,1)S(1)} %get-tuple-element.25), channel_id=1, source_target_pairs={{0,8},{8,16},{16,24},{24,32},{32,40},{40,48},{48,56},{56,64},{64,7... | collective-permute-start | bytes 700424 | tf_op jit(solution)/shard_map/ppermute | solution.py:414
  4.3 12.5 %collective-permute-start.1 = (bf16[19,16,384]{2,1,0:T(8,128)(2,1)S(1)}, bf16[19,16,384]{2,1,0:T(8,128)(2,1)S(1)}, u32[]{:S(2)}, u32[]{:S(2)}) collective-permute-start(bf16[19,16,384]{2,1,0:T(8,128)(2,1)S(1)} %get-tuple-element.26), channel_id=1, source_target_pairs={{0,120},{8,0},{16,8},{24,16},{32,24},{40,32},{48,40},{56,48},{64,5... | collective-permute-start | bytes 700424 | tf_op jit(solution)/shard_map/ppermute | solution.py:415
  16.9 5.7 %collective-permute-start.2 = (bf16[19,16,384]{2,1,0:T(8,128)(2,1)S(1)}, bf16[19,16,384]{2,1,0:T(8,128)(2,1)S(1)}, u32[]{:S(2)}, u32[]{:S(2)}) collective-permute-start(bf16[19,16,384]{2,1,0:T(8,128)(2,1)S(1)} %get-tuple-element.32), channel_id=1, source_target_pairs={{0,1},{1,2},{2,3},{3,4},{4,5},{5,6},{6,7},{7,0},{8,9},{9,10},{10,1... | collective-permute-start | bytes 700424 | tf_op jit(solution)/shard_map/ppermute | solution.py:432
  19.4 5.5 %collective-permute-start.3 = (bf16[19,16,384]{2,1,0:T(8,128)(2,1)S(1)}, bf16[19,16,384]{2,1,0:T(8,128)(2,1)S(1)}, u32[]{:S(2)}, u32[]{:S(2)}) collective-permute-start(bf16[19,16,384]{2,1,0:T(8,128)(2,1)S(1)} %get-tuple-element.33), channel_id=1, source_target_pairs={{0,7},{1,0},{2,1},{3,2},{4,3},{5,4},{6,5},{7,6},{8,15},{9,8},{10,9... | collective-permute-start | bytes 700424 | tf_op jit(solution)/shard_map/ppermute | solution.py:433

commit v6 on v5

--- a/solution.py
+++ b/solution.py
@@ -145,7 +145,7 @@
     return ha > 0, ha < lax.axis_size("ha") - 1, wa > 0, wa < lax.axis_size("wa") - 1
 
 
-def inner_kernel(own, plain, cfw, csw, vec, w1, w2, wh, acc, s2, w1v, w2v, wy, raw, s1, sems):
+def inner_kernel(own, cfw, w1, w2, wh, acc, w1v, w2v, wy, s1, sems):
     def group(src, dst, a, sem):
         return [
             pltpu.make_async_copy(src.at[t, a, b], dst.at[a, b * 3 + t], sem) for b in range(3) for t in range(3)
@@ -182,15 +182,11 @@
         part = jnp.dot(s1[...].reshape(R * Q * F, 3 * C), three(w1v, a), preferred_element_type=F32)
         for b in range(3):
             acc[2 - a : 2 - a + R, 2 - b : 2 - b + Q] += part[:, b * C : (b + 1) * C].reshape(R, Q, F, C)
-    for h in range(2):
-        hidden(s2, (h, pl.ds(0, 6)), acc[2 + h, 2:8].reshape(6 * F, C), vec, cached_row(csw, (1 + h) * 16, 1, 6))
-    for k in range(R * Q):
-        raw[k] = rows_at(plain, k, F, R * Q).astype(BF16)
     for copy in later:
         copy.wait()
 
 
-def rows_kernel(top, bot, acc, csw, vec, w1v, sides, s2, s1, add):
+def rows_kernel(top, bot, acc, plain, csw, vec, w1v, sides, s2, raw, s1, add):
     up, down, _, _ = place()
     for msg, h0, valid in ((top, 0, up), (bot, 2, down)):
         for h in range(2):
@@ -207,10 +203,15 @@
     for n, cached, valid in (
         (0, [c[1:7] for c in cached_msg(top[18])], up),
         (1, cached_row(csw, 0, 1, 6), None),
-        (2, cached_row(csw, 48, 1, 6), None),
-        (3, [c[1:7] for c in cached_msg(bot[18])], down),
+        (2, cached_row(csw, 16, 1, 6), None),
+        (3, cached_row(csw, 32, 1, 6), None),
+        (4, cached_row(csw, 48, 1, 6), None),
+        (5, [c[1:7] for c in cached_msg(bot[18])], down),
     ):
-        hidden(s2, (n, pl.ds(0, 6)), add[n, 2:8].reshape(6 * F, C), vec, cached, valid)
+        total = acc[n, 2:8] if 2 <= n < 4 else add[n if n < 2 else n - 2, 2:8]
+        hidden(s2, (n, pl.ds(0, 6)), total.reshape(6 * F, C), vec, cached, valid)
+    for k in range(R * Q):
+        raw[k] = rows_at(plain, k, F, R * Q).astype(BF16)
     for n, col in enumerate((0, 8)):
         sides[0:2, 2 * n : 2 * n + 2] = add[0:2, col : col + 2]
         sides[2:4, 2 * n : 2 * n + 2] = acc[2:4, col : col + 2]
@@ -218,7 +219,7 @@
 
 
 def finish_kernel(
-    left, right, top, bot, sides, inner2, rows2, raw, csw, chw, vec, w1v, w2v, wy, out,
+    left, right, top, bot, sides, rows2, raw, csw, chw, vec, w1v, w2v, wy, out,
     s1, acc1, s2, s3, acc2, acch, side_f, side_s,
 ):
     up, down, west, east = place()
@@ -247,9 +248,7 @@
         part = jnp.dot(taken, weight, preferred_element_type=F32).reshape(6, 2, F, C)
         for n, col in enumerate(targets):
             acc1[:, col] += part[:, n]
-    s2[2:4, 2:8] = inner2[...]
-    s2[0:2, 2:8] = rows2[0:2]
-    s2[4:6, 2:8] = rows2[2:4]
+    s2[:, 2:8] = rows2[...]
     for h in range(6):
         inside = up if h == 0 else down if h == 5 else True
         if h == 0:
@@ -414,34 +413,33 @@
     top = lax.ppermute(hi, "ha", around("ha", 1))
     bot = lax.ppermute(lo, "ha", around("ha", -1))
     cell_flops = 2 * F * 27 * C * C
-    sums1, inner2, w1v, w2v, wy, raw = kernel(
+    sums1, w1v, w2v, wy = kernel(
         inner_kernel,
-        [near(R + 2, Q + 2, F, C, dtype=F32), near(2, 6, F, 3 * C), near(3, 9, C, C), near(3, 9, C, C), near(3 * 128, 3 * C),
-         near(32, F, C)],
-        [VM] * 5 + [ANY] * 3,
+        [near(R + 2, Q + 2, F, C, dtype=F32), near(3, 9, C, C), near(3, 9, C, C), near(3 * 128, 3 * C)],
+        [VM] * 2 + [ANY] * 3,
         [pltpu.VMEM((R * Q, F, 3 * C), BF16), pltpu.SemaphoreType.DMA((7,))],
         12, "inner", 32 * cell_flops, 17 * 2**20,
-    )(own, plain, cfw, csw, vec, far(conv_first), far(conv_second), far(jnp.swapaxes(conv_head, 3, 4)))
+    )(own, cfw, far(conv_first), far(conv_second), far(jnp.swapaxes(conv_head, 3, 4)))
     to_left, to_right = kernel(
         pack_kernel,
         [near(MSG, F, C)] * 2,
         [VM] * 6,
         [pltpu.VMEM((3, 128, 128), F32)] * 2,
         4, "pack_columns",
-    )(own, top, bot, cfw, csw, inner2)
+    )(own, top, bot, cfw, csw, wy)
     left = lax.ppermute(to_right, "wa", around("wa", 1))
     right = lax.ppermute(to_left, "wa", around("wa", -1))
-    sides, rows2 = kernel(
+    sides, rows2, raw = kernel(
         rows_kernel,
-        [near(R + 2, 4, F, C, dtype=F32), near(4, 6, F, 3 * C)],
-        [VM] * 6,
+        [near(R + 2, 4, F, C, dtype=F32), near(R + 2, 6, F, 3 * C), near(32, F, C)],
+        [VM] * 7,
         [pltpu.VMEM((4, Q, F, 3 * C), BF16), pltpu.VMEM((4, Q + 2, F, C), F32)],
         10, "rows", 16 * cell_flops, 10 * 2**20,
-    )(top, bot, sums1, csw, vec, w1v)
+    )(top, bot, sums1, plain, csw, vec, w1v)
     (slots,) = kernel(
         finish_kernel,
         [shape(F, 8, 16, 128)],
-        [VM] * 14,
+        [VM] * 13,
         [
             pltpu.VMEM((8, 4, F, 3 * C), BF16),
             pltpu.VMEM((R + 2, 4, F, C), F32),
@@ -453,7 +451,7 @@
             pltpu.VMEM((2, 16, C), F32),
         ],
         20, "finish", 48 * cell_flops, 20 * 2**20,
-    )(left, right, top, bot, sides, inner2, rows2, raw, csw, chw, vec, w1v, w2v, wy)
+    )(left, right, top, bot, sides, rows2, raw, csw, chw, vec, w1v, w2v, wy)
     arrived = lax.all_to_all(slots.reshape(F * 8, 16, 128), ("ha", "wa"), 0, 0, tiled=True)
     return pl.pallas_call(
         last_kernel,

time: 56.7 us -> 56.3 us (level)
  no operation moved by 1% of the time
where the time goes in v6:
time: 56.3 us; the launch traced here: 56.1 us
  Pallas kernels  25.8 us (46%)
  blocking collectives  20 us (36%)
  starting transfers between devices  8.45 us (15%)
  waiting for transfers between devices  1.82 us (3%)
    all_to_all x1, blocking collectives, local(): lax.all_to_all(slots.reshape(F * 8, 16, 128), ('ha', 'wa'), 0, 0, tiled=T...  20 us
    pallas_call x1, Pallas kernels, local(): kernel(finish_kernel, [shape(F, 8, 16, 128)], [VM] * 13, [pltpu.VMEM((8,...  11.1 us
    pallas_call x1, Pallas kernels, local(): kernel(inner_kernel, [near(R + 2, Q + 2, F, C, dtype=F32), near(3, 9, C,...  8.1 us
    ppermute x1, starting transfers between devices, local(): bot = lax.ppermute(lo, 'ha', around('ha', -1))  3.71 us
    pallas_call x1, Pallas kernels, local(): kernel(rows_kernel, [near(R + 2, 4, F, C, dtype=F32), near(R + 2, 6, F, 3...  3.66 us
    ppermute x1, starting transfers between devices, local(): left = lax.ppermute(to_right, 'wa', around('wa', 1))  2.54 us
    ppermute x1, starting transfers between devices, local(): top = lax.ppermute(hi, 'ha', around('ha', 1))  2.19 us
    pallas_call x1, Pallas kernels, local(): kernel(first_kernel, [near(32, F, C), near(3, F * R * Q, 128, dtype=F32),...  2.08 us
  transfers between devices with their start and end apart: 4, of which 1 were waited for; matrix products, arithmetic and copies ran while one was open for 0% of the time, Pallas kernels for 21%

profile of v6, /device:TPU:1, one launch (start us, length us, event | category | flops | bytes accessed | tf_op | source)
XLA Modules:
  0.0 56.1 jit_solution(12968763316171684990)
XLA Ops:
  0.0 2.1 %act_first.1 = (bf16[32,16,384]{2,1,0:T(8,128)(2,1)S(1)}, f32[3,512,128]{2,1,0:T(8,128)S(1)}, bf16[19,16,384]{2,1,0:T(8,128)(2,1)S(1)}, bf16[19,16,384]{2,1,0:T(...) custom-call(bf16[16,4,8,384]{3,2,1,0:T(8,128)(2,1)} %feat_h.1, ...), custom_call_target="tpu_custom_call" | custom-call | tf_op jit(solution)/shard_map/act_first/pallas_call | solution.py:395
  2.1 2.2 %collective-permute-start = (bf16[19,16,384]{2,1,0:T(8,128)(2,1)S(1)}, bf16[19,16,384]{2,1,0:T(8,128)(2,1)S(1)}, u32[]{:S(2)}, u32[]{:S(2)}) collective-permute-start(bf16[19,16,384]{2,1,0:T(8,128)(2,1)S(1)} %get-tuple-element.24), channel_id=1, source_target_pairs={{0,8},{8,16},{16,24},{24,32},{32,40},{40,48},{48,56},{56,64},{64,7... | collective-permute-start | bytes 700424 | tf_op jit(solution)/shard_map/ppermute | solution.py:413
  4.3 3.7 %collective-permute-start.1 = (bf16[19,16,384]{2,1,0:T(8,128)(2,1)S(1)}, bf16[19,16,384]{2,1,0:T(8,128)(2,1)S(1)}, u32[]{:S(2)}, u32[]{:S(2)}) collective-permute-start(bf16[19,16,384]{2,1,0:T(8,128)(2,1)S(1)} %get-tuple-element.25), channel_id=1, source_target_pairs={{0,120},{8,0},{16,8},{24,16},{32,24},{40,32},{48,40},{56,48},{64,5... | collective-permute-start | bytes 700424 | tf_op jit(solution)/shard_map/ppermute | solution.py:414
  8.0 8.1 %inner.1 = (f32[6,10,16,384]{3,2,1,0:T(8,128)S(1)}, bf16[3,9,384,384]{3,2,1,0:T(8,128)(2,1)S(1)}, bf16[3,9,384,384]{3,2,1,0:T(8,128)(2,1)S(1)}, bf16[384,1152]{1,0:T(8,128)(2,1)S(1)}) custom-call(bf16[32,16,384]{2,1,0:T(8,128)(2,1)S(1)} %get-tuple-element.23.own, f32[3,64,128]{2,1,0:T(8,128)S(1)} %get-tuple-element.26.cfw, bf16[3,3,3,384,384]{4,3,2,1,0:T(8,128)(2,1)} %w1.1, ...), custom_call_target="tpu_custom_call" | custom-call | flops 4076863488 | bytes 17825792 | tf_op jit(solution)/shard_map/inner/pallas_call | solution.py:416
  16.1 0.0 collective-permute-done.top
  16.1 0.0 collective-permute-done.1.bot
  16.1 0.1 pack_columns.1
  16.2 2.5 %collective-permute-start.2 = (bf16[19,16,384]{2,1,0:T(8,128)(2,1)S(1)}, bf16[19,16,384]{2,1,0:T(8,128)(2,1)S(1)}, u32[]{:S(2)}, u32[]{:S(2)}) collective-permute-start(bf16[19,16,384]{2,1,0:T(8,128)(2,1)S(1)} %get-tuple-element.29), channel_id=1, source_target_pairs={{0,1},{1,2},{2,3},{3,4},{4,5},{5,6},{6,7},{7,0},{8,9},{9,10},{10,1... | collective-permute-start | bytes 700424 | tf_op jit(solution)/shard_map/ppermute | solution.py:430
  18.8 0.0 collective-permute-start.3
  18.8 3.7 %rows.1 = (f32[6,4,16,384]{3,2,1,0:T(8,128)S(1)}, bf16[6,6,16,1152]{3,2,1,0:T(8,128)(2,1)S(1)}, bf16[32,16,384]{2,1,0:T(8,128)(2,1)S(1)}) custom-call(bf16[19,16,384]{2,1,0:T(8,128)(2,1)S(1)} %collective-permute-done.top, bf16[19,16,384]{2,1,0:T(8,128)(2,1)S(1)} %collective-permute-done.1.bot, f32[6,10,16,384]{3,2,1,0:T(8,128)S(1)} %get-tuple-element.31.acc, ...), custom_call_target="tpu_custom_call" | custom-call | flops 2038431744 | bytes 10485760 | tf_op jit(solution)/shard_map/rows/pallas_call | solution.py:432
  22.4 0.0 collective-permute-done.2.left
  22.4 1.8 %collective-permute-done.3.right = bf16[19,16,384]{2,1,0:T(8,128)(2,1)S(1)} collective-permute-done((bf16[19,16,384]{2,1,0:T(8,128)(2,1)S(1)}, bf16[19,16,384]{2,1,0:T(8,128)(2,1)S(1)}, u32[]{:S(2)}, u32[]{:S(2)}) %collective-permute-start.3) | collective-permute-done | bytes 233504 | tf_op jit(solution)/shard_map/ppermute | solution.py:431
  24.3 11.1 %finish.1 = bf16[16,8,16,128]{3,2,1,0:T(8,128)(2,1)S(1)} custom-call(bf16[19,16,384]{2,1,0:T(8,128)(2,1)S(1)} %collective-permute-done.2.left, bf16[19,16,384]{2,1,0:T(8,128)(2,1)S(1)} %collective-permute-done.3.right, bf16[19,16,384]{2,1,0:T(8,128)(2,1)S(1)} %collective-permute-done.top, bf16[19,16,384]{2,1,0:T(8,128)(2,1)S(1)} %collective-permute-done.1.bot, ...), custom_call_target="tpu_custom_call" | custom-call | flops 6115295232 | bytes 20971520 | tf_op jit(solution)/shard_map/finish/pallas_call | solution.py:439
  35.4 20.0 %all_to_all.5.slots = bf16[128,16,128]{2,1,0:T(8,128)(2,1)S(1)} all-to-all(bf16[128,16,128]{2,1,0:T(8,128)(2,1)S(1)} %bitcast.2), channel_id=1, replica_groups=mesh['ha'=16,'wa'=8] {'ha','wa'}, dimensions={0} | all-to-all | bytes 1048576 | tf_op jit(solution)/shard_map/all_to_all | solution.py:455
  55.4 0.7 %sum_patches.1 = bf16[128,128]{1,0:T(8,128)(2,1)} custom-call(bf16[128,16,128]{2,1,0:T(8,128)(2,1)S(1)} %all_to_all.5.slots, f32[8,128]{1,0:T(8,128)S(1)} %get-tuple-element.40.bias), custom_call_target="tpu_custom_call" | custom-call | tf_op jit(solution)/shard_map/sum_patches/pallas_call | solution.py:456
Async XLA Ops:
  2.1 14.0 %collective-permute-start = (bf16[19,16,384]{2,1,0:T(8,128)(2,1)S(1)}, bf16[19,16,384]{2,1,0:T(8,128)(2,1)S(1)}, u32[]{:S(2)}, u32[]{:S(2)}) collective-permute-start(bf16[19,16,384]{2,1,0:T(8,128)(2,1)S(1)} %get-tuple-element.24), channel_id=1, source_target_pairs={{0,8},{8,16},{16,24},{24,32},{32,40},{40,48},{48,56},{56,64},{64,7... | collective-permute-start | bytes 700424 | tf_op jit(solution)/shard_map/ppermute | solution.py:413
  4.3 11.8 %collective-permute-start.1 = (bf16[19,16,384]{2,1,0:T(8,128)(2,1)S(1)}, bf16[19,16,384]{2,1,0:T(8,128)(2,1)S(1)}, u32[]{:S(2)}, u32[]{:S(2)}) collective-permute-start(bf16[19,16,384]{2,1,0:T(8,128)(2,1)S(1)} %get-tuple-element.25), channel_id=1, source_target_pairs={{0,120},{8,0},{16,8},{24,16},{32,24},{40,32},{48,40},{56,48},{64,5... | collective-permute-start | bytes 700424 | tf_op jit(solution)/shard_map/ppermute | solution.py:414
  16.2 6.2 %collective-permute-start.2 = (bf16[19,16,384]{2,1,0:T(8,128)(2,1)S(1)}, bf16[19,16,384]{2,1,0:T(8,128)(2,1)S(1)}, u32[]{:S(2)}, u32[]{:S(2)}) collective-permute-start(bf16[19,16,384]{2,1,0:T(8,128)(2,1)S(1)} %get-tuple-element.29), channel_id=1, source_target_pairs={{0,1},{1,2},{2,3},{3,4},{4,5},{5,6},{6,7},{7,0},{8,9},{9,10},{10,1... | collective-permute-start | bytes 700424 | tf_op jit(solution)/shard_map/ppermute | solution.py:430
  18.8 5.5 %collective-permute-start.3 = (bf16[19,16,384]{2,1,0:T(8,128)(2,1)S(1)}, bf16[19,16,384]{2,1,0:T(8,128)(2,1)S(1)}, u32[]{:S(2)}, u32[]{:S(2)}) collective-permute-start(bf16[19,16,384]{2,1,0:T(8,128)(2,1)S(1)} %get-tuple-element.30), channel_id=1, source_target_pairs={{0,7},{1,0},{2,1},{3,2},{4,3},{5,4},{6,5},{7,6},{8,15},{9,8},{10,9... | collective-permute-start | bytes 700424 | tf_op jit(solution)/shard_map/ppermute | solution.py:431

commit v7 on v6

--- a/solution.py
+++ b/solution.py
@@ -145,6 +145,13 @@
     return ha > 0, ha < lax.axis_size("ha") - 1, wa > 0, wa < lax.axis_size("wa") - 1
 
 
+def reach(rh, rw):
+    return [
+        (2 * (rh - 1 + m) + r, 2 * (rw - 1 + n) + s)
+        for m in range(2) for n in range(2) for r in range(2) for s in range(2)
+    ]
+
+
 def inner_kernel(own, cfw, w1, w2, wh, acc, w1v, w2v, wy, s1, sems):
     def group(src, dst, a, sem):
         return [
@@ -153,19 +160,26 @@
 
     first = [group(w1, w1v, a, sems.at[a]) for a in range(3)]
     later = [copy for a in range(3) for copy in group(w2, w2v, a, sems.at[3 + a])]
-    for t in range(3):
-        for a in range(3):
-            for b in range(3):
-                later.append(
-                    pltpu.make_async_copy(
-                        wh.at[t, a, b], wy.at[pl.ds(a * 128 + b * 32, 32), pl.ds(t * C, C)], sems.at[6]
-                    )
-                )
+    empty = []
+    for rh in range(2):
+        for rw in range(2):
+            for k, (row, col) in enumerate(reach(rh, rw)):
+                a, b = rh + 1 - row, rw + 1 - col
+                where = pl.ds(k * 32, 32)
+                if 0 <= a <= 2 and 0 <= b <= 2:
+                    for t in range(3):
+                        later.append(
+                            pltpu.make_async_copy(
+                                wh.at[t, a, b], wy.at[rh * 2 + rw, where, pl.ds(t * C, C)], sems.at[6]
+                            )
+                        )
+                else:
+                    empty.append((rh * 2 + rw, where))
     for copies in first[:2]:
         for copy in copies:
             copy.start()
-    for a in range(3):
-        wy[pl.ds(a * 128 + 96, 32)] = jnp.zeros((32, 3 * C), BF16)
+    for where in empty:
+        wy[where] = jnp.zeros((32, 3 * C), BF16)
     acc[...] = jnp.zeros_like(acc)
 
     def cells(h, _):
@@ -228,18 +242,13 @@
             side_f[n, pl.ds(c * 16, 16)] = msg[16 + c].astype(F32)
         side_s[n] = msg[18].astype(F32)
     for n, (msg, side) in enumerate(((left, west), (right, east))):
-        def cells(h, _, n=n, msg=msg, side=side):
-            for k in range(2):
-                hh = h * 2 + k
-                put(
-                    s1, (hh, pl.ds(2 * n, 2)), msg[pl.ds(hh * 2, 2)].reshape(2 * F, C).astype(F32),
-                    [side_f[n, pl.ds(c * 16 + hh * 2, 1), :] for c in range(2)],
-                    [side_f[n, pl.ds(c * 16 + hh * 2 + 1, 1), :] for c in range(2)],
-                    side & (up | (hh >= 2)) & (down | (hh < 6)),
-                )
-            return 0
-
-        lax.fori_loop(0, 4, cells, 0)
+        for h in range(8):
+            valid = side & up if h < 2 else side & down if h >= 6 else side
+            put(
+                s1, (h, pl.ds(2 * n, 2)), msg[pl.ds(h * 2, 2)].reshape(2 * F, C).astype(F32),
+                [side_f[n, pl.ds(c * 16 + h * 2, 1), :] for c in range(2)],
+                [side_f[n, pl.ds(c * 16 + h * 2 + 1, 1), :] for c in range(2)], valid,
+            )
 
     acc1[...] = sides[...]
     for b, targets in enumerate(((0, 1), (0, 3), (2, 3))):
@@ -289,33 +298,29 @@
         + jnp.dot(window(2, R), side[2], preferred_element_type=F32)
     )
 
-    def last(h, _):
+    for h in range(R):
         wide = acc2[pl.ds(h * Q * F, Q * F)] + vec[pl.ds(3, 1), :]
         wide = wide + raw[pl.ds(h * Q, Q)].reshape(Q * F, C).astype(F32)
         c0, c1 = cached_row(chw, h * 16, 0, Q)
-        put(s3, (pl.ds(h * Q, Q),), act(wide.astype(BF16).astype(F32), vec[pl.ds(1, 1), :]), c0, c1)
-        return 0
-
-    lax.fori_loop(0, R, last, 0)
-    part = lax.dot_general(
-        s3[...].reshape(R * Q * F, 3 * C), wy[...], (((1,), (1,)), ((), ())), preferred_element_type=F32
-    )
-    lane = lax.broadcasted_iota(jnp.int32, (F, 128), 1)
+        now = act(wide.astype(BF16).astype(F32), vec[pl.ds(1, 1), :])
+        for n, part in enumerate(stack(now, c0, c1)):
+            part = part.reshape(Q, F, C)
+            for w in range(Q):
+                s3[h % 2 * 2 + w % 2, h // 2 * 4 + w // 2, :, pl.ds(n * C, C)] = part[w]
     sums = {}
-    for h in range(R):
-        for w in range(Q):
-            k = h * Q + w
-            for a in range(3):
-                block = part[k * F : (k + 1) * F, a * 128 : (a + 1) * 128]
-                for b in range(3):
-                    row, col = h + 1 - a, w + 1 - b
-                    pp, qq = (row // 2) % 3, (col // 2) % 5
-                    slot = pp * 4 + qq if qq < 4 else 12 + pp
-                    low = (2 * (row % 2) + col % 2) * 32
-                    shift = (low - 32 * b) % 128
-                    moved = pltpu.roll(block, shift, 1) if shift else block
-                    term = jnp.where((lane >= low) & (lane < low + 32), moved, 0.0)
-                    sums[slot] = sums[slot] + term if slot in sums else term
+    for rh in range(2):
+        for rw in range(2):
+            part = lax.dot_general(
+                s3[rh * 2 + rw].reshape(8 * F, 3 * C), wy[rh * 2 + rw], (((1,), (1,)), ((), ())),
+                preferred_element_type=F32,
+            )
+            for k in range(8):
+                for m in range(2):
+                    for n in range(2):
+                        pp, qq = (k // 4 + rh - 1 + m) % 3, (k % 4 + rw - 1 + n) % 5
+                        slot = pp * 4 + qq if qq < 4 else 12 + pp
+                        term = part[k * F : (k + 1) * F, (m * 2 + n) * 128 : (m * 2 + n + 1) * 128]
+                        sums[slot] = sums[slot] + term if slot in sums else term
     for slot, total in sums.items():
         acch[pl.ds(slot * F, F)] = total
     acch[pl.ds(15 * F, F)] = jnp.zeros((F, 128), F32)
@@ -415,7 +420,7 @@
     cell_flops = 2 * F * 27 * C * C
     sums1, w1v, w2v, wy = kernel(
         inner_kernel,
-        [near(R + 2, Q + 2, F, C, dtype=F32), near(3, 9, C, C), near(3, 9, C, C), near(3 * 128, 3 * C)],
+        [near(R + 2, Q + 2, F, C, dtype=F32), near(3, 9, C, C), near(3, 9, C, C), near(4, 512, 3 * C)],
         [VM] * 2 + [ANY] * 3,
         [pltpu.VMEM((R * Q, F, 3 * C), BF16), pltpu.SemaphoreType.DMA((7,))],
         12, "inner", 32 * cell_flops, 17 * 2**20,
@@ -444,7 +449,7 @@
             pltpu.VMEM((8, 4, F, 3 * C), BF16),
             pltpu.VMEM((R + 2, 4, F, C), F32),
             pltpu.VMEM((R + 2, Q + 2, F, 3 * C), BF16),
-            pltpu.VMEM((R * Q, F, 3 * C), BF16),
+            pltpu.VMEM((4, 8, F, 3 * C), BF16),
             pltpu.VMEM((R * Q * F, C), F32),
             pltpu.VMEM((16 * F, 128), F32),
             pltpu.VMEM((2, 32, C), F32),

time: 56.3 us -> 55.9 us (level)
  no operation moved by 1% of the time
where the time goes in v7:
time: 55.9 us; the launch traced here: 55.7 us
  Pallas kernels  25.4 us (45%)
  blocking collectives  20 us (36%)
  starting transfers between devices  8.46 us (15%)
  waiting for transfers between devices  1.82 us (3%)
    all_to_all x1, blocking collectives, local(): lax.all_to_all(slots.reshape(F * 8, 16, 128), ('ha', 'wa'), 0, 0, tiled=T...  20 us
    pallas_call x1, Pallas kernels, local(): kernel(finish_kernel, [shape(F, 8, 16, 128)], [VM] * 13, [pltpu.VMEM((8,...  10.7 us
    pallas_call x1, Pallas kernels, local(): kernel(inner_kernel, [near(R + 2, Q + 2, F, C, dtype=F32), near(3, 9, C,...  8.13 us
    ppermute x1, starting transfers between devices, local(): bot = lax.ppermute(lo, 'ha', around('ha', -1))  3.71 us
    pallas_call x1, Pallas kernels, local(): kernel(rows_kernel, [near(R + 2, 4, F, C, dtype=F32), near(R + 2, 6, F, 3...  3.66 us
    ppermute x1, starting transfers between devices, local(): left = lax.ppermute(to_right, 'wa', around('wa', 1))  2.55 us
    ppermute x1, starting transfers between devices, local(): top = lax.ppermute(hi, 'ha', around('ha', 1))  2.19 us
    pallas_call x1, Pallas kernels, local(): kernel(first_kernel, [near(32, F, C), near(3, F * R * Q, 128, dtype=F32),...  2.08 us
  transfers between devices with their start and end apart: 4, of which 1 were waited for; matrix products, arithmetic and copies ran while one was open for 0% of the time, Pallas kernels for 21%

profile of v7, /device:TPU:1, one launch (start us, length us, event | category | flops | bytes accessed | tf_op | source)
XLA Modules:
  0.0 55.7 jit_solution(10116531843002427070)
XLA Ops:
  0.0 2.1 %act_first.1 = (bf16[32,16,384]{2,1,0:T(8,128)(2,1)S(1)}, f32[3,512,128]{2,1,0:T(8,128)S(1)}, bf16[19,16,384]{2,1,0:T(8,128)(2,1)S(1)}, bf16[19,16,384]{2,1,0:T(...) custom-call(bf16[16,4,8,384]{3,2,1,0:T(8,128)(2,1)} %feat_h.1, ...), custom_call_target="tpu_custom_call" | custom-call | tf_op jit(solution)/shard_map/act_first/pallas_call | solution.py:400
  2.1 2.2 %collective-permute-start = (bf16[19,16,384]{2,1,0:T(8,128)(2,1)S(1)}, bf16[19,16,384]{2,1,0:T(8,128)(2,1)S(1)}, u32[]{:S(2)}, u32[]{:S(2)}) collective-permute-start(bf16[19,16,384]{2,1,0:T(8,128)(2,1)S(1)} %get-tuple-element.24), channel_id=1, source_target_pairs={{0,8},{8,16},{16,24},{24,32},{32,40},{40,48},{48,56},{56,64},{64,7... | collective-permute-start | bytes 700424 | tf_op jit(solution)/shard_map/ppermute | solution.py:418
  4.3 3.7 %collective-permute-start.1 = (bf16[19,16,384]{2,1,0:T(8,128)(2,1)S(1)}, bf16[19,16,384]{2,1,0:T(8,128)(2,1)S(1)}, u32[]{:S(2)}, u32[]{:S(2)}) collective-permute-start(bf16[19,16,384]{2,1,0:T(8,128)(2,1)S(1)} %get-tuple-element.25), channel_id=1, source_target_pairs={{0,120},{8,0},{16,8},{24,16},{32,24},{40,32},{48,40},{56,48},{64,5... | collective-permute-start | bytes 700424 | tf_op jit(solution)/shard_map/ppermute | solution.py:419
  8.0 8.1 %inner.1 = (f32[6,10,16,384]{3,2,1,0:T(8,128)S(1)}, bf16[3,9,384,384]{3,2,1,0:T(8,128)(2,1)S(1)}, bf16[3,9,384,384]{3,2,1,0:T(8,128)(2,1)S(1)}, bf16[4,512,1152]{2,1,0:T(8,128)(2,1)S(1)}) custom-call(bf16[32,16,384]{2,1,0:T(8,128)(2,1)S(1)} %get-tuple-element.23.own, f32[3,64,128]{2,1,0:T(8,128)S(1)} %get-tuple-element.26.cfw, ...), custom_call_target="tpu_custom_call" | custom-call | flops 4076863488 | bytes 17825792 | tf_op jit(solution)/shard_map/inner/pallas_call | solution.py:421
  16.1 0.0 collective-permute-done.top
  16.1 0.0 collective-permute-done.1.bot
  16.2 0.1 pack_columns.1
  16.3 2.6 %collective-permute-start.2 = (bf16[19,16,384]{2,1,0:T(8,128)(2,1)S(1)}, bf16[19,16,384]{2,1,0:T(8,128)(2,1)S(1)}, u32[]{:S(2)}, u32[]{:S(2)}) collective-permute-start(bf16[19,16,384]{2,1,0:T(8,128)(2,1)S(1)} %get-tuple-element.29), channel_id=1, source_target_pairs={{0,1},{1,2},{2,3},{3,4},{4,5},{5,6},{6,7},{7,0},{8,9},{9,10},{10,1... | collective-permute-start | bytes 700424 | tf_op jit(solution)/shard_map/ppermute | solution.py:435
  18.8 0.0 collective-permute-start.3
  18.8 3.7 %rows.1 = (f32[6,4,16,384]{3,2,1,0:T(8,128)S(1)}, bf16[6,6,16,1152]{3,2,1,0:T(8,128)(2,1)S(1)}, bf16[32,16,384]{2,1,0:T(8,128)(2,1)S(1)}) custom-call(bf16[19,16,384]{2,1,0:T(8,128)(2,1)S(1)} %collective-permute-done.top, bf16[19,16,384]{2,1,0:T(8,128)(2,1)S(1)} %collective-permute-done.1.bot, f32[6,10,16,384]{3,2,1,0:T(8,128)S(1)} %get-tuple-element.31.acc, ...), custom_call_target="tpu_custom_call" | custom-call | flops 2038431744 | bytes 10485760 | tf_op jit(solution)/shard_map/rows/pallas_call | solution.py:437
  22.5 0.0 collective-permute-done.2.left
  22.5 1.8 %collective-permute-done.3.right = bf16[19,16,384]{2,1,0:T(8,128)(2,1)S(1)} collective-permute-done((bf16[19,16,384]{2,1,0:T(8,128)(2,1)S(1)}, bf16[19,16,384]{2,1,0:T(8,128)(2,1)S(1)}, u32[]{:S(2)}, u32[]{:S(2)}) %collective-permute-start.3) | collective-permute-done | bytes 233504 | tf_op jit(solution)/shard_map/ppermute | solution.py:436
  24.3 10.7 %finish.1 = bf16[16,8,16,128]{3,2,1,0:T(8,128)(2,1)S(1)} custom-call(bf16[19,16,384]{2,1,0:T(8,128)(2,1)S(1)} %collective-permute-done.2.left, bf16[19,16,384]{2,1,0:T(8,128)(2,1)S(1)} %collective-permute-done.3.right, bf16[19,16,384]{2,1,0:T(8,128)(2,1)S(1)} %collective-permute-done.top, bf16[19,16,384]{2,1,0:T(8,128)(2,1)S(1)} %collective-permute-done.1.bot, ...), custom_call_target="tpu_custom_call" | custom-call | flops 6115295232 | bytes 20971520 | tf_op jit(solution)/shard_map/finish/pallas_call | solution.py:444
  35.0 20.0 %all_to_all.5.slots = bf16[128,16,128]{2,1,0:T(8,128)(2,1)S(1)} all-to-all(bf16[128,16,128]{2,1,0:T(8,128)(2,1)S(1)} %bitcast.2), channel_id=1, replica_groups=mesh['ha'=16,'wa'=8] {'ha','wa'}, dimensions={0} | all-to-all | bytes 1048576 | tf_op jit(solution)/shard_map/all_to_all | solution.py:460
  55.0 0.7 %sum_patches.1 = bf16[128,128]{1,0:T(8,128)(2,1)} custom-call(bf16[128,16,128]{2,1,0:T(8,128)(2,1)S(1)} %all_to_all.5.slots, f32[8,128]{1,0:T(8,128)S(1)} %get-tuple-element.40.bias), custom_call_target="tpu_custom_call" | custom-call | tf_op jit(solution)/shard_map/sum_patches/pallas_call | solution.py:461
Async XLA Ops:
  2.1 14.0 %collective-permute-start = (bf16[19,16,384]{2,1,0:T(8,128)(2,1)S(1)}, bf16[19,16,384]{2,1,0:T(8,128)(2,1)S(1)}, u32[]{:S(2)}, u32[]{:S(2)}) collective-permute-start(bf16[19,16,384]{2,1,0:T(8,128)(2,1)S(1)} %get-tuple-element.24), channel_id=1, source_target_pairs={{0,8},{8,16},{16,24},{24,32},{32,40},{40,48},{48,56},{56,64},{64,7... | collective-permute-start | bytes 700424 | tf_op jit(solution)/shard_map/ppermute | solution.py:418
  4.3 11.9 %collective-permute-start.1 = (bf16[19,16,384]{2,1,0:T(8,128)(2,1)S(1)}, bf16[19,16,384]{2,1,0:T(8,128)(2,1)S(1)}, u32[]{:S(2)}, u32[]{:S(2)}) collective-permute-start(bf16[19,16,384]{2,1,0:T(8,128)(2,1)S(1)} %get-tuple-element.25), channel_id=1, source_target_pairs={{0,120},{8,0},{16,8},{24,16},{32,24},{40,32},{48,40},{56,48},{64,5... | collective-permute-start | bytes 700424 | tf_op jit(solution)/shard_map/ppermute | solution.py:419
  16.3 6.2 %collective-permute-start.2 = (bf16[19,16,384]{2,1,0:T(8,128)(2,1)S(1)}, bf16[19,16,384]{2,1,0:T(8,128)(2,1)S(1)}, u32[]{:S(2)}, u32[]{:S(2)}) collective-permute-start(bf16[19,16,384]{2,1,0:T(8,128)(2,1)S(1)} %get-tuple-element.29), channel_id=1, source_target_pairs={{0,1},{1,2},{2,3},{3,4},{4,5},{5,6},{6,7},{7,0},{8,9},{9,10},{10,1... | collective-permute-start | bytes 700424 | tf_op jit(solution)/shard_map/ppermute | solution.py:435
  18.8 5.5 %collective-permute-start.3 = (bf16[19,16,384]{2,1,0:T(8,128)(2,1)S(1)}, bf16[19,16,384]{2,1,0:T(8,128)(2,1)S(1)}, u32[]{:S(2)}, u32[]{:S(2)}) collective-permute-start(bf16[19,16,384]{2,1,0:T(8,128)(2,1)S(1)} %get-tuple-element.30), channel_id=1, source_target_pairs={{0,7},{1,0},{2,1},{3,2},{4,3},{5,4},{6,5},{7,6},{8,15},{9,8},{10,9... | collective-permute-start | bytes 700424 | tf_op jit(solution)/shard_map/ppermute | solution.py:436

commit v8 on v7

--- a/solution.py
+++ b/solution.py
@@ -251,12 +251,21 @@
             )
 
     acc1[...] = sides[...]
+    def columns(first):
+        return jnp.concatenate([s1[a : a + 6, first : first + 2].reshape(12 * F, 3 * C) for a in range(3)], axis=-1)
+
+    def column_tap(b, low, high):
+        return jnp.concatenate([w1v[a, 3 * b : 3 * b + 3, :, low:high].reshape(3 * C, high - low) for a in range(3)], axis=0)
+
     for b, targets in enumerate(((0, 1), (0, 3), (2, 3))):
-        taken = jnp.concatenate([s1[a : a + 6, b : b + 2].reshape(12 * F, 3 * C) for a in range(3)], axis=-1)
-        weight = jnp.concatenate([w1v[a, 3 * b : 3 * b + 3].reshape(3 * C, C) for a in range(3)], axis=0)
-        part = jnp.dot(taken, weight, preferred_element_type=F32).reshape(6, 2, F, C)
+        part = jnp.dot(columns(b), column_tap(b, 0, 256), preferred_element_type=F32).reshape(6, 2, F, 256)
         for n, col in enumerate(targets):
-            acc1[:, col] += part[:, n]
+            acc1[:, col, :, 0:256] += part[:, n]
+    for b, moves in ((0, ((0, 0, 0), (1, 0, 1), (1, 1, 0))), (1, ((0, 0, 3), (0, 1, 2), (1, 1, 3)))):
+        weight = jnp.concatenate([column_tap(b, 256, 384), column_tap(b + 1, 256, 384)], axis=-1)
+        part = jnp.dot(columns(2 * b), weight, preferred_element_type=F32).reshape(6, 2, F, 256)
+        for n, tap, col in moves:
+            acc1[:, col, :, 256:384] += part[:, n, :, tap * 128 : (tap + 1) * 128]
     s2[:, 2:8] = rows2[...]
     for h in range(6):
         inside = up if h == 0 else down if h == 5 else True
@@ -291,11 +300,18 @@
             acc2[:, 0:256] = part
         else:
             acc2[:, 0:256] += part
-    side = [w2v[a, :, :, 256:384].reshape(9 * C, 128) for a in range(3)]
-    pair = jnp.dot(window(0, R + 1), jnp.concatenate(side[:2], axis=-1), preferred_element_type=F32)
+    side = [w2v[a, :, :, 256:384].reshape(9 * C, 128) for a in range(2)]
+    pair = jnp.dot(window(0, R + 1), jnp.concatenate(side, axis=-1), preferred_element_type=F32)
+    def one(b):
+        return w2v[2, 3 * b : 3 * b + 3, :, 256:384].reshape(3 * C, 128)
+
+    wider = s2[2 : 2 + R, 0 : Q + 1].reshape(R * (Q + 1) * F, 3 * C)
+    two = jnp.dot(wider, jnp.concatenate([one(0), one(1)], axis=-1), preferred_element_type=F32)
+    two = two.reshape(R, Q + 1, F, 256)
+    last_tap = jnp.dot(s2[2 : 2 + R, 2 : 2 + Q].reshape(R * Q * F, 3 * C), one(2), preferred_element_type=F32)
     acc2[:, 256:384] = (
-        pair[: R * Q * F, :128] + pair[Q * F :, 128:]
-        + jnp.dot(window(2, R), side[2], preferred_element_type=F32)
+        pair[: R * Q * F, :128] + pair[Q * F :, 128:] + last_tap
+        + (two[:, :Q, :, :128] + two[:, 1:, :, 128:]).reshape(R * Q * F, 128)
     )
 
     for h in range(R):
@@ -328,16 +344,19 @@
     for f in range(F):
         patches = acch[pl.ds(f, 16, stride=F), :].astype(BF16)
         for g in range(8):
-            out[f, g] = patches
-
-
-def last_kernel(slots, bias, out, sums):
+            out[f, g] = patches[8 * (g % 2) : 8 * (g % 2) + 8]
+
+
+def last_kernel(mine, theirs, bias, out, sums):
     ha_count = 16
     g = lax.axis_index("wa")
+    even = g % 2 == 0
     first = [jnp.clip(2 * g - 1 + k, 0, ha_count - 1) * 8 for k in range(4)]
 
     def held(k, j, low, count):
-        return slots[first[k] + j, pl.ds(low, count)].astype(F32)
+        where = (first[k] + j, pl.ds(low % 8, count))
+        here, there = mine[where].astype(F32), theirs[where].astype(F32)
+        return jnp.where(even == (low < 8), here, there)
 
     lane = lax.broadcasted_iota(jnp.int32, (4, 128), 1)
     row = lax.broadcasted_iota(jnp.int32, (4, 128), 0)
@@ -443,7 +462,7 @@
     )(top, bot, sums1, plain, csw, vec, w1v)
     (slots,) = kernel(
         finish_kernel,
-        [shape(F, 8, 16, 128)],
+        [shape(F, 8, 8, 128)],
         [VM] * 13,
         [
             pltpu.VMEM((8, 4, F, 3 * C), BF16),
@@ -457,16 +476,18 @@
         ],
         20, "finish", 48 * cell_flops, 20 * 2**20,
     )(left, right, top, bot, sides, rows2, raw, csw, chw, vec, w1v, w2v, wy)
-    arrived = lax.all_to_all(slots.reshape(F * 8, 16, 128), ("ha", "wa"), 0, 0, tiled=True)
+    arrived = lax.all_to_all(slots.reshape(F * 8, 8, 128), ("ha", "wa"), 0, 0, tiled=True)
+    pairs = [(n, n ^ 1) for n in range(lax.axis_size("wa"))]
+    swapped = lax.ppermute(arrived, "wa", pairs)
     return pl.pallas_call(
         last_kernel,
         out_shape=shape(128, 128),
-        in_specs=[VM] * 2,
+        in_specs=[VM] * 3,
         out_specs=VM,
         scratch_shapes=[pltpu.VMEM((128, 128), F32)],
         compiler_params=pltpu.CompilerParams(vmem_limit_bytes=4 * 2**20),
         name="sum_patches",
-    )(arrived, bias)
+    )(arrived, swapped, bias)
 
 
 def solution(mesh):

time: 55.9 us -> 55.1 us (0.986)
  blocking collectives: 20 us -> 17.3 us
  waiting for transfers between devices: 1.82 us -> 2.98 us
  starting transfers between devices: 8.46 us -> 9.55 us
    all_to_all x1, blocking collectives: 20 us -> 17.3 us  [local(): lax.all_to_all(slots.reshape(F * 8, 8, 128), ('ha', 'wa'), 0, 0, tiled=True)]
    ppermute x0 -> x1, waiting for transfers between devices: none -> 1.16 us  [local(): swapped = lax.ppermute(arrived, 'wa', pairs)]
    ppermute x0 -> x1, starting transfers between devices: none -> 1.09 us  [local(): swapped = lax.ppermute(arrived, 'wa', pairs)]
  transfers between devices with their start and end apart: 4 -> 5, of which waited for: 1 -> 2; matrix products, arithmetic and copies ran while one was open for 0% -> 0% of each run, Pallas kernels for 21% -> 21%
where the time goes in v8:
time: 55.1 us; the launch traced here: 54.9 us
  Pallas kernels  25 us (45%)
  blocking collectives  17.3 us (31%)
  starting transfers between devices  9.55 us (17%)
  waiting for transfers between devices  2.98 us (5%)
    all_to_all x1, blocking collectives, local(): lax.all_to_all(slots.reshape(F * 8, 8, 128), ('ha', 'wa'), 0, 0, tiled=True)  17.3 us
    pallas_call x1, Pallas kernels, local(): kernel(finish_kernel, [shape(F, 8, 8, 128)], [VM] * 13, [pltpu.VMEM((8, 4...  10.4 us
    pallas_call x1, Pallas kernels, local(): kernel(inner_kernel, [near(R + 2, Q + 2, F, C, dtype=F32), near(3, 9, C,...  8.13 us
    ppermute x1, starting transfers between devices, local(): bot = lax.ppermute(lo, 'ha', around('ha', -1))  3.71 us
    pallas_call x1, Pallas kernels, local(): kernel(rows_kernel, [near(R + 2, 4, F, C, dtype=F32), near(R + 2, 6, F, 3...  3.66 us
    ppermute x1, starting transfers between devices, local(): left = lax.ppermute(to_right, 'wa', around('wa', 1))  2.55 us
    ppermute x1, starting transfers between devices, local(): top = lax.ppermute(hi, 'ha', around('ha', 1))  2.19 us
    pallas_call x1, Pallas kernels, local(): kernel(first_kernel, [near(32, F, C), near(3, F * R * Q, 128, dtype=F32),...  2.08 us
  transfers between devices with their start and end apart: 5, of which 2 were waited for; matrix products, arithmetic and copies ran while one was open for 0% of the time, Pallas kernels for 21%

profile of v8, /device:TPU:1, one launch (start us, length us, event | category | flops | bytes accessed | tf_op | source)
XLA Modules:
  0.0 54.9 jit_solution(6862142544909186834)
XLA Ops:
  0.0 2.1 %act_first.1 = (bf16[32,16,384]{2,1,0:T(8,128)(2,1)S(1)}, f32[3,512,128]{2,1,0:T(8,128)S(1)}, bf16[19,16,384]{2,1,0:T(8,128)(2,1)S(1)}, bf16[19,16,384]{2,1,0:T(...) custom-call(bf16[16,4,8,384]{3,2,1,0:T(8,128)(2,1)} %feat_h.1, ...), custom_call_target="tpu_custom_call" | custom-call | tf_op jit(solution)/shard_map/act_first/pallas_call | solution.py:419
  2.1 2.2 %collective-permute-start = (bf16[19,16,384]{2,1,0:T(8,128)(2,1)S(1)}, bf16[19,16,384]{2,1,0:T(8,128)(2,1)S(1)}, u32[]{:S(2)}, u32[]{:S(2)}) collective-permute-start(bf16[19,16,384]{2,1,0:T(8,128)(2,1)S(1)} %get-tuple-element.24), channel_id=1, source_target_pairs={{0,8},{8,16},{16,24},{24,32},{32,40},{40,48},{48,56},{56,64},{64,7... | collective-permute-start | bytes 700424 | tf_op jit(solution)/shard_map/ppermute | solution.py:437
  4.3 3.7 %collective-permute-start.1 = (bf16[19,16,384]{2,1,0:T(8,128)(2,1)S(1)}, bf16[19,16,384]{2,1,0:T(8,128)(2,1)S(1)}, u32[]{:S(2)}, u32[]{:S(2)}) collective-permute-start(bf16[19,16,384]{2,1,0:T(8,128)(2,1)S(1)} %get-tuple-element.25), channel_id=1, source_target_pairs={{0,120},{8,0},{16,8},{24,16},{32,24},{40,32},{48,40},{56,48},{64,5... | collective-permute-start | bytes 700424 | tf_op jit(solution)/shard_map/ppermute | solution.py:438
  8.0 8.1 %inner.1 = (f32[6,10,16,384]{3,2,1,0:T(8,128)S(1)}, bf16[3,9,384,384]{3,2,1,0:T(8,128)(2,1)S(1)}, bf16[3,9,384,384]{3,2,1,0:T(8,128)(2,1)S(1)}, bf16[4,512,1152]{2,1,0:T(8,128)(2,1)S(1)}) custom-call(bf16[32,16,384]{2,1,0:T(8,128)(2,1)S(1)} %get-tuple-element.23.own, f32[3,64,128]{2,1,0:T(8,128)S(1)} %get-tuple-element.26.cfw, ...), custom_call_target="tpu_custom_call" | custom-call | flops 4076863488 | bytes 17825792 | tf_op jit(solution)/shard_map/inner/pallas_call | solution.py:440
  16.1 0.0 collective-permute-done.top
  16.1 0.0 collective-permute-done.1.bot
  16.2 0.1 pack_columns.1
  16.3 2.6 %collective-permute-start.2 = (bf16[19,16,384]{2,1,0:T(8,128)(2,1)S(1)}, bf16[19,16,384]{2,1,0:T(8,128)(2,1)S(1)}, u32[]{:S(2)}, u32[]{:S(2)}) collective-permute-start(bf16[19,16,384]{2,1,0:T(8,128)(2,1)S(1)} %get-tuple-element.29), channel_id=1, source_target_pairs={{0,1},{1,2},{2,3},{3,4},{4,5},{5,6},{6,7},{7,0},{8,9},{9,10},{10,1... | collective-permute-start | bytes 700424 | tf_op jit(solution)/shard_map/ppermute | solution.py:454
  18.8 0.0 collective-permute-start.3
  18.8 3.7 %rows.1 = (f32[6,4,16,384]{3,2,1,0:T(8,128)S(1)}, bf16[6,6,16,1152]{3,2,1,0:T(8,128)(2,1)S(1)}, bf16[32,16,384]{2,1,0:T(8,128)(2,1)S(1)}) custom-call(bf16[19,16,384]{2,1,0:T(8,128)(2,1)S(1)} %collective-permute-done.top, bf16[19,16,384]{2,1,0:T(8,128)(2,1)S(1)} %collective-permute-done.1.bot, f32[6,10,16,384]{3,2,1,0:T(8,128)S(1)} %get-tuple-element.31.acc, ...), custom_call_target="tpu_custom_call" | custom-call | flops 2038431744 | bytes 10485760 | tf_op jit(solution)/shard_map/rows/pallas_call | solution.py:456
  22.5 0.0 collective-permute-done.2.left
  22.5 1.8 %collective-permute-done.3.right = bf16[19,16,384]{2,1,0:T(8,128)(2,1)S(1)} collective-permute-done((bf16[19,16,384]{2,1,0:T(8,128)(2,1)S(1)}, bf16[19,16,384]{2,1,0:T(8,128)(2,1)S(1)}, u32[]{:S(2)}, u32[]{:S(2)}) %collective-permute-start.3) | collective-permute-done | bytes 233504 | tf_op jit(solution)/shard_map/ppermute | solution.py:455
  24.3 10.4 %finish.1 = bf16[16,8,8,128]{3,2,1,0:T(8,128)(2,1)S(1)} custom-call(bf16[19,16,384]{2,1,0:T(8,128)(2,1)S(1)} %collective-permute-done.2.left, bf16[19,16,384]{2,1,0:T(8,128)(2,1)S(1)} %collective-permute-done.3.right, bf16[19,16,384]{2,1,0:T(8,128)(2,1)S(1)} %collective-permute-done.top, bf16[19,16,384]{2,1,0:T(8,128)(2,1)S(1)} %collective-permute-done.1.bot, ...), custom_call_target="tpu_custom_call" | custom-call | flops 6115295232 | bytes 20971520 | tf_op jit(solution)/shard_map/finish/pallas_call | solution.py:463
  34.7 17.3 %all_to_all.5.mine = bf16[128,8,128]{2,1,0:T(8,128)(2,1)S(1)} all-to-all(bf16[128,8,128]{2,1,0:T(8,128)(2,1)S(1)} %bitcast.2), channel_id=1, replica_groups=mesh['ha'=16,'wa'=8] {'ha','wa'}, dimensions={0} | all-to-all | bytes 524288 | tf_op jit(solution)/shard_map/all_to_all | solution.py:479
  51.9 1.1 %collective-permute-start.4 = (bf16[128,8,128]{2,1,0:T(8,128)(2,1)S(1)}, bf16[128,8,128]{2,1,0:T(8,128)(2,1)S(1)}, u32[]{:S(2)}, u32[]{:S(2)}) collective-permute-start(bf16[128,8,128]{2,1,0:T(8,128)(2,1)S(1)} %all_to_all.5.mine), channel_id=1, source_target_pairs={{0,1},{1,0},{2,3},{3,2},{4,5},{5,4},{6,7},{7,6},{8,9},{9,8},{10,11... | collective-permute-start | bytes 786440 | tf_op jit(solution)/shard_map/ppermute | solution.py:481
  53.0 1.2 %collective-permute-done.4.theirs = bf16[128,8,128]{2,1,0:T(8,128)(2,1)S(1)} collective-permute-done((bf16[128,8,128]{2,1,0:T(8,128)(2,1)S(1)}, bf16[128,8,128]{2,1,0:T(8,128)(2,1)S(1)}, u32[]{:S(2)}, u32[]{:S(2)}) %collective-permute-start.4) | collective-permute-done | bytes 262176 | tf_op jit(solution)/shard_map/ppermute | solution.py:481
  54.2 0.7 %sum_patches.1 = bf16[128,128]{1,0:T(8,128)(2,1)} custom-call(bf16[128,8,128]{2,1,0:T(8,128)(2,1)S(1)} %all_to_all.5.mine, bf16[128,8,128]{2,1,0:T(8,128)(2,1)S(1)} %collective-permute-done.4.theirs, f32[8,128]{1,0:T(8,128)S(1)} %get-tuple-element.40.bias), custom_call_target="tpu_custom_call" | custom-call | tf_op jit(solution)/shard_map/sum_patches/pallas_call | solution.py:482
Async XLA Ops:
  2.1 14.0 %collective-permute-start = (bf16[19,16,384]{2,1,0:T(8,128)(2,1)S(1)}, bf16[19,16,384]{2,1,0:T(8,128)(2,1)S(1)}, u32[]{:S(2)}, u32[]{:S(2)}) collective-permute-start(bf16[19,16,384]{2,1,0:T(8,128)(2,1)S(1)} %get-tuple-element.24), channel_id=1, source_target_pairs={{0,8},{8,16},{16,24},{24,32},{32,40},{40,48},{48,56},{56,64},{64,7... | collective-permute-start | bytes 700424 | tf_op jit(solution)/shard_map/ppermute | solution.py:437
  4.3 11.9 %collective-permute-start.1 = (bf16[19,16,384]{2,1,0:T(8,128)(2,1)S(1)}, bf16[19,16,384]{2,1,0:T(8,128)(2,1)S(1)}, u32[]{:S(2)}, u32[]{:S(2)}) collective-permute-start(bf16[19,16,384]{2,1,0:T(8,128)(2,1)S(1)} %get-tuple-element.25), channel_id=1, source_target_pairs={{0,120},{8,0},{16,8},{24,16},{32,24},{40,32},{48,40},{56,48},{64,5... | collective-permute-start | bytes 700424 | tf_op jit(solution)/shard_map/ppermute | solution.py:438
  16.3 6.2 %collective-permute-start.2 = (bf16[19,16,384]{2,1,0:T(8,128)(2,1)S(1)}, bf16[19,16,384]{2,1,0:T(8,128)(2,1)S(1)}, u32[]{:S(2)}, u32[]{:S(2)}) collective-permute-start(bf16[19,16,384]{2,1,0:T(8,128)(2,1)S(1)} %get-tuple-element.29), channel_id=1, source_target_pairs={{0,1},{1,2},{2,3},{3,4},{4,5},{5,6},{6,7},{7,0},{8,9},{9,10},{10,1... | collective-permute-start | bytes 700424 | tf_op jit(solution)/shard_map/ppermute | solution.py:454
  18.8 5.5 %collective-permute-start.3 = (bf16[19,16,384]{2,1,0:T(8,128)(2,1)S(1)}, bf16[19,16,384]{2,1,0:T(8,128)(2,1)S(1)}, u32[]{:S(2)}, u32[]{:S(2)}) collective-permute-start(bf16[19,16,384]{2,1,0:T(8,128)(2,1)S(1)} %get-tuple-element.30), channel_id=1, source_target_pairs={{0,7},{1,0},{2,1},{3,2},{4,3},{5,4},{6,5},{7,6},{8,15},{9,8},{10,9... | collective-permute-start | bytes 700424 | tf_op jit(solution)/shard_map/ppermute | solution.py:455
  51.9 2.3 %collective-permute-start.4 = (bf16[128,8,128]{2,1,0:T(8,128)(2,1)S(1)}, bf16[128,8,128]{2,1,0:T(8,128)(2,1)S(1)}, u32[]{:S(2)}, u32[]{:S(2)}) collective-permute-start(bf16[128,8,128]{2,1,0:T(8,128)(2,1)S(1)} %all_to_all.5.mine), channel_id=1, source_target_pairs={{0,1},{1,0},{2,3},{3,2},{4,5},{5,4},{6,7},{7,6},{8,9},{9,8},{10,11... | collective-permute-start | bytes 786440 | tf_op jit(solution)/shard_map/ppermute | solution.py:481

commit v9 on v8

--- a/solution.py
+++ b/solution.py
@@ -57,7 +57,7 @@
 
 
 def first_kernel(
-    feat_h, cf_h, cs_h, ch_h, g1_h, g2_h, gh_h, b1_h, b2_h, b3_h, own, plain, lo, hi, cfw, csw, chw, vec, bias,
+    feat_h, cf_h, cs_h, ch_h, g1_h, g2_h, gh_h, b1_h, b2_h, b3_h, own, plain, pair_a, pair_b, cfw, csw, chw, vec, bias,
     feat, caches, g1, g2, gh, b1, b2, b3, wide, sems,
 ):
     parts = [pl.ds(4 * n, 4) for n in range(4)]
@@ -66,60 +66,75 @@
         + [(cf_h, caches.at[0]), (cs_h, caches.at[1]), (ch_h, caches.at[2]),
            (g2_h, g2), (gh_h, gh), (b1_h, b1), (b2_h, b2), (b3_h, b3)], sems
     )
-    copies[0].wait()
+    even = lax.axis_index("ha") % 2 == 0
+
+    def send(k, low, high):
+        pair_a[k] = jnp.where(even, high, low).astype(BF16)
+        pair_b[k] = jnp.where(even, low, high).astype(BF16)
+
+    for n in (0, 5, 6, 7, 8, 9, 10, 11, 12):
+        copies[n].wait()
+    for n, out in enumerate((cfw, csw, chw)):
+        for h in range(R):
+            for f in range(2):
+                put_rows(out, h * 16 + f * 8, caches[n, f, h].astype(F32))
+    for n in range(2):
+        send(16 + n, rows_at(cfw, n * 16, 16, 1), rows_at(cfw, (2 + n) * 16, 16, 1))
+    send(18, rows_at(csw, 0, 16, 1), rows_at(csw, 48, 16, 1))
+    for n, value in enumerate((0.5 * line(g2), 0.5 * line(gh), line(b1), line(b2))):
+        vec[pl.ds(n, 1)] = value
+    bias[pl.ds(0, 1)] = jnp.concatenate([line(b3)] * 4, axis=-1)
     half = 0.5 * line(g1)
     for n, part in enumerate(parts):
         copies[1 + n].wait()
         x = feat[part].astype(F32).reshape(4 * R * Q, C)
         put_rows(plain, n * 4 * R * Q, x)
         put_rows(wide, n * 4 * R * Q, act(x, half))
-    for k in range(R * Q):
-        cell = rows_at(wide, k, F, R * Q).astype(BF16)
-        own[k] = cell
-        if k < 16:
-            lo[k] = cell
-        else:
-            hi[k - 16] = cell
-    for copy in copies[5:]:
-        copy.wait()
-    for n, value in enumerate((0.5 * line(g2), 0.5 * line(gh), line(b1), line(b2))):
-        vec[pl.ds(n, 1)] = value
-    bias[pl.ds(0, 1)] = jnp.concatenate([line(b3)] * 4, axis=-1)
-    for n, out in enumerate((cfw, csw, chw)):
-        for h in range(R):
-            for f in range(2):
-                put_rows(out, h * 16 + f * 8, caches[n, f, h].astype(F32))
-    for n in range(2):
-        lo[16 + n] = rows_at(cfw, n * 16, 16, 1).astype(BF16)
-        hi[16 + n] = rows_at(cfw, (2 + n) * 16, 16, 1).astype(BF16)
-    lo[18] = rows_at(csw, 0, 16, 1).astype(BF16)
-    hi[18] = rows_at(csw, 48, 16, 1).astype(BF16)
-
-
-def pack_kernel(own, top, bot, cfw, csw, after, left, right, wide_f, wide_s):
+    for k in range(16):
+        low, high = rows_at(wide, k, F, R * Q), rows_at(wide, k + 16, F, R * Q)
+        own[k] = low.astype(BF16)
+        own[k + 16] = high.astype(BF16)
+        send(k, low, high)
+
+
+def pack_kernel(own, got_a, got_b, cfw, csw, after, top, bot, pair_a, pair_b, wide_f, wide_s):
     del after
-    for n in range(2):
-        put_rows(wide_f, n * 16, top[16 + n].astype(F32))
-        put_rows(wide_f, (6 + n) * 16, bot[16 + n].astype(F32))
-    put_rows(wide_s, 0, top[18].astype(F32))
-    put_rows(wide_s, 5 * 16, bot[18].astype(F32))
+    even_h, even_w = lax.axis_index("ha") % 2 == 0, lax.axis_index("wa") % 2 == 0
+
+    def choose(first, one, other):
+        return jnp.where(first, one.astype(F32), other.astype(F32))
+
+    for k in range(MSG):
+        above, below = choose(even_h, got_b[k], got_a[k]), choose(even_h, got_a[k], got_b[k])
+        top[k], bot[k] = above.astype(BF16), below.astype(BF16)
+        if k in (16, 17):
+            put_rows(wide_f, (k - 16) * 16, above)
+            put_rows(wide_f, (k - 10) * 16, below)
+        elif k == 18:
+            put_rows(wide_s, 0, above)
+            put_rows(wide_s, 5 * 16, below)
     for n in range(3):
         wide_f[n, pl.ds(32, 64)] = cfw[n]
         wide_s[n, pl.ds(16, 64)] = csw[n]
         wide_s[n, pl.ds(96, 32)] = jnp.zeros((32, 128), F32)
-    for out, base, edge in ((left, 0, 0), (right, 6, 7)):
-        for c in range(2):
-            for h in range(8):
-                w = base + c
+
+    def send(k, left, right):
+        pair_a[k] = choose(even_w, right, left).astype(BF16)
+        pair_b[k] = choose(even_w, left, right).astype(BF16)
+
+    for c in range(2):
+        for h in range(8):
+            cells = []
+            for w in (c, 6 + c):
                 if h < 2:
-                    cell = top[h * Q + w]
+                    cells.append(top[h * Q + w])
                 elif h < 6:
-                    cell = own[(h - 2) * Q + w]
+                    cells.append(own[(h - 2) * Q + w])
                 else:
-                    cell = bot[(h - 6) * Q + w]
-                out[h * 2 + c] = cell
-            out[16 + c] = rows_at(wide_f, base + c, 16, 8).astype(BF16)
-        out[18] = rows_at(wide_s, edge, 16, 8).astype(BF16)
+                    cells.append(bot[(h - 6) * Q + w])
+            send(h * 2 + c, *cells)
+        send(16 + c, rows_at(wide_f, c, 16, 8), rows_at(wide_f, 6 + c, 16, 8))
+    send(18, rows_at(wide_s, 0, 16, 8), rows_at(wide_s, 7, 16, 8))
 
 
 def cached_row(ref, base, w0, count):
@@ -180,7 +195,8 @@
             copy.start()
     for where in empty:
         wy[where] = jnp.zeros((32, 3 * C), BF16)
-    acc[...] = jnp.zeros_like(acc)
+    for col in (0, Q + 1):
+        acc[:, col] = jnp.zeros((R + 2, F, C), F32)
 
     def cells(h, _):
         c0, c1 = cached_row(cfw, h * 16, 0, Q)
@@ -194,8 +210,13 @@
         for copy in (first[2], later, ())[a]:
             copy.start()
         part = jnp.dot(s1[...].reshape(R * Q * F, 3 * C), three(w1v, a), preferred_element_type=F32)
-        for b in range(3):
-            acc[2 - a : 2 - a + R, 2 - b : 2 - b + Q] += part[:, b * C : (b + 1) * C].reshape(R, Q, F, C)
+        part = part.reshape(R, Q, F, 3 * C)
+        fresh = R if a == 0 else 1
+        acc[2 - a : 2 - a + fresh, 1 : 1 + Q] = part[:fresh, :, :, C : 2 * C]
+        if a > 0:
+            acc[3 - a : 2 - a + R, 1 : 1 + Q] += part[1:, :, :, C : 2 * C]
+        for b in (0, 2):
+            acc[2 - a : 2 - a + R, 2 - b : 2 - b + Q] += part[:, :, :, b * C : (b + 1) * C]
     for copy in later:
         copy.wait()
 
@@ -233,19 +254,25 @@
 
 
 def finish_kernel(
-    left, right, top, bot, sides, rows2, raw, csw, chw, vec, w1v, w2v, wy, out,
+    got_a, got_b, top, bot, sides, rows2, raw, csw, chw, vec, w1v, w2v, wy, out,
     s1, acc1, s2, s3, acc2, acch, side_f, side_s,
 ):
     up, down, west, east = place()
-    for n, msg in enumerate((left, right)):
+    even = lax.axis_index("wa") % 2 == 0
+
+    def arrived(n, k):
+        one, other = got_a[k].astype(F32), got_b[k].astype(F32)
+        return jnp.where(even, other, one) if n == 0 else jnp.where(even, one, other)
+
+    for n in range(2):
         for c in range(2):
-            side_f[n, pl.ds(c * 16, 16)] = msg[16 + c].astype(F32)
-        side_s[n] = msg[18].astype(F32)
-    for n, (msg, side) in enumerate(((left, west), (right, east))):
+            side_f[n, pl.ds(c * 16, 16)] = arrived(n, 16 + c)
+        side_s[n] = arrived(n, 18)
+    for n, side in enumerate((west, east)):
         for h in range(8):
             valid = side & up if h < 2 else side & down if h >= 6 else side
             put(
-                s1, (h, pl.ds(2 * n, 2)), msg[pl.ds(h * 2, 2)].reshape(2 * F, C).astype(F32),
+                s1, (h, pl.ds(2 * n, 2)), arrived(n, pl.ds(h * 2, 2)).reshape(2 * F, C),
                 [side_f[n, pl.ds(c * 16 + h * 2, 1), :] for c in range(2)],
                 [side_f[n, pl.ds(c * 16 + h * 2 + 1, 1), :] for c in range(2)], valid,
             )
@@ -407,16 +434,17 @@
     )
 
 
-def around(axis, step):
+def neighbours(axis, first):
     count = lax.axis_size(axis)
-    return [(n, (n + step) % count) for n in range(count)]
+    pairs = [(n, (n + 1) % count) for n in range(first, count, 2)]
+    return sorted(pairs + [(b, a) for a, b in pairs])
 
 
 def local(
     features, cache_first, cache_second, cache_head, gain_first, gain_second, gain_head,
     conv_first, conv_second, conv_head, bias_first, bias_second, bias_head,
 ):
-    own, plain, lo, hi, cfw, csw, chw, vec, bias = kernel(
+    own, plain, rows_a, rows_b, cfw, csw, chw, vec, bias = kernel(
         first_kernel,
         [near(32, F, C), near(3, F * R * Q, 128, dtype=F32), near(MSG, F, C), near(MSG, F, C)]
         + [near(3, 64, 128, dtype=F32)] * 3 + [near(8, C, dtype=F32), near(8, 128, dtype=F32)],
@@ -434,8 +462,8 @@
         12, "act_first",
     )(*[far(v) for v in (features, cache_first, cache_second, cache_head, gain_first, gain_second, gain_head,
                          bias_first, bias_second, bias_head)])
-    top = lax.ppermute(hi, "ha", around("ha", 1))
-    bot = lax.ppermute(lo, "ha", around("ha", -1))
+    got_a = lax.ppermute(rows_a, "ha", neighbours("ha", 0))
+    got_b = lax.ppermute(rows_b, "ha", neighbours("ha", 1))
     cell_flops = 2 * F * 27 * C * C
     sums1, w1v, w2v, wy = kernel(
         inner_kernel,
@@ -444,15 +472,15 @@
         [pltpu.VMEM((R * Q, F, 3 * C), BF16), pltpu.SemaphoreType.DMA((7,))],
         12, "inner", 32 * cell_flops, 17 * 2**20,
     )(own, cfw, far(conv_first), far(conv_second), far(jnp.swapaxes(conv_head, 3, 4)))
-    to_left, to_right = kernel(
+    top, bot, columns_a, columns_b = kernel(
         pack_kernel,
-        [near(MSG, F, C)] * 2,
+        [near(MSG, F, C)] * 4,
         [VM] * 6,
         [pltpu.VMEM((3, 128, 128), F32)] * 2,
         4, "pack_columns",
-    )(own, top, bot, cfw, csw, wy)
-    left = lax.ppermute(to_right, "wa", around("wa", 1))
-    right = lax.ppermute(to_left, "wa", around("wa", -1))
+    )(own, got_a, got_b, cfw, csw, wy)
+    side_a = lax.ppermute(columns_a, "wa", neighbours("wa", 0))
+    side_b = lax.ppermute(columns_b, "wa", neighbours("wa", 1))
     sides, rows2, raw = kernel(
         rows_kernel,
         [near(R + 2, 4, F, C, dtype=F32), near(R + 2, 6, F, 3 * C), near(32, F, C)],
@@ -475,10 +503,9 @@
             pltpu.VMEM((2, 16, C), F32),
         ],
         20, "finish", 48 * cell_flops, 20 * 2**20,
-    )(left, right, top, bot, sides, rows2, raw, csw, chw, vec, w1v, w2v, wy)
+    )(side_a, side_b, top, bot, sides, rows2, raw, csw, chw, vec, w1v, w2v, wy)
     arrived = lax.all_to_all(slots.reshape(F * 8, 8, 128), ("ha", "wa"), 0, 0, tiled=True)
-    pairs = [(n, n ^ 1) for n in range(lax.axis_size("wa"))]
-    swapped = lax.ppermute(arrived, "wa", pairs)
+    swapped = lax.ppermute(arrived, "wa", neighbours("wa", 0))
     return pl.pallas_call(
         last_kernel,
         out_shape=shape(128, 128),

time: 55.1 us -> 55.8 us (1.013)
  waiting for transfers between devices: 2.98 us -> 1.53 us
  blocking collectives: 17.3 us -> 18.4 us
  starting transfers between devices: 9.55 us -> 10.5 us
    ppermute x5, waiting for transfers between devices: 2.98 us -> 1.53 us  [the longest x1 1.16 us: local(): swapped = lax.ppermute(arrived, 'wa', neighbours('wa', 0))]
    all_to_all x1, blocking collectives: 17.3 us -> 18.4 us  [local(): lax.all_to_all(slots.reshape(F * 8, 8, 128), ('ha', 'wa'), 0, 0, tiled=True)]
    ppermute x5, starting transfers between devices: 9.55 us -> 10.5 us  [the longest x1 4.1 us: local(): got_b = lax.ppermute(rows_b, 'ha', neighbours('ha', 1))]
where the time goes in v9:
time: 55.8 us; the launch traced here: 55.7 us
  Pallas kernels  25.2 us (45%)
  blocking collectives  18.4 us (33%)
  starting transfers between devices  10.5 us (19%)
  waiting for transfers between devices  1.53 us (3%)
    all_to_all x1, blocking collectives, local(): lax.all_to_all(slots.reshape(F * 8, 8, 128), ('ha', 'wa'), 0, 0, tiled=True)  18.4 us
    pallas_call x1, Pallas kernels, local(): kernel(finish_kernel, [shape(F, 8, 8, 128)], [VM] * 13, [pltpu.VMEM((8, 4...  10.3 us
    pallas_call x1, Pallas kernels, local(): kernel(inner_kernel, [near(R + 2, Q + 2, F, C, dtype=F32), near(3, 9, C,...  8.09 us
    ppermute x1, starting transfers between devices, local(): got_b = lax.ppermute(rows_b, 'ha', neighbours('ha', 1))  4.1 us
    pallas_call x1, Pallas kernels, local(): kernel(rows_kernel, [near(R + 2, 4, F, C, dtype=F32), near(R + 2, 6, F, 3...  3.67 us
    pallas_call x1, Pallas kernels, local(): kernel(first_kernel, [near(32, F, C), near(3, F * R * Q, 128, dtype=F32),...  2.21 us
    ppermute x1, starting transfers between devices, local(): got_a = lax.ppermute(rows_a, 'ha', neighbours('ha', 0))  2.21 us
    ppermute x1, starting transfers between devices, local(): side_b = lax.ppermute(columns_b, 'wa', neighbours('wa', 1))  1.79 us
  transfers between devices with their start and end apart: 5, of which 2 were waited for; matrix products, arithmetic and copies ran while one was open for 0% of the time, Pallas kernels for 21%

profile of v9, /device:TPU:1, one launch (start us, length us, event | category | flops | bytes accessed | tf_op | source)
XLA Modules:
  0.0 55.7 jit_solution(4216051049071460779)
XLA Ops:
  0.0 2.2 %act_first.1 = (bf16[32,16,384]{2,1,0:T(8,128)(2,1)S(1)}, f32[3,512,128]{2,1,0:T(8,128)S(1)}, bf16[19,16,384]{2,1,0:T(8,128)(2,1)S(1)}, bf16[19,16,384]{2,1,0:T(...) custom-call(bf16[16,4,8,384]{3,2,1,0:T(8,128)(2,1)} %feat_h.1, ...), custom_call_target="tpu_custom_call" | custom-call | tf_op jit(solution)/shard_map/act_first/pallas_call | solution.py:447
  2.2 2.2 %collective-permute-start = (bf16[19,16,384]{2,1,0:T(8,128)(2,1)S(1)}, bf16[19,16,384]{2,1,0:T(8,128)(2,1)S(1)}, u32[]{:S(2)}, u32[]{:S(2)}) collective-permute-start(bf16[19,16,384]{2,1,0:T(8,128)(2,1)S(1)} %get-tuple-element.26), channel_id=1, source_target_pairs={{0,8},{8,0},{16,24},{24,16},{32,40},{40,32},{48,56},{56,48},{64,72... | collective-permute-start | bytes 700424 | tf_op jit(solution)/shard_map/ppermute | solution.py:465
  4.4 4.1 %collective-permute-start.1 = (bf16[19,16,384]{2,1,0:T(8,128)(2,1)S(1)}, bf16[19,16,384]{2,1,0:T(8,128)(2,1)S(1)}, u32[]{:S(2)}, u32[]{:S(2)}) collective-permute-start(bf16[19,16,384]{2,1,0:T(8,128)(2,1)S(1)} %get-tuple-element.27), channel_id=1, source_target_pairs={{0,120},{8,16},{16,8},{24,32},{32,24},{40,48},{48,40},{56,64},{64,... | collective-permute-start | bytes 700424 | tf_op jit(solution)/shard_map/ppermute | solution.py:466
  8.5 8.1 %inner.1 = (f32[6,10,16,384]{3,2,1,0:T(8,128)S(1)}, bf16[3,9,384,384]{3,2,1,0:T(8,128)(2,1)S(1)}, bf16[3,9,384,384]{3,2,1,0:T(8,128)(2,1)S(1)}, bf16[4,512,1152]{2,1,0:T(8,128)(2,1)S(1)}) custom-call(bf16[32,16,384]{2,1,0:T(8,128)(2,1)S(1)} %get-tuple-element.25.own, f32[3,64,128]{2,1,0:T(8,128)S(1)} %get-tuple-element.28.cfw, ...), custom_call_target="tpu_custom_call" | custom-call | flops 4076863488 | bytes 17825792 | tf_op jit(solution)/shard_map/inner/pallas_call | solution.py:468
  16.6 0.0 collective-permute-done.got_a
  16.6 0.0 collective-permute-done.1.got_b
  16.6 0.2 pack_columns.1
  16.9 1.3 %collective-permute-start.2 = (bf16[19,16,384]{2,1,0:T(8,128)(2,1)S(1)}, bf16[19,16,384]{2,1,0:T(8,128)(2,1)S(1)}, u32[]{:S(2)}, u32[]{:S(2)}) collective-permute-start(bf16[19,16,384]{2,1,0:T(8,128)(2,1)S(1)} %get-tuple-element.31), channel_id=1, source_target_pairs={{0,1},{1,0},{2,3},{3,2},{4,5},{5,4},{6,7},{7,6},{8,9},{9,8},{10,11... | collective-permute-start | bytes 700424 | tf_op jit(solution)/shard_map/ppermute | solution.py:482
  18.2 1.8 %collective-permute-start.3 = (bf16[19,16,384]{2,1,0:T(8,128)(2,1)S(1)}, bf16[19,16,384]{2,1,0:T(8,128)(2,1)S(1)}, u32[]{:S(2)}, u32[]{:S(2)}) collective-permute-start(bf16[19,16,384]{2,1,0:T(8,128)(2,1)S(1)} %get-tuple-element.32), channel_id=1, source_target_pairs={{0,7},{1,2},{2,1},{3,4},{4,3},{5,6},{6,5},{7,0},{8,15},{9,10},{10,... | collective-permute-start | bytes 700424 | tf_op jit(solution)/shard_map/ppermute | solution.py:483
  20.0 3.7 %rows.1 = (f32[6,4,16,384]{3,2,1,0:T(8,128)S(1)}, bf16[6,6,16,1152]{3,2,1,0:T(8,128)(2,1)S(1)}, bf16[32,16,384]{2,1,0:T(8,128)(2,1)S(1)}) custom-call(bf16[19,16,384]{2,1,0:T(8,128)(2,1)S(1)} %get-tuple-element.33.top, bf16[19,16,384]{2,1,0:T(8,128)(2,1)S(1)} %get-tuple-element.34.bot, f32[6,10,16,384]{3,2,1,0:T(8,128)S(1)} %get-tuple-element.35.acc, ...), custom_call_target="tpu_custom_call" | custom-call | flops 2038431744 | bytes 10485760 | tf_op jit(solution)/shard_map/rows/pallas_call | solution.py:484
  23.6 0.0 collective-permute-done.2.got_a
  23.6 0.4 collective-permute-done.3.got_b
  24.0 10.3 %finish.1 = bf16[16,8,8,128]{3,2,1,0:T(8,128)(2,1)S(1)} custom-call(bf16[19,16,384]{2,1,0:T(8,128)(2,1)S(1)} %collective-permute-done.2.got_a, bf16[19,16,384]{2,1,0:T(8,128)(2,1)S(1)} %collective-permute-done.3.got_b, bf16[19,16,384]{2,1,0:T(8,128)(2,1)S(1)} %get-tuple-element.33.top, bf16[19,16,384]{2,1,0:T(8,128)(2,1)S(1)} %get-tuple-element.34.bot, ...), custom_call_target="tpu_custom_call" | custom-call | flops 6115295232 | bytes 20971520 | tf_op jit(solution)/shard_map/finish/pallas_call | solution.py:491
  34.3 18.4 %all_to_all.5.mine = bf16[128,8,128]{2,1,0:T(8,128)(2,1)S(1)} all-to-all(bf16[128,8,128]{2,1,0:T(8,128)(2,1)S(1)} %bitcast.2), channel_id=1, replica_groups=mesh['ha'=16,'wa'=8] {'ha','wa'}, dimensions={0} | all-to-all | bytes 524288 | tf_op jit(solution)/shard_map/all_to_all | solution.py:507
  52.7 1.1 %collective-permute-start.4 = (bf16[128,8,128]{2,1,0:T(8,128)(2,1)S(1)}, bf16[128,8,128]{2,1,0:T(8,128)(2,1)S(1)}, u32[]{:S(2)}, u32[]{:S(2)}) collective-permute-start(bf16[128,8,128]{2,1,0:T(8,128)(2,1)S(1)} %all_to_all.5.mine), channel_id=1, source_target_pairs={{0,1},{1,0},{2,3},{3,2},{4,5},{5,4},{6,7},{7,6},{8,9},{9,8},{10,11... | collective-permute-start | bytes 786440 | tf_op jit(solution)/shard_map/ppermute | solution.py:508
  53.8 1.2 %collective-permute-done.4.theirs = bf16[128,8,128]{2,1,0:T(8,128)(2,1)S(1)} collective-permute-done((bf16[128,8,128]{2,1,0:T(8,128)(2,1)S(1)}, bf16[128,8,128]{2,1,0:T(8,128)(2,1)S(1)}, u32[]{:S(2)}, u32[]{:S(2)}) %collective-permute-start.4) | collective-permute-done | bytes 262176 | tf_op jit(solution)/shard_map/ppermute | solution.py:508
  54.9 0.7 %sum_patches.1 = bf16[128,128]{1,0:T(8,128)(2,1)} custom-call(bf16[128,8,128]{2,1,0:T(8,128)(2,1)S(1)} %all_to_all.5.mine, bf16[128,8,128]{2,1,0:T(8,128)(2,1)S(1)} %collective-permute-done.4.theirs, f32[8,128]{1,0:T(8,128)S(1)} %get-tuple-element.44.bias), custom_call_target="tpu_custom_call" | custom-call | tf_op jit(solution)/shard_map/sum_patches/pallas_call | solution.py:509
Async XLA Ops:
  2.2 14.4 %collective-permute-start = (bf16[19,16,384]{2,1,0:T(8,128)(2,1)S(1)}, bf16[19,16,384]{2,1,0:T(8,128)(2,1)S(1)}, u32[]{:S(2)}, u32[]{:S(2)}) collective-permute-start(bf16[19,16,384]{2,1,0:T(8,128)(2,1)S(1)} %get-tuple-element.26), channel_id=1, source_target_pairs={{0,8},{8,0},{16,24},{24,16},{32,40},{40,32},{48,56},{56,48},{64,72... | collective-permute-start | bytes 700424 | tf_op jit(solution)/shard_map/ppermute | solution.py:465
  4.4 12.2 %collective-permute-start.1 = (bf16[19,16,384]{2,1,0:T(8,128)(2,1)S(1)}, bf16[19,16,384]{2,1,0:T(8,128)(2,1)S(1)}, u32[]{:S(2)}, u32[]{:S(2)}) collective-permute-start(bf16[19,16,384]{2,1,0:T(8,128)(2,1)S(1)} %get-tuple-element.27), channel_id=1, source_target_pairs={{0,120},{8,16},{16,8},{24,32},{32,24},{40,48},{48,40},{56,64},{64,... | collective-permute-start | bytes 700424 | tf_op jit(solution)/shard_map/ppermute | solution.py:466
  16.9 6.8 %collective-permute-start.2 = (bf16[19,16,384]{2,1,0:T(8,128)(2,1)S(1)}, bf16[19,16,384]{2,1,0:T(8,128)(2,1)S(1)}, u32[]{:S(2)}, u32[]{:S(2)}) collective-permute-start(bf16[19,16,384]{2,1,0:T(8,128)(2,1)S(1)} %get-tuple-element.31), channel_id=1, source_target_pairs={{0,1},{1,0},{2,3},{3,2},{4,5},{5,4},{6,7},{7,6},{8,9},{9,8},{10,11... | collective-permute-start | bytes 700424 | tf_op jit(solution)/shard_map/ppermute | solution.py:482
  18.2 5.8 %collective-permute-start.3 = (bf16[19,16,384]{2,1,0:T(8,128)(2,1)S(1)}, bf16[19,16,384]{2,1,0:T(8,128)(2,1)S(1)}, u32[]{:S(2)}, u32[]{:S(2)}) collective-permute-start(bf16[19,16,384]{2,1,0:T(8,128)(2,1)S(1)} %get-tuple-element.32), channel_id=1, source_target_pairs={{0,7},{1,2},{2,1},{3,4},{4,3},{5,6},{6,5},{7,0},{8,15},{9,10},{10,... | collective-permute-start | bytes 700424 | tf_op jit(solution)/shard_map/ppermute | solution.py:483
  52.7 2.3 %collective-permute-start.4 = (bf16[128,8,128]{2,1,0:T(8,128)(2,1)S(1)}, bf16[128,8,128]{2,1,0:T(8,128)(2,1)S(1)}, u32[]{:S(2)}, u32[]{:S(2)}) collective-permute-start(bf16[128,8,128]{2,1,0:T(8,128)(2,1)S(1)} %all_to_all.5.mine), channel_id=1, source_target_pairs={{0,1},{1,0},{2,3},{3,2},{4,5},{5,4},{6,7},{7,6},{8,9},{9,8},{10,11... | collective-permute-start | bytes 786440 | tf_op jit(solution)/shard_map/ppermute | solution.py:508

commit v10 on v8

--- a/solution.py
+++ b/solution.py
@@ -9,6 +9,7 @@
 F32 = jnp.float32
 F, R, Q, C = 16, 4, 8, 384
 MSG = 19
+PITCH = 40
 VM = pl.BlockSpec(memory_space=pltpu.VMEM)
 ANY = pl.BlockSpec(memory_space=pl.ANY)
 
@@ -71,10 +72,12 @@
     for n, part in enumerate(parts):
         copies[1 + n].wait()
         x = feat[part].astype(F32).reshape(4 * R * Q, C)
-        put_rows(plain, n * 4 * R * Q, x)
-        put_rows(wide, n * 4 * R * Q, act(x, half))
+        y = act(x, half)
+        for m in range(4):
+            put_rows(plain, (n * 4 + m) * PITCH, x[m * R * Q : (m + 1) * R * Q])
+            put_rows(wide, (n * 4 + m) * PITCH, y[m * R * Q : (m + 1) * R * Q])
     for k in range(R * Q):
-        cell = rows_at(wide, k, F, R * Q).astype(BF16)
+        cell = rows_at(wide, k, F, PITCH).astype(BF16)
         own[k] = cell
         if k < 16:
             lo[k] = cell
@@ -225,7 +228,7 @@
         total = acc[n, 2:8] if 2 <= n < 4 else add[n if n < 2 else n - 2, 2:8]
         hidden(s2, (n, pl.ds(0, 6)), total.reshape(6 * F, C), vec, cached, valid)
     for k in range(R * Q):
-        raw[k] = rows_at(plain, k, F, R * Q).astype(BF16)
+        raw[k] = rows_at(plain, k, F, PITCH).astype(BF16)
     for n, col in enumerate((0, 8)):
         sides[0:2, 2 * n : 2 * n + 2] = add[0:2, col : col + 2]
         sides[2:4, 2 * n : 2 * n + 2] = acc[2:4, col : col + 2]
@@ -291,38 +294,47 @@
                 olds.append(two if n == 0 else two[::-1])
             put(s2, (h, pl.ds(8 * n, 2)), now, olds[0], olds[1], None if inside is True else inside)
 
-    def window(a, rows):
-        return jnp.concatenate([s2[a : a + rows, b : b + Q].reshape(rows * Q * F, 3 * C) for b in range(3)], axis=-1)
-
-    for a in range(3):
-        part = jnp.dot(window(a, R), w2v[a, :, :, 0:256].reshape(9 * C, 256), preferred_element_type=F32)
-        if a == 0:
-            acc2[:, 0:256] = part
-        else:
-            acc2[:, 0:256] += part
-    side = [w2v[a, :, :, 256:384].reshape(9 * C, 128) for a in range(2)]
-    pair = jnp.dot(window(0, R + 1), jnp.concatenate(side, axis=-1), preferred_element_type=F32)
+    def window(row, rows):
+        return jnp.concatenate(
+            [s2[row : row + rows, b : b + Q].reshape(rows * Q * F, 3 * C) for b in range(3)], axis=-1
+        )
+
     def one(b):
         return w2v[2, 3 * b : 3 * b + 3, :, 256:384].reshape(3 * C, 128)
 
-    wider = s2[2 : 2 + R, 0 : Q + 1].reshape(R * (Q + 1) * F, 3 * C)
-    two = jnp.dot(wider, jnp.concatenate([one(0), one(1)], axis=-1), preferred_element_type=F32)
-    two = two.reshape(R, Q + 1, F, 256)
-    last_tap = jnp.dot(s2[2 : 2 + R, 2 : 2 + Q].reshape(R * Q * F, 3 * C), one(2), preferred_element_type=F32)
-    acc2[:, 256:384] = (
-        pair[: R * Q * F, :128] + pair[Q * F :, 128:] + last_tap
-        + (two[:, :Q, :, :128] + two[:, 1:, :, 128:]).reshape(R * Q * F, 128)
-    )
-
-    for h in range(R):
-        wide = acc2[pl.ds(h * Q * F, Q * F)] + vec[pl.ds(3, 1), :]
-        wide = wide + raw[pl.ds(h * Q, Q)].reshape(Q * F, C).astype(F32)
-        c0, c1 = cached_row(chw, h * 16, 0, Q)
-        now = act(wide.astype(BF16).astype(F32), vec[pl.ds(1, 1), :])
-        for n, part in enumerate(stack(now, c0, c1)):
-            part = part.reshape(Q, F, C)
-            for w in range(Q):
-                s3[h % 2 * 2 + w % 2, h // 2 * 4 + w // 2, :, pl.ds(n * C, C)] = part[w]
+    half = R // 2
+    size = half * Q * F
+    side = [w2v[a, :, :, 256:384].reshape(9 * C, 128) for a in range(2)]
+    for top_row in range(0, R, half):
+        rows = pl.ds(top_row * Q * F, size)
+        for a in range(3):
+            part = jnp.dot(
+                window(top_row + a, half), w2v[a, :, :, 0:256].reshape(9 * C, 256), preferred_element_type=F32
+            )
+            if a == 0:
+                acc2[rows, 0:256] = part
+            else:
+                acc2[rows, 0:256] += part
+        pair = jnp.dot(window(top_row, half + 1), jnp.concatenate(side, axis=-1), preferred_element_type=F32)
+        wider = s2[top_row + 2 : top_row + 2 + half, 0 : Q + 1].reshape(half * (Q + 1) * F, 3 * C)
+        two = jnp.dot(wider, jnp.concatenate([one(0), one(1)], axis=-1), preferred_element_type=F32)
+        two = two.reshape(half, Q + 1, F, 256)
+        last_tap = jnp.dot(
+            s2[top_row + 2 : top_row + 2 + half, 2 : 2 + Q].reshape(size, 3 * C), one(2), preferred_element_type=F32
+        )
+        acc2[rows, 256:384] = (
+            pair[:size, :128] + pair[Q * F :, 128:] + last_tap
+            + (two[:, :Q, :, :128] + two[:, 1:, :, 128:]).reshape(size, 128)
+        )
+        for h in range(top_row, top_row + half):
+            wide = acc2[pl.ds(h * Q * F, Q * F)] + vec[pl.ds(3, 1), :]
+            wide = wide + raw[pl.ds(h * Q, Q)].reshape(Q * F, C).astype(F32)
+            c0, c1 = cached_row(chw, h * 16, 0, Q)
+            now = act(wide.astype(BF16).astype(F32), vec[pl.ds(1, 1), :])
+            for n, part in enumerate(stack(now, c0, c1)):
+                part = part.reshape(Q, F, C)
+                for w in range(Q):
+                    s3[h % 2 * 2 + w % 2, h // 2 * 4 + w // 2, :, pl.ds(n * C, C)] = part[w]
     sums = {}
     for rh in range(2):
         for rw in range(2):
@@ -418,7 +430,7 @@
 ):
     own, plain, lo, hi, cfw, csw, chw, vec, bias = kernel(
         first_kernel,
-        [near(32, F, C), near(3, F * R * Q, 128, dtype=F32), near(MSG, F, C), near(MSG, F, C)]
+        [near(32, F, C), near(3, F * PITCH, 128, dtype=F32), near(MSG, F, C), near(MSG, F, C)]
         + [near(3, 64, 128, dtype=F32)] * 3 + [near(8, C, dtype=F32), near(8, 128, dtype=F32)],
         [ANY] * 10,
         [
@@ -428,7 +440,7 @@
         + [pltpu.VMEM((C,), F32)] * 5
         + [
             pltpu.VMEM((32,), F32),
-            pltpu.VMEM((3, F * R * Q, 128), F32),
+            pltpu.VMEM((3, F * PITCH, 128), F32),
             pltpu.SemaphoreType.DMA((13,)),
         ],
         12, "act_first",

time: 55.1 us -> 54.3 us (0.985)
  Pallas kernels: 25 us -> 24 us
where the time goes in v10:
time: 54.3 us; the launch traced here: 54.2 us
  Pallas kernels  24 us (44%)
  blocking collectives  17.3 us (32%)
  starting transfers between devices  9.55 us (18%)
  waiting for transfers between devices  3.29 us (6%)
    all_to_all x1, blocking collectives, local(): lax.all_to_all(slots.reshape(F * 8, 8, 128), ('ha', 'wa'), 0, 0, tiled=True)  17.3 us
    pallas_call x1, Pallas kernels, local(): kernel(finish_kernel, [shape(F, 8, 8, 128)], [VM] * 13, [pltpu.VMEM((8, 4...  9.92 us
    pallas_call x1, Pallas kernels, local(): kernel(inner_kernel, [near(R + 2, Q + 2, F, C, dtype=F32), near(3, 9, C,...  8.13 us
    ppermute x1, starting transfers between devices, local(): bot = lax.ppermute(lo, 'ha', around('ha', -1))  3.71 us
    pallas_call x1, Pallas kernels, local(): kernel(rows_kernel, [near(R + 2, 4, F, C, dtype=F32), near(R + 2, 6, F, 3...  3.35 us
    ppermute x1, starting transfers between devices, local(): left = lax.ppermute(to_right, 'wa', around('wa', 1))  2.54 us
    ppermute x1, starting transfers between devices, local(): top = lax.ppermute(hi, 'ha', around('ha', 1))  2.19 us
    ppermute x1, waiting for transfers between devices, local(): right = lax.ppermute(to_left, 'wa', around('wa', -1))  2.12 us
  transfers between devices with their start and end apart: 5, of which 2 were waited for; matrix products, arithmetic and copies ran while one was open for 0% of the time, Pallas kernels for 21%

profile of v10, /device:TPU:1, one launch (start us, length us, event | category | flops | bytes accessed | tf_op | source)
XLA Modules:
  0.0 54.2 jit_solution(17120360952789674176)
XLA Ops:
  0.0 1.8 %act_first.1 = (bf16[32,16,384]{2,1,0:T(8,128)(2,1)S(1)}, f32[3,640,128]{2,1,0:T(8,128)S(1)}, bf16[19,16,384]{2,1,0:T(8,128)(2,1)S(1)}, bf16[19,16,384]{2,1,0:T(...) custom-call(bf16[16,4,8,384]{3,2,1,0:T(8,128)(2,1)} %feat_h.1, ...), custom_call_target="tpu_custom_call" | custom-call | tf_op jit(solution)/shard_map/act_first/pallas_call | solution.py:431
  1.8 2.2 %collective-permute-start = (bf16[19,16,384]{2,1,0:T(8,128)(2,1)S(1)}, bf16[19,16,384]{2,1,0:T(8,128)(2,1)S(1)}, u32[]{:S(2)}, u32[]{:S(2)}) collective-permute-start(bf16[19,16,384]{2,1,0:T(8,128)(2,1)S(1)} %get-tuple-element.24), channel_id=1, source_target_pairs={{0,8},{8,16},{16,24},{24,32},{32,40},{40,48},{48,56},{56,64},{64,7... | collective-permute-start | bytes 700424 | tf_op jit(solution)/shard_map/ppermute | solution.py:449
  4.0 3.7 %collective-permute-start.1 = (bf16[19,16,384]{2,1,0:T(8,128)(2,1)S(1)}, bf16[19,16,384]{2,1,0:T(8,128)(2,1)S(1)}, u32[]{:S(2)}, u32[]{:S(2)}) collective-permute-start(bf16[19,16,384]{2,1,0:T(8,128)(2,1)S(1)} %get-tuple-element.25), channel_id=1, source_target_pairs={{0,120},{8,0},{16,8},{24,16},{32,24},{40,32},{48,40},{56,48},{64,5... | collective-permute-start | bytes 700424 | tf_op jit(solution)/shard_map/ppermute | solution.py:450
  7.7 8.1 %inner.1 = (f32[6,10,16,384]{3,2,1,0:T(8,128)S(1)}, bf16[3,9,384,384]{3,2,1,0:T(8,128)(2,1)S(1)}, bf16[3,9,384,384]{3,2,1,0:T(8,128)(2,1)S(1)}, bf16[4,512,1152]{2,1,0:T(8,128)(2,1)S(1)}) custom-call(bf16[32,16,384]{2,1,0:T(8,128)(2,1)S(1)} %get-tuple-element.23.own, f32[3,64,128]{2,1,0:T(8,128)S(1)} %get-tuple-element.26.cfw, ...), custom_call_target="tpu_custom_call" | custom-call | flops 4076863488 | bytes 17825792 | tf_op jit(solution)/shard_map/inner/pallas_call | solution.py:452
  15.8 0.0 collective-permute-done.top
  15.9 0.0 collective-permute-done.1.bot
  15.9 0.1 pack_columns.1
  16.0 2.5 %collective-permute-start.2 = (bf16[19,16,384]{2,1,0:T(8,128)(2,1)S(1)}, bf16[19,16,384]{2,1,0:T(8,128)(2,1)S(1)}, u32[]{:S(2)}, u32[]{:S(2)}) collective-permute-start(bf16[19,16,384]{2,1,0:T(8,128)(2,1)S(1)} %get-tuple-element.29), channel_id=1, source_target_pairs={{0,1},{1,2},{2,3},{3,4},{4,5},{5,6},{6,7},{7,0},{8,9},{9,10},{10,1... | collective-permute-start | bytes 700424 | tf_op jit(solution)/shard_map/ppermute | solution.py:466
  18.5 0.0 collective-permute-start.3
  18.5 3.3 %rows.1 = (f32[6,4,16,384]{3,2,1,0:T(8,128)S(1)}, bf16[6,6,16,1152]{3,2,1,0:T(8,128)(2,1)S(1)}, bf16[32,16,384]{2,1,0:T(8,128)(2,1)S(1)}) custom-call(bf16[19,16,384]{2,1,0:T(8,128)(2,1)S(1)} %collective-permute-done.top, bf16[19,16,384]{2,1,0:T(8,128)(2,1)S(1)} %collective-permute-done.1.bot, f32[6,10,16,384]{3,2,1,0:T(8,128)S(1)} %get-tuple-element.31.acc, ...), custom_call_target="tpu_custom_call" | custom-call | flops 2038431744 | bytes 10485760 | tf_op jit(solution)/shard_map/rows/pallas_call | solution.py:468
  21.9 0.0 collective-permute-done.2.left
  21.9 2.1 %collective-permute-done.3.right = bf16[19,16,384]{2,1,0:T(8,128)(2,1)S(1)} collective-permute-done((bf16[19,16,384]{2,1,0:T(8,128)(2,1)S(1)}, bf16[19,16,384]{2,1,0:T(8,128)(2,1)S(1)}, u32[]{:S(2)}, u32[]{:S(2)}) %collective-permute-start.3) | collective-permute-done | bytes 233504 | tf_op jit(solution)/shard_map/ppermute | solution.py:467
  24.0 9.9 %finish.1 = bf16[16,8,8,128]{3,2,1,0:T(8,128)(2,1)S(1)} custom-call(bf16[19,16,384]{2,1,0:T(8,128)(2,1)S(1)} %collective-permute-done.2.left, bf16[19,16,384]{2,1,0:T(8,128)(2,1)S(1)} %collective-permute-done.3.right, bf16[19,16,384]{2,1,0:T(8,128)(2,1)S(1)} %collective-permute-done.top, bf16[19,16,384]{2,1,0:T(8,128)(2,1)S(1)} %collective-permute-done.1.bot, ...), custom_call_target="tpu_custom_call" | custom-call | flops 6115295232 | bytes 20971520 | tf_op jit(solution)/shard_map/finish/pallas_call | solution.py:475
  33.9 17.3 %all_to_all.5.mine = bf16[128,8,128]{2,1,0:T(8,128)(2,1)S(1)} all-to-all(bf16[128,8,128]{2,1,0:T(8,128)(2,1)S(1)} %bitcast.2), channel_id=1, replica_groups=mesh['ha'=16,'wa'=8] {'ha','wa'}, dimensions={0} | all-to-all | bytes 524288 | tf_op jit(solution)/shard_map/all_to_all | solution.py:491
  51.2 1.1 %collective-permute-start.4 = (bf16[128,8,128]{2,1,0:T(8,128)(2,1)S(1)}, bf16[128,8,128]{2,1,0:T(8,128)(2,1)S(1)}, u32[]{:S(2)}, u32[]{:S(2)}) collective-permute-start(bf16[128,8,128]{2,1,0:T(8,128)(2,1)S(1)} %all_to_all.5.mine), channel_id=1, source_target_pairs={{0,1},{1,0},{2,3},{3,2},{4,5},{5,4},{6,7},{7,6},{8,9},{9,8},{10,11... | collective-permute-start | bytes 786440 | tf_op jit(solution)/shard_map/ppermute | solution.py:493
  52.3 1.2 %collective-permute-done.4.theirs = bf16[128,8,128]{2,1,0:T(8,128)(2,1)S(1)} collective-permute-done((bf16[128,8,128]{2,1,0:T(8,128)(2,1)S(1)}, bf16[128,8,128]{2,1,0:T(8,128)(2,1)S(1)}, u32[]{:S(2)}, u32[]{:S(2)}) %collective-permute-start.4) | collective-permute-done | bytes 262176 | tf_op jit(solution)/shard_map/ppermute | solution.py:493
  53.4 0.7 %sum_patches.1 = bf16[128,128]{1,0:T(8,128)(2,1)} custom-call(bf16[128,8,128]{2,1,0:T(8,128)(2,1)S(1)} %all_to_all.5.mine, bf16[128,8,128]{2,1,0:T(8,128)(2,1)S(1)} %collective-permute-done.4.theirs, f32[8,128]{1,0:T(8,128)S(1)} %get-tuple-element.40.bias), custom_call_target="tpu_custom_call" | custom-call | tf_op jit(solution)/shard_map/sum_patches/pallas_call | solution.py:494
Async XLA Ops:
  1.8 14.1 %collective-permute-start = (bf16[19,16,384]{2,1,0:T(8,128)(2,1)S(1)}, bf16[19,16,384]{2,1,0:T(8,128)(2,1)S(1)}, u32[]{:S(2)}, u32[]{:S(2)}) collective-permute-start(bf16[19,16,384]{2,1,0:T(8,128)(2,1)S(1)} %get-tuple-element.24), channel_id=1, source_target_pairs={{0,8},{8,16},{16,24},{24,32},{32,40},{40,48},{48,56},{56,64},{64,7... | collective-permute-start | bytes 700424 | tf_op jit(solution)/shard_map/ppermute | solution.py:449
  4.0 11.9 %collective-permute-start.1 = (bf16[19,16,384]{2,1,0:T(8,128)(2,1)S(1)}, bf16[19,16,384]{2,1,0:T(8,128)(2,1)S(1)}, u32[]{:S(2)}, u32[]{:S(2)}) collective-permute-start(bf16[19,16,384]{2,1,0:T(8,128)(2,1)S(1)} %get-tuple-element.25), channel_id=1, source_target_pairs={{0,120},{8,0},{16,8},{24,16},{32,24},{40,32},{48,40},{56,48},{64,5... | collective-permute-start | bytes 700424 | tf_op jit(solution)/shard_map/ppermute | solution.py:450
  16.0 5.9 %collective-permute-start.2 = (bf16[19,16,384]{2,1,0:T(8,128)(2,1)S(1)}, bf16[19,16,384]{2,1,0:T(8,128)(2,1)S(1)}, u32[]{:S(2)}, u32[]{:S(2)}) collective-permute-start(bf16[19,16,384]{2,1,0:T(8,128)(2,1)S(1)} %get-tuple-element.29), channel_id=1, source_target_pairs={{0,1},{1,2},{2,3},{3,4},{4,5},{5,6},{6,7},{7,0},{8,9},{9,10},{10,1... | collective-permute-start | bytes 700424 | tf_op jit(solution)/shard_map/ppermute | solution.py:466
  18.5 5.5 %collective-permute-start.3 = (bf16[19,16,384]{2,1,0:T(8,128)(2,1)S(1)}, bf16[19,16,384]{2,1,0:T(8,128)(2,1)S(1)}, u32[]{:S(2)}, u32[]{:S(2)}) collective-permute-start(bf16[19,16,384]{2,1,0:T(8,128)(2,1)S(1)} %get-tuple-element.30), channel_id=1, source_target_pairs={{0,7},{1,0},{2,1},{3,2},{4,3},{5,4},{6,5},{7,6},{8,15},{9,8},{10,9... | collective-permute-start | bytes 700424 | tf_op jit(solution)/shard_map/ppermute | solution.py:467
  51.2 2.3 %collective-permute-start.4 = (bf16[128,8,128]{2,1,0:T(8,128)(2,1)S(1)}, bf16[128,8,128]{2,1,0:T(8,128)(2,1)S(1)}, u32[]{:S(2)}, u32[]{:S(2)}) collective-permute-start(bf16[128,8,128]{2,1,0:T(8,128)(2,1)S(1)} %all_to_all.5.mine), channel_id=1, source_target_pairs={{0,1},{1,0},{2,3},{3,2},{4,5},{5,4},{6,7},{7,6},{8,9},{9,8},{10,11... | collective-permute-start | bytes 786440 | tf_op jit(solution)/shard_map/ppermute | solution.py:493

commit v11 on v10

--- a/solution.py
+++ b/solution.py
@@ -155,7 +155,7 @@
     ]
 
 
-def inner_kernel(own, cfw, w1, w2, wh, acc, w1v, w2v, wy, s1, sems):
+def inner_kernel(own, cfw, w1, w2, wh, acc, w1v, w2v, flat, s1, sems):
     def group(src, dst, a, sem):
         return [
             pltpu.make_async_copy(src.at[t, a, b], dst.at[a, b * 3 + t], sem) for b in range(3) for t in range(3)
@@ -163,26 +163,17 @@
 
     first = [group(w1, w1v, a, sems.at[a]) for a in range(3)]
     later = [copy for a in range(3) for copy in group(w2, w2v, a, sems.at[3 + a])]
-    empty = []
-    for rh in range(2):
-        for rw in range(2):
-            for k, (row, col) in enumerate(reach(rh, rw)):
-                a, b = rh + 1 - row, rw + 1 - col
-                where = pl.ds(k * 32, 32)
-                if 0 <= a <= 2 and 0 <= b <= 2:
-                    for t in range(3):
-                        later.append(
-                            pltpu.make_async_copy(
-                                wh.at[t, a, b], wy.at[rh * 2 + rw, where, pl.ds(t * C, C)], sems.at[6]
-                            )
-                        )
-                else:
-                    empty.append((rh * 2 + rw, where))
+    for t in range(3):
+        for a in range(3):
+            for b in range(3):
+                later.append(
+                    pltpu.make_async_copy(
+                        wh.at[t, a, b], flat.at[pl.ds((a * 3 + b) * 32, 32), pl.ds(t * C, C)], sems.at[6]
+                    )
+                )
     for copies in first[:2]:
         for copy in copies:
             copy.start()
-    for where in empty:
-        wy[where] = jnp.zeros((32, 3 * C), BF16)
     acc[...] = jnp.zeros_like(acc)
 
     def cells(h, _):
@@ -203,7 +194,7 @@
         copy.wait()
 
 
-def rows_kernel(top, bot, acc, plain, csw, vec, w1v, sides, s2, raw, s1, add):
+def rows_kernel(top, bot, acc, plain, csw, vec, w1v, flat, sides, s2, raw, wy, s1, add):
     up, down, _, _ = place()
     for msg, h0, valid in ((top, 0, up), (bot, 2, down)):
         for h in range(2):
@@ -229,6 +220,18 @@
         hidden(s2, (n, pl.ds(0, 6)), total.reshape(6 * F, C), vec, cached, valid)
     for k in range(R * Q):
         raw[k] = rows_at(plain, k, F, PITCH).astype(BF16)
+    turned = jnp.transpose(flat[...])
+    none = jnp.zeros((3 * C, 32), BF16)
+    for rh in range(2):
+        for rw in range(2):
+            targets = reach(rh, rw)
+            for patch in range(4):
+                parts = []
+                for row, col in targets[4 * patch : 4 * patch + 4]:
+                    a, b = rh + 1 - row, rw + 1 - col
+                    low = (a * 3 + b) * 32
+                    parts.append(turned[:, low : low + 32] if 0 <= a <= 2 and 0 <= b <= 2 else none)
+                wy[rh * 2 + rw, :, patch * 128 : (patch + 1) * 128] = jnp.concatenate(parts, axis=-1)
     for n, col in enumerate((0, 8)):
         sides[0:2, 2 * n : 2 * n + 2] = add[0:2, col : col + 2]
         sides[2:4, 2 * n : 2 * n + 2] = acc[2:4, col : col + 2]
@@ -338,9 +341,8 @@
     sums = {}
     for rh in range(2):
         for rw in range(2):
-            part = lax.dot_general(
-                s3[rh * 2 + rw].reshape(8 * F, 3 * C), wy[rh * 2 + rw], (((1,), (1,)), ((), ())),
-                preferred_element_type=F32,
+            part = jnp.dot(
+                s3[rh * 2 + rw].reshape(8 * F, 3 * C), wy[rh * 2 + rw], preferred_element_type=F32
             )
             for k in range(8):
                 for m in range(2):
@@ -449,9 +451,9 @@
     top = lax.ppermute(hi, "ha", around("ha", 1))
     bot = lax.ppermute(lo, "ha", around("ha", -1))
     cell_flops = 2 * F * 27 * C * C
-    sums1, w1v, w2v, wy = kernel(
+    sums1, w1v, w2v, flat = kernel(
         inner_kernel,
-        [near(R + 2, Q + 2, F, C, dtype=F32), near(3, 9, C, C), near(3, 9, C, C), near(4, 512, 3 * C)],
+        [near(R + 2, Q + 2, F, C, dtype=F32), near(3, 9, C, C), near(3, 9, C, C), near(9 * 32, 3 * C)],
         [VM] * 2 + [ANY] * 3,
         [pltpu.VMEM((R * Q, F, 3 * C), BF16), pltpu.SemaphoreType.DMA((7,))],
         12, "inner", 32 * cell_flops, 17 * 2**20,
@@ -462,16 +464,17 @@
         [VM] * 6,
         [pltpu.VMEM((3, 128, 128), F32)] * 2,
         4, "pack_columns",
-    )(own, top, bot, cfw, csw, wy)
+    )(own, top, bot, cfw, csw, flat)
     left = lax.ppermute(to_right, "wa", around("wa", 1))
     right = lax.ppermute(to_left, "wa", around("wa", -1))
-    sides, rows2, raw = kernel(
+    sides, rows2, raw, wy = kernel(
         rows_kernel,
-        [near(R + 2, 4, F, C, dtype=F32), near(R + 2, 6, F, 3 * C), near(32, F, C)],
-        [VM] * 7,
+        [near(R + 2, 4, F, C, dtype=F32), near(R + 2, 6, F, 3 * C), near(32, F, C),
+         near(4, 3 * C, 512)],
+        [VM] * 8,
         [pltpu.VMEM((4, Q, F, 3 * C), BF16), pltpu.VMEM((4, Q + 2, F, C), F32)],
-        10, "rows", 16 * cell_flops, 10 * 2**20,
-    )(top, bot, sums1, plain, csw, vec, w1v)
+        16, "rows", 16 * cell_flops, 10 * 2**20,
+    )(top, bot, sums1, plain, csw, vec, w1v, flat)
     (slots,) = kernel(
         finish_kernel,
         [shape(F, 8, 8, 128)],

time: 54.3 us -> 53.9 us (level)
  waiting for transfers between devices: 3.29 us -> 2.58 us
    pallas_call x1, Pallas kernels: 3.35 us -> 4.06 us  [local(): kernel(rows_kernel, [near(R + 2, 4, F, C, dtype=F32), near(R + 2, 6, F, 3...]
    ppermute x1, waiting for transfers between devices: 2.12 us -> 1.41 us  [local(): right = lax.ppermute(to_left, 'wa', around('wa', -1))]
  transfers between devices with their start and end apart: 5 -> 5, of which waited for: 2 -> 2; matrix products, arithmetic and copies ran while one was open for 0% -> 0% of each run, Pallas kernels for 21% -> 23%
where the time goes in v11:
time: 53.9 us; the launch traced here: 53.7 us
  Pallas kernels  24.3 us (45%)
  blocking collectives  17.3 us (32%)
  starting transfers between devices  9.55 us (18%)
  waiting for transfers between devices  2.58 us (5%)
    all_to_all x1, blocking collectives, local(): lax.all_to_all(slots.reshape(F * 8, 8, 128), ('ha', 'wa'), 0, 0, tiled=True)  17.3 us
    pallas_call x1, Pallas kernels, local(): kernel(finish_kernel, [shape(F, 8, 8, 128)], [VM] * 13, [pltpu.VMEM((8, 4...  9.45 us
    pallas_call x1, Pallas kernels, local(): kernel(inner_kernel, [near(R + 2, Q + 2, F, C, dtype=F32), near(3, 9, C,...  8.13 us
    pallas_call x1, Pallas kernels, local(): kernel(rows_kernel, [near(R + 2, 4, F, C, dtype=F32), near(R + 2, 6, F, 3...  4.06 us
    ppermute x1, starting transfers between devices, local(): bot = lax.ppermute(lo, 'ha', around('ha', -1))  3.71 us
    ppermute x1, starting transfers between devices, local(): left = lax.ppermute(to_right, 'wa', around('wa', 1))  2.54 us
    ppermute x1, starting transfers between devices, local(): top = lax.ppermute(hi, 'ha', around('ha', 1))  2.19 us
    pallas_call x1, Pallas kernels, local(): kernel(first_kernel, [near(32, F, C), near(3, F * PITCH, 128, dtype=F32),...  1.79 us
  transfers between devices with their start and end apart: 5, of which 2 were waited for; matrix products, arithmetic and copies ran while one was open for 0% of the time, Pallas kernels for 23%

profile of v11, /device:TPU:1, one launch (start us, length us, event | category | flops | bytes accessed | tf_op | source)
XLA Modules:
  0.0 53.7 jit_solution(5873164913943240614)
XLA Ops:
  0.0 1.8 %act_first.1 = (bf16[32,16,384]{2,1,0:T(8,128)(2,1)S(1)}, f32[3,640,128]{2,1,0:T(8,128)S(1)}, bf16[19,16,384]{2,1,0:T(8,128)(2,1)S(1)}, bf16[19,16,384]{2,1,0:T(...) custom-call(bf16[16,4,8,384]{3,2,1,0:T(8,128)(2,1)} %feat_h.1, ...), custom_call_target="tpu_custom_call" | custom-call | tf_op jit(solution)/shard_map/act_first/pallas_call | solution.py:433
  1.8 2.2 %collective-permute-start = (bf16[19,16,384]{2,1,0:T(8,128)(2,1)S(1)}, bf16[19,16,384]{2,1,0:T(8,128)(2,1)S(1)}, u32[]{:S(2)}, u32[]{:S(2)}) collective-permute-start(bf16[19,16,384]{2,1,0:T(8,128)(2,1)S(1)} %get-tuple-element.25), channel_id=1, source_target_pairs={{0,8},{8,16},{16,24},{24,32},{32,40},{40,48},{48,56},{56,64},{64,7... | collective-permute-start | bytes 700424 | tf_op jit(solution)/shard_map/ppermute | solution.py:451
  4.0 3.7 %collective-permute-start.1 = (bf16[19,16,384]{2,1,0:T(8,128)(2,1)S(1)}, bf16[19,16,384]{2,1,0:T(8,128)(2,1)S(1)}, u32[]{:S(2)}, u32[]{:S(2)}) collective-permute-start(bf16[19,16,384]{2,1,0:T(8,128)(2,1)S(1)} %get-tuple-element.26), channel_id=1, source_target_pairs={{0,120},{8,0},{16,8},{24,16},{32,24},{40,32},{48,40},{56,48},{64,5... | collective-permute-start | bytes 700424 | tf_op jit(solution)/shard_map/ppermute | solution.py:452
  7.7 8.1 %inner.1 = (f32[6,10,16,384]{3,2,1,0:T(8,128)S(1)}, bf16[3,9,384,384]{3,2,1,0:T(8,128)(2,1)S(1)}, bf16[3,9,384,384]{3,2,1,0:T(8,128)(2,1)S(1)}, bf16[288,1152]{1,0:T(8,128)(2,1)S(1)}) custom-call(bf16[32,16,384]{2,1,0:T(8,128)(2,1)S(1)} %get-tuple-element.24.own, f32[3,64,128]{2,1,0:T(8,128)S(1)} %get-tuple-element.27.cfw, bf16[3,3,3,384,384]{4,3,2,1,0:T(8,128)(2,1)} %w1.1, ...), custom_call_target="tpu_custom_call" | custom-call | flops 4076863488 | bytes 17825792 | tf_op jit(solution)/shard_map/inner/pallas_call | solution.py:454
  15.9 0.0 collective-permute-done.top
  15.9 0.0 collective-permute-done.1.bot
  15.9 0.1 pack_columns.1
  16.0 2.5 %collective-permute-start.2 = (bf16[19,16,384]{2,1,0:T(8,128)(2,1)S(1)}, bf16[19,16,384]{2,1,0:T(8,128)(2,1)S(1)}, u32[]{:S(2)}, u32[]{:S(2)}) collective-permute-start(bf16[19,16,384]{2,1,0:T(8,128)(2,1)S(1)} %get-tuple-element.30), channel_id=1, source_target_pairs={{0,1},{1,2},{2,3},{3,4},{4,5},{5,6},{6,7},{7,0},{8,9},{9,10},{10,1... | collective-permute-start | bytes 700424 | tf_op jit(solution)/shard_map/ppermute | solution.py:468
  18.5 0.0 collective-permute-start.3
  18.5 4.1 %rows.1 = (f32[6,4,16,384]{3,2,1,0:T(8,128)S(1)}, bf16[6,6,16,1152]{3,2,1,0:T(8,128)(2,1)S(1)}, bf16[32,16,384]{2,1,0:T(8,128)(2,1)S(1)}, bf16[4,1152,512]{2,1,0:T(8,128)(2,1)S(1)}) custom-call(bf16[19,16,384]{2,1,0:T(8,128)(2,1)S(1)} %collective-permute-done.top, bf16[19,16,384]{2,1,0:T(8,128)(2,1)S(1)} %collective-permute-done.1.bot, ...), custom_call_target="tpu_custom_call" | custom-call | flops 2038431744 | bytes 10485760 | tf_op jit(solution)/shard_map/rows/pallas_call | solution.py:470
  22.6 0.0 collective-permute-done.2.left
  22.6 1.4 %collective-permute-done.3.right = bf16[19,16,384]{2,1,0:T(8,128)(2,1)S(1)} collective-permute-done((bf16[19,16,384]{2,1,0:T(8,128)(2,1)S(1)}, bf16[19,16,384]{2,1,0:T(8,128)(2,1)S(1)}, u32[]{:S(2)}, u32[]{:S(2)}) %collective-permute-start.3) | collective-permute-done | bytes 233504 | tf_op jit(solution)/shard_map/ppermute | solution.py:469
  24.0 9.4 %finish.1 = bf16[16,8,8,128]{3,2,1,0:T(8,128)(2,1)S(1)} custom-call(bf16[19,16,384]{2,1,0:T(8,128)(2,1)S(1)} %collective-permute-done.2.left, bf16[19,16,384]{2,1,0:T(8,128)(2,1)S(1)} %collective-permute-done.3.right, bf16[19,16,384]{2,1,0:T(8,128)(2,1)S(1)} %collective-permute-done.top, bf16[19,16,384]{2,1,0:T(8,128)(2,1)S(1)} %collective-permute-done.1.bot, ...), custom_call_target="tpu_custom_call" | custom-call | flops 6115295232 | bytes 20971520 | tf_op jit(solution)/shard_map/finish/pallas_call | solution.py:478
  33.5 17.3 %all_to_all.5.mine = bf16[128,8,128]{2,1,0:T(8,128)(2,1)S(1)} all-to-all(bf16[128,8,128]{2,1,0:T(8,128)(2,1)S(1)} %bitcast.2), channel_id=1, replica_groups=mesh['ha'=16,'wa'=8] {'ha','wa'}, dimensions={0} | all-to-all | bytes 524288 | tf_op jit(solution)/shard_map/all_to_all | solution.py:494
  50.7 1.1 %collective-permute-start.4 = (bf16[128,8,128]{2,1,0:T(8,128)(2,1)S(1)}, bf16[128,8,128]{2,1,0:T(8,128)(2,1)S(1)}, u32[]{:S(2)}, u32[]{:S(2)}) collective-permute-start(bf16[128,8,128]{2,1,0:T(8,128)(2,1)S(1)} %all_to_all.5.mine), channel_id=1, source_target_pairs={{0,1},{1,0},{2,3},{3,2},{4,5},{5,4},{6,7},{7,6},{8,9},{9,8},{10,11... | collective-permute-start | bytes 786440 | tf_op jit(solution)/shard_map/ppermute | solution.py:496
  51.8 1.2 %collective-permute-done.4.theirs = bf16[128,8,128]{2,1,0:T(8,128)(2,1)S(1)} collective-permute-done((bf16[128,8,128]{2,1,0:T(8,128)(2,1)S(1)}, bf16[128,8,128]{2,1,0:T(8,128)(2,1)S(1)}, u32[]{:S(2)}, u32[]{:S(2)}) %collective-permute-start.4) | collective-permute-done | bytes 262176 | tf_op jit(solution)/shard_map/ppermute | solution.py:496
  53.0 0.7 %sum_patches.1 = bf16[128,128]{1,0:T(8,128)(2,1)} custom-call(bf16[128,8,128]{2,1,0:T(8,128)(2,1)S(1)} %all_to_all.5.mine, bf16[128,8,128]{2,1,0:T(8,128)(2,1)S(1)} %collective-permute-done.4.theirs, f32[8,128]{1,0:T(8,128)S(1)} %get-tuple-element.42.bias), custom_call_target="tpu_custom_call" | custom-call | tf_op jit(solution)/shard_map/sum_patches/pallas_call | solution.py:497
Async XLA Ops:
  1.8 14.1 %collective-permute-start = (bf16[19,16,384]{2,1,0:T(8,128)(2,1)S(1)}, bf16[19,16,384]{2,1,0:T(8,128)(2,1)S(1)}, u32[]{:S(2)}, u32[]{:S(2)}) collective-permute-start(bf16[19,16,384]{2,1,0:T(8,128)(2,1)S(1)} %get-tuple-element.25), channel_id=1, source_target_pairs={{0,8},{8,16},{16,24},{24,32},{32,40},{40,48},{48,56},{56,64},{64,7... | collective-permute-start | bytes 700424 | tf_op jit(solution)/shard_map/ppermute | solution.py:451
  4.0 11.9 %collective-permute-start.1 = (bf16[19,16,384]{2,1,0:T(8,128)(2,1)S(1)}, bf16[19,16,384]{2,1,0:T(8,128)(2,1)S(1)}, u32[]{:S(2)}, u32[]{:S(2)}) collective-permute-start(bf16[19,16,384]{2,1,0:T(8,128)(2,1)S(1)} %get-tuple-element.26), channel_id=1, source_target_pairs={{0,120},{8,0},{16,8},{24,16},{32,24},{40,32},{48,40},{56,48},{64,5... | collective-permute-start | bytes 700424 | tf_op jit(solution)/shard_map/ppermute | solution.py:452
  16.0 6.6 %collective-permute-start.2 = (bf16[19,16,384]{2,1,0:T(8,128)(2,1)S(1)}, bf16[19,16,384]{2,1,0:T(8,128)(2,1)S(1)}, u32[]{:S(2)}, u32[]{:S(2)}) collective-permute-start(bf16[19,16,384]{2,1,0:T(8,128)(2,1)S(1)} %get-tuple-element.30), channel_id=1, source_target_pairs={{0,1},{1,2},{2,3},{3,4},{4,5},{5,6},{6,7},{7,0},{8,9},{9,10},{10,1... | collective-permute-start | bytes 700424 | tf_op jit(solution)/shard_map/ppermute | solution.py:468
  18.5 5.5 %collective-permute-start.3 = (bf16[19,16,384]{2,1,0:T(8,128)(2,1)S(1)}, bf16[19,16,384]{2,1,0:T(8,128)(2,1)S(1)}, u32[]{:S(2)}, u32[]{:S(2)}) collective-permute-start(bf16[19,16,384]{2,1,0:T(8,128)(2,1)S(1)} %get-tuple-element.31), channel_id=1, source_target_pairs={{0,7},{1,0},{2,1},{3,2},{4,3},{5,4},{6,5},{7,6},{8,15},{9,8},{10,9... | collective-permute-start | bytes 700424 | tf_op jit(solution)/shard_map/ppermute | solution.py:469
  50.7 2.3 %collective-permute-start.4 = (bf16[128,8,128]{2,1,0:T(8,128)(2,1)S(1)}, bf16[128,8,128]{2,1,0:T(8,128)(2,1)S(1)}, u32[]{:S(2)}, u32[]{:S(2)}) collective-permute-start(bf16[128,8,128]{2,1,0:T(8,128)(2,1)S(1)} %all_to_all.5.mine), channel_id=1, source_target_pairs={{0,1},{1,0},{2,3},{3,2},{4,5},{5,4},{6,7},{7,6},{8,9},{9,8},{10,11... | collective-permute-start | bytes 786440 | tf_op jit(solution)/shard_map/ppermute | solution.py:496

commit v12 on v11

--- a/solution.py
+++ b/solution.py
@@ -256,22 +256,30 @@
                 [side_f[n, pl.ds(c * 16 + h * 2 + 1, 1), :] for c in range(2)], valid,
             )
 
-    acc1[...] = sides[...]
     def columns(first):
         return jnp.concatenate([s1[a : a + 6, first : first + 2].reshape(12 * F, 3 * C) for a in range(3)], axis=-1)
 
     def column_tap(b, low, high):
         return jnp.concatenate([w1v[a, 3 * b : 3 * b + 3, :, low:high].reshape(3 * C, high - low) for a in range(3)], axis=0)
 
-    for b, targets in enumerate(((0, 1), (0, 3), (2, 3))):
+    main, last = slice(0, 256), slice(256, 384)
+    for b in (0, 2, 1):
         part = jnp.dot(columns(b), column_tap(b, 0, 256), preferred_element_type=F32).reshape(6, 2, F, 256)
-        for n, col in enumerate(targets):
-            acc1[:, col, :, 0:256] += part[:, n]
-    for b, moves in ((0, ((0, 0, 0), (1, 0, 1), (1, 1, 0))), (1, ((0, 0, 3), (0, 1, 2), (1, 1, 3)))):
+        if b == 1:
+            for n, col in enumerate((0, 3)):
+                acc1[:, col, :, main] += part[:, n]
+        else:
+            acc1[:, b : b + 2, :, main] = sides[:, b : b + 2, :, main] + part
+    for b in range(2):
         weight = jnp.concatenate([column_tap(b, 256, 384), column_tap(b + 1, 256, 384)], axis=-1)
         part = jnp.dot(columns(2 * b), weight, preferred_element_type=F32).reshape(6, 2, F, 256)
-        for n, tap, col in moves:
-            acc1[:, col, :, 256:384] += part[:, n, :, tap * 128 : (tap + 1) * 128]
+        both = part[:, 0, :, :128] + part[:, 1, :, 128:]
+        if b == 0:
+            acc1[:, 0, :, last] = sides[:, 0, :, last] + both
+            acc1[:, 1, :, last] = sides[:, 1, :, last] + part[:, 1, :, :128]
+        else:
+            acc1[:, 3, :, last] = sides[:, 3, :, last] + both
+            acc1[:, 2, :, last] = sides[:, 2, :, last] + part[:, 0, :, 128:]
     s2[:, 2:8] = rows2[...]
     for h in range(6):
         inside = up if h == 0 else down if h == 5 else True
@@ -367,10 +375,14 @@
     even = g % 2 == 0
     first = [jnp.clip(2 * g - 1 + k, 0, ha_count - 1) * 8 for k in range(4)]
 
+    halves = {}
+    for k in range(4):
+        for j in range(8):
+            here, there = mine[first[k] + j].astype(F32), theirs[first[k] + j].astype(F32)
+            halves[k, j] = jnp.where(even, here, there), jnp.where(even, there, here)
+
     def held(k, j, low, count):
-        where = (first[k] + j, pl.ds(low % 8, count))
-        here, there = mine[where].astype(F32), theirs[where].astype(F32)
-        return jnp.where(even == (low < 8), here, there)
+        return halves[k, j][low // 8][low % 8 : low % 8 + count]
 
     lane = lax.broadcasted_iota(jnp.int32, (4, 128), 1)
     row = lax.broadcasted_iota(jnp.int32, (4, 128), 0)

time: 53.9 us -> 53.9 us (level)
  no operation moved by 1% of the time
where the time goes in v12:
time: 53.9 us; the launch traced here: 53.8 us
  Pallas kernels  24.3 us (45%)
  blocking collectives  17.3 us (32%)
  starting transfers between devices  9.55 us (18%)
  waiting for transfers between devices  2.58 us (5%)
    all_to_all x1, blocking collectives, local(): lax.all_to_all(slots.reshape(F * 8, 8, 128), ('ha', 'wa'), 0, 0, tiled=True)  17.3 us
    pallas_call x1, Pallas kernels, local(): kernel(finish_kernel, [shape(F, 8, 8, 128)], [VM] * 13, [pltpu.VMEM((8, 4...  9.57 us
    pallas_call x1, Pallas kernels, local(): kernel(inner_kernel, [near(R + 2, Q + 2, F, C, dtype=F32), near(3, 9, C,...  8.13 us
    pallas_call x1, Pallas kernels, local(): kernel(rows_kernel, [near(R + 2, 4, F, C, dtype=F32), near(R + 2, 6, F, 3...  4.06 us
    ppermute x1, starting transfers between devices, local(): bot = lax.ppermute(lo, 'ha', around('ha', -1))  3.71 us
    ppermute x1, starting transfers between devices, local(): left = lax.ppermute(to_right, 'wa', around('wa', 1))  2.54 us
    ppermute x1, starting transfers between devices, local(): top = lax.ppermute(hi, 'ha', around('ha', 1))  2.19 us
    pallas_call x1, Pallas kernels, local(): kernel(first_kernel, [near(32, F, C), near(3, F * PITCH, 128, dtype=F32),...  1.79 us
  transfers between devices with their start and end apart: 5, of which 2 were waited for; matrix products, arithmetic and copies ran while one was open for 0% of the time, Pallas kernels for 23%

profile of v12, /device:TPU:1, one launch (start us, length us, event | category | flops | bytes accessed | tf_op | source)
XLA Modules:
  0.0 53.8 jit_solution(10426865545182756111)
XLA Ops:
  0.0 1.8 %act_first.1 = (bf16[32,16,384]{2,1,0:T(8,128)(2,1)S(1)}, f32[3,640,128]{2,1,0:T(8,128)S(1)}, bf16[19,16,384]{2,1,0:T(8,128)(2,1)S(1)}, bf16[19,16,384]{2,1,0:T(...) custom-call(bf16[16,4,8,384]{3,2,1,0:T(8,128)(2,1)} %feat_h.1, ...), custom_call_target="tpu_custom_call" | custom-call | tf_op jit(solution)/shard_map/act_first/pallas_call | solution.py:445
  1.8 2.2 %collective-permute-start = (bf16[19,16,384]{2,1,0:T(8,128)(2,1)S(1)}, bf16[19,16,384]{2,1,0:T(8,128)(2,1)S(1)}, u32[]{:S(2)}, u32[]{:S(2)}) collective-permute-start(bf16[19,16,384]{2,1,0:T(8,128)(2,1)S(1)} %get-tuple-element.25), channel_id=1, source_target_pairs={{0,8},{8,16},{16,24},{24,32},{32,40},{40,48},{48,56},{56,64},{64,7... | collective-permute-start | bytes 700424 | tf_op jit(solution)/shard_map/ppermute | solution.py:463
  4.0 3.7 %collective-permute-start.1 = (bf16[19,16,384]{2,1,0:T(8,128)(2,1)S(1)}, bf16[19,16,384]{2,1,0:T(8,128)(2,1)S(1)}, u32[]{:S(2)}, u32[]{:S(2)}) collective-permute-start(bf16[19,16,384]{2,1,0:T(8,128)(2,1)S(1)} %get-tuple-element.26), channel_id=1, source_target_pairs={{0,120},{8,0},{16,8},{24,16},{32,24},{40,32},{48,40},{56,48},{64,5... | collective-permute-start | bytes 700424 | tf_op jit(solution)/shard_map/ppermute | solution.py:464
  7.7 8.1 %inner.1 = (f32[6,10,16,384]{3,2,1,0:T(8,128)S(1)}, bf16[3,9,384,384]{3,2,1,0:T(8,128)(2,1)S(1)}, bf16[3,9,384,384]{3,2,1,0:T(8,128)(2,1)S(1)}, bf16[288,1152]{1,0:T(8,128)(2,1)S(1)}) custom-call(bf16[32,16,384]{2,1,0:T(8,128)(2,1)S(1)} %get-tuple-element.24.own, f32[3,64,128]{2,1,0:T(8,128)S(1)} %get-tuple-element.27.cfw, bf16[3,3,3,384,384]{4,3,2,1,0:T(8,128)(2,1)} %w1.1, ...), custom_call_target="tpu_custom_call" | custom-call | flops 4076863488 | bytes 17825792 | tf_op jit(solution)/shard_map/inner/pallas_call | solution.py:466
  15.9 0.0 collective-permute-done.top
  15.9 0.0 collective-permute-done.1.bot
  15.9 0.1 pack_columns.1
  16.0 2.5 %collective-permute-start.2 = (bf16[19,16,384]{2,1,0:T(8,128)(2,1)S(1)}, bf16[19,16,384]{2,1,0:T(8,128)(2,1)S(1)}, u32[]{:S(2)}, u32[]{:S(2)}) collective-permute-start(bf16[19,16,384]{2,1,0:T(8,128)(2,1)S(1)} %get-tuple-element.30), channel_id=1, source_target_pairs={{0,1},{1,2},{2,3},{3,4},{4,5},{5,6},{6,7},{7,0},{8,9},{9,10},{10,1... | collective-permute-start | bytes 700424 | tf_op jit(solution)/shard_map/ppermute | solution.py:480
  18.5 0.0 collective-permute-start.3
  18.5 4.1 %rows.1 = (f32[6,4,16,384]{3,2,1,0:T(8,128)S(1)}, bf16[6,6,16,1152]{3,2,1,0:T(8,128)(2,1)S(1)}, bf16[32,16,384]{2,1,0:T(8,128)(2,1)S(1)}, bf16[4,1152,512]{2,1,0:T(8,128)(2,1)S(1)}) custom-call(bf16[19,16,384]{2,1,0:T(8,128)(2,1)S(1)} %collective-permute-done.top, bf16[19,16,384]{2,1,0:T(8,128)(2,1)S(1)} %collective-permute-done.1.bot, ...), custom_call_target="tpu_custom_call" | custom-call | flops 2038431744 | bytes 10485760 | tf_op jit(solution)/shard_map/rows/pallas_call | solution.py:482
  22.6 0.0 collective-permute-done.2.left
  22.6 1.4 %collective-permute-done.3.right = bf16[19,16,384]{2,1,0:T(8,128)(2,1)S(1)} collective-permute-done((bf16[19,16,384]{2,1,0:T(8,128)(2,1)S(1)}, bf16[19,16,384]{2,1,0:T(8,128)(2,1)S(1)}, u32[]{:S(2)}, u32[]{:S(2)}) %collective-permute-start.3) | collective-permute-done | bytes 233504 | tf_op jit(solution)/shard_map/ppermute | solution.py:481
  24.0 9.6 %finish.1 = bf16[16,8,8,128]{3,2,1,0:T(8,128)(2,1)S(1)} custom-call(bf16[19,16,384]{2,1,0:T(8,128)(2,1)S(1)} %collective-permute-done.2.left, bf16[19,16,384]{2,1,0:T(8,128)(2,1)S(1)} %collective-permute-done.3.right, bf16[19,16,384]{2,1,0:T(8,128)(2,1)S(1)} %collective-permute-done.top, bf16[19,16,384]{2,1,0:T(8,128)(2,1)S(1)} %collective-permute-done.1.bot, ...), custom_call_target="tpu_custom_call" | custom-call | flops 6115295232 | bytes 20971520 | tf_op jit(solution)/shard_map/finish/pallas_call | solution.py:490
  33.6 17.3 %all_to_all.5.mine = bf16[128,8,128]{2,1,0:T(8,128)(2,1)S(1)} all-to-all(bf16[128,8,128]{2,1,0:T(8,128)(2,1)S(1)} %bitcast.2), channel_id=1, replica_groups=mesh['ha'=16,'wa'=8] {'ha','wa'}, dimensions={0} | all-to-all | bytes 524288 | tf_op jit(solution)/shard_map/all_to_all | solution.py:506
  50.8 1.1 %collective-permute-start.4 = (bf16[128,8,128]{2,1,0:T(8,128)(2,1)S(1)}, bf16[128,8,128]{2,1,0:T(8,128)(2,1)S(1)}, u32[]{:S(2)}, u32[]{:S(2)}) collective-permute-start(bf16[128,8,128]{2,1,0:T(8,128)(2,1)S(1)} %all_to_all.5.mine), channel_id=1, source_target_pairs={{0,1},{1,0},{2,3},{3,2},{4,5},{5,4},{6,7},{7,6},{8,9},{9,8},{10,11... | collective-permute-start | bytes 786440 | tf_op jit(solution)/shard_map/ppermute | solution.py:508
  51.9 1.2 %collective-permute-done.4.theirs = bf16[128,8,128]{2,1,0:T(8,128)(2,1)S(1)} collective-permute-done((bf16[128,8,128]{2,1,0:T(8,128)(2,1)S(1)}, bf16[128,8,128]{2,1,0:T(8,128)(2,1)S(1)}, u32[]{:S(2)}, u32[]{:S(2)}) %collective-permute-start.4) | collective-permute-done | bytes 262176 | tf_op jit(solution)/shard_map/ppermute | solution.py:508
  53.1 0.7 %sum_patches.1 = bf16[128,128]{1,0:T(8,128)(2,1)} custom-call(bf16[128,8,128]{2,1,0:T(8,128)(2,1)S(1)} %all_to_all.5.mine, bf16[128,8,128]{2,1,0:T(8,128)(2,1)S(1)} %collective-permute-done.4.theirs, f32[8,128]{1,0:T(8,128)S(1)} %get-tuple-element.42.bias), custom_call_target="tpu_custom_call" | custom-call | tf_op jit(solution)/shard_map/sum_patches/pallas_call | solution.py:509
Async XLA Ops:
  1.8 14.1 %collective-permute-start = (bf16[19,16,384]{2,1,0:T(8,128)(2,1)S(1)}, bf16[19,16,384]{2,1,0:T(8,128)(2,1)S(1)}, u32[]{:S(2)}, u32[]{:S(2)}) collective-permute-start(bf16[19,16,384]{2,1,0:T(8,128)(2,1)S(1)} %get-tuple-element.25), channel_id=1, source_target_pairs={{0,8},{8,16},{16,24},{24,32},{32,40},{40,48},{48,56},{56,64},{64,7... | collective-permute-start | bytes 700424 | tf_op jit(solution)/shard_map/ppermute | solution.py:463
  4.0 11.9 %collective-permute-start.1 = (bf16[19,16,384]{2,1,0:T(8,128)(2,1)S(1)}, bf16[19,16,384]{2,1,0:T(8,128)(2,1)S(1)}, u32[]{:S(2)}, u32[]{:S(2)}) collective-permute-start(bf16[19,16,384]{2,1,0:T(8,128)(2,1)S(1)} %get-tuple-element.26), channel_id=1, source_target_pairs={{0,120},{8,0},{16,8},{24,16},{32,24},{40,32},{48,40},{56,48},{64,5... | collective-permute-start | bytes 700424 | tf_op jit(solution)/shard_map/ppermute | solution.py:464
  16.0 6.6 %collective-permute-start.2 = (bf16[19,16,384]{2,1,0:T(8,128)(2,1)S(1)}, bf16[19,16,384]{2,1,0:T(8,128)(2,1)S(1)}, u32[]{:S(2)}, u32[]{:S(2)}) collective-permute-start(bf16[19,16,384]{2,1,0:T(8,128)(2,1)S(1)} %get-tuple-element.30), channel_id=1, source_target_pairs={{0,1},{1,2},{2,3},{3,4},{4,5},{5,6},{6,7},{7,0},{8,9},{9,10},{10,1... | collective-permute-start | bytes 700424 | tf_op jit(solution)/shard_map/ppermute | solution.py:480
  18.5 5.5 %collective-permute-start.3 = (bf16[19,16,384]{2,1,0:T(8,128)(2,1)S(1)}, bf16[19,16,384]{2,1,0:T(8,128)(2,1)S(1)}, u32[]{:S(2)}, u32[]{:S(2)}) collective-permute-start(bf16[19,16,384]{2,1,0:T(8,128)(2,1)S(1)} %get-tuple-element.31), channel_id=1, source_target_pairs={{0,7},{1,0},{2,1},{3,2},{4,3},{5,4},{6,5},{7,6},{8,15},{9,8},{10,9... | collective-permute-start | bytes 700424 | tf_op jit(solution)/shard_map/ppermute | solution.py:481
  50.8 2.3 %collective-permute-start.4 = (bf16[128,8,128]{2,1,0:T(8,128)(2,1)S(1)}, bf16[128,8,128]{2,1,0:T(8,128)(2,1)S(1)}, u32[]{:S(2)}, u32[]{:S(2)}) collective-permute-start(bf16[128,8,128]{2,1,0:T(8,128)(2,1)S(1)} %all_to_all.5.mine), channel_id=1, source_target_pairs={{0,1},{1,0},{2,3},{3,2},{4,5},{5,4},{6,7},{7,6},{8,9},{9,8},{10,11... | collective-permute-start | bytes 786440 | tf_op jit(solution)/shard_map/ppermute | solution.py:508

commit v13 on v12

--- a/solution.py
+++ b/solution.py
@@ -109,7 +109,7 @@
     for n in range(3):
         wide_f[n, pl.ds(32, 64)] = cfw[n]
         wide_s[n, pl.ds(16, 64)] = csw[n]
-        wide_s[n, pl.ds(96, 32)] = jnp.zeros((32, 128), F32)
+        wide_s[n, pl.ds(96, 40)] = jnp.zeros((40, 128), F32)
     for out, base, edge in ((left, 0, 0), (right, 6, 7)):
         for c in range(2):
             for h in range(8):
@@ -364,9 +364,10 @@
     acch[pl.ds(15 * F, F)] = jnp.zeros((F, 128), F32)
 
     for f in range(F):
-        patches = acch[pl.ds(f, 16, stride=F), :].astype(BF16)
+        patches = acch[pl.ds(f, 16, stride=F), :]
+        halves = [patches[:8].astype(BF16), patches[8:].astype(BF16)]
         for g in range(8):
-            out[f, g] = patches[8 * (g % 2) : 8 * (g % 2) + 8]
+            out[f, g] = halves[g % 2]
 
 
 def last_kernel(mine, theirs, bias, out, sums):
@@ -444,7 +445,7 @@
 ):
     own, plain, lo, hi, cfw, csw, chw, vec, bias = kernel(
         first_kernel,
-        [near(32, F, C), near(3, F * PITCH, 128, dtype=F32), near(MSG, F, C), near(MSG, F, C)]
+        [near(32, F, C), near(3, (F + 1) * PITCH, 128, dtype=F32), near(MSG, F, C), near(MSG, F, C)]
         + [near(3, 64, 128, dtype=F32)] * 3 + [near(8, C, dtype=F32), near(8, 128, dtype=F32)],
         [ANY] * 10,
         [
@@ -454,7 +455,7 @@
         + [pltpu.VMEM((C,), F32)] * 5
         + [
             pltpu.VMEM((32,), F32),
-            pltpu.VMEM((3, F * PITCH, 128), F32),
+            pltpu.VMEM((3, (F + 1) * PITCH, 128), F32),
             pltpu.SemaphoreType.DMA((13,)),
         ],
         12, "act_first",
@@ -474,7 +475,7 @@
         pack_kernel,
         [near(MSG, F, C)] * 2,
         [VM] * 6,
-        [pltpu.VMEM((3, 128, 128), F32)] * 2,
+        [pltpu.VMEM((3, 136, 128), F32)] * 2,
         4, "pack_columns",
     )(own, top, bot, cfw, csw, flat)
     left = lax.ppermute(to_right, "wa", around("wa", 1))
@@ -497,7 +498,7 @@
             pltpu.VMEM((R + 2, Q + 2, F, 3 * C), BF16),
             pltpu.VMEM((4, 8, F, 3 * C), BF16),
             pltpu.VMEM((R * Q * F, C), F32),
-            pltpu.VMEM((16 * F, 128), F32),
+            pltpu.VMEM((17 * F, 128), F32),
             pltpu.VMEM((2, 32, C), F32),
             pltpu.VMEM((2, 16, C), F32),
         ],

time: 53.9 us -> 54 us (level)
  no operation moved by 1% of the time
where the time goes in v13:
time: 54 us; the launch traced here: 53.8 us
  Pallas kernels  24.3 us (45%)
  blocking collectives  17.3 us (32%)
  starting transfers between devices  9.54 us (18%)
  waiting for transfers between devices  2.61 us (5%)
    all_to_all x1, blocking collectives, local(): lax.all_to_all(slots.reshape(F * 8, 8, 128), ('ha', 'wa'), 0, 0, tiled=True)  17.3 us
    pallas_call x1, Pallas kernels, local(): kernel(finish_kernel, [shape(F, 8, 8, 128)], [VM] * 13, [pltpu.VMEM((8, 4...  9.59 us
    pallas_call x1, Pallas kernels, local(): kernel(inner_kernel, [near(R + 2, Q + 2, F, C, dtype=F32), near(3, 9, C,...  8.1 us
    pallas_call x1, Pallas kernels, local(): kernel(rows_kernel, [near(R + 2, 4, F, C, dtype=F32), near(R + 2, 6, F, 3...  4.03 us
    ppermute x1, starting transfers between devices, local(): bot = lax.ppermute(lo, 'ha', around('ha', -1))  3.71 us
    ppermute x1, starting transfers between devices, local(): left = lax.ppermute(to_right, 'wa', around('wa', 1))  2.54 us
    ppermute x1, starting transfers between devices, local(): top = lax.ppermute(hi, 'ha', around('ha', 1))  2.19 us
    pallas_call x1, Pallas kernels, local(): kernel(first_kernel, [near(32, F, C), near(3, (F + 1) * PITCH, 128, dtype...  1.79 us
  transfers between devices with their start and end apart: 5, of which 2 were waited for; matrix products, arithmetic and copies ran while one was open for 0% of the time, Pallas kernels for 23%

profile of v13, /device:TPU:1, one launch (start us, length us, event | category | flops | bytes accessed | tf_op | source)
XLA Modules:
  0.0 53.8 jit_solution(16549363857652260071)
XLA Ops:
  0.0 1.8 %act_first.1 = (bf16[32,16,384]{2,1,0:T(8,128)(2,1)S(1)}, f32[3,680,128]{2,1,0:T(8,128)S(1)}, bf16[19,16,384]{2,1,0:T(8,128)(2,1)S(1)}, bf16[19,16,384]{2,1,0:T(...) custom-call(bf16[16,4,8,384]{3,2,1,0:T(8,128)(2,1)} %feat_h.1, ...), custom_call_target="tpu_custom_call" | custom-call | tf_op jit(solution)/shard_map/act_first/pallas_call | solution.py:446
  1.8 2.2 %collective-permute-start = (bf16[19,16,384]{2,1,0:T(8,128)(2,1)S(1)}, bf16[19,16,384]{2,1,0:T(8,128)(2,1)S(1)}, u32[]{:S(2)}, u32[]{:S(2)}) collective-permute-start(bf16[19,16,384]{2,1,0:T(8,128)(2,1)S(1)} %get-tuple-element.25), channel_id=1, source_target_pairs={{0,8},{8,16},{16,24},{24,32},{32,40},{40,48},{48,56},{56,64},{64,7... | collective-permute-start | bytes 700424 | tf_op jit(solution)/shard_map/ppermute | solution.py:464
  4.0 3.7 %collective-permute-start.1 = (bf16[19,16,384]{2,1,0:T(8,128)(2,1)S(1)}, bf16[19,16,384]{2,1,0:T(8,128)(2,1)S(1)}, u32[]{:S(2)}, u32[]{:S(2)}) collective-permute-start(bf16[19,16,384]{2,1,0:T(8,128)(2,1)S(1)} %get-tuple-element.26), channel_id=1, source_target_pairs={{0,120},{8,0},{16,8},{24,16},{32,24},{40,32},{48,40},{56,48},{64,5... | collective-permute-start | bytes 700424 | tf_op jit(solution)/shard_map/ppermute | solution.py:465
  7.7 8.1 %inner.1 = (f32[6,10,16,384]{3,2,1,0:T(8,128)S(1)}, bf16[3,9,384,384]{3,2,1,0:T(8,128)(2,1)S(1)}, bf16[3,9,384,384]{3,2,1,0:T(8,128)(2,1)S(1)}, bf16[288,1152]{1,0:T(8,128)(2,1)S(1)}) custom-call(bf16[32,16,384]{2,1,0:T(8,128)(2,1)S(1)} %get-tuple-element.24.own, f32[3,64,128]{2,1,0:T(8,128)S(1)} %get-tuple-element.27.cfw, bf16[3,3,3,384,384]{4,3,2,1,0:T(8,128)(2,1)} %w1.1, ...), custom_call_target="tpu_custom_call" | custom-call | flops 4076863488 | bytes 17825792 | tf_op jit(solution)/shard_map/inner/pallas_call | solution.py:467
  15.8 0.0 collective-permute-done.top
  15.8 0.0 collective-permute-done.1.bot
  15.8 0.1 pack_columns.1
  15.9 2.5 %collective-permute-start.2 = (bf16[19,16,384]{2,1,0:T(8,128)(2,1)S(1)}, bf16[19,16,384]{2,1,0:T(8,128)(2,1)S(1)}, u32[]{:S(2)}, u32[]{:S(2)}) collective-permute-start(bf16[19,16,384]{2,1,0:T(8,128)(2,1)S(1)} %get-tuple-element.30), channel_id=1, source_target_pairs={{0,1},{1,2},{2,3},{3,4},{4,5},{5,6},{6,7},{7,0},{8,9},{9,10},{10,1... | collective-permute-start | bytes 700424 | tf_op jit(solution)/shard_map/ppermute | solution.py:481
  18.5 0.0 collective-permute-start.3
  18.5 4.0 %rows.1 = (f32[6,4,16,384]{3,2,1,0:T(8,128)S(1)}, bf16[6,6,16,1152]{3,2,1,0:T(8,128)(2,1)S(1)}, bf16[32,16,384]{2,1,0:T(8,128)(2,1)S(1)}, bf16[4,1152,512]{2,1,0:T(8,128)(2,1)S(1)}) custom-call(bf16[19,16,384]{2,1,0:T(8,128)(2,1)S(1)} %collective-permute-done.top, bf16[19,16,384]{2,1,0:T(8,128)(2,1)S(1)} %collective-permute-done.1.bot, ...), custom_call_target="tpu_custom_call" | custom-call | flops 2038431744 | bytes 10485760 | tf_op jit(solution)/shard_map/rows/pallas_call | solution.py:483
  22.5 0.0 collective-permute-done.2.left
  22.5 1.4 %collective-permute-done.3.right = bf16[19,16,384]{2,1,0:T(8,128)(2,1)S(1)} collective-permute-done((bf16[19,16,384]{2,1,0:T(8,128)(2,1)S(1)}, bf16[19,16,384]{2,1,0:T(8,128)(2,1)S(1)}, u32[]{:S(2)}, u32[]{:S(2)}) %collective-permute-start.3) | collective-permute-done | bytes 233504 | tf_op jit(solution)/shard_map/ppermute | solution.py:482
  24.0 9.6 %finish.1 = bf16[16,8,8,128]{3,2,1,0:T(8,128)(2,1)S(1)} custom-call(bf16[19,16,384]{2,1,0:T(8,128)(2,1)S(1)} %collective-permute-done.2.left, bf16[19,16,384]{2,1,0:T(8,128)(2,1)S(1)} %collective-permute-done.3.right, bf16[19,16,384]{2,1,0:T(8,128)(2,1)S(1)} %collective-permute-done.top, bf16[19,16,384]{2,1,0:T(8,128)(2,1)S(1)} %collective-permute-done.1.bot, ...), custom_call_target="tpu_custom_call" | custom-call | flops 6115295232 | bytes 20971520 | tf_op jit(solution)/shard_map/finish/pallas_call | solution.py:491
  33.6 17.3 %all_to_all.5.mine = bf16[128,8,128]{2,1,0:T(8,128)(2,1)S(1)} all-to-all(bf16[128,8,128]{2,1,0:T(8,128)(2,1)S(1)} %bitcast.2), channel_id=1, replica_groups=mesh['ha'=16,'wa'=8] {'ha','wa'}, dimensions={0} | all-to-all | bytes 524288 | tf_op jit(solution)/shard_map/all_to_all | solution.py:507
  50.9 1.1 %collective-permute-start.4 = (bf16[128,8,128]{2,1,0:T(8,128)(2,1)S(1)}, bf16[128,8,128]{2,1,0:T(8,128)(2,1)S(1)}, u32[]{:S(2)}, u32[]{:S(2)}) collective-permute-start(bf16[128,8,128]{2,1,0:T(8,128)(2,1)S(1)} %all_to_all.5.mine), channel_id=1, source_target_pairs={{0,1},{1,0},{2,3},{3,2},{4,5},{5,4},{6,7},{7,6},{8,9},{9,8},{10,11... | collective-permute-start | bytes 786440 | tf_op jit(solution)/shard_map/ppermute | solution.py:509
  52.0 1.2 %collective-permute-done.4.theirs = bf16[128,8,128]{2,1,0:T(8,128)(2,1)S(1)} collective-permute-done((bf16[128,8,128]{2,1,0:T(8,128)(2,1)S(1)}, bf16[128,8,128]{2,1,0:T(8,128)(2,1)S(1)}, u32[]{:S(2)}, u32[]{:S(2)}) %collective-permute-start.4) | collective-permute-done | bytes 262176 | tf_op jit(solution)/shard_map/ppermute | solution.py:509
  53.1 0.7 %sum_patches.1 = bf16[128,128]{1,0:T(8,128)(2,1)} custom-call(bf16[128,8,128]{2,1,0:T(8,128)(2,1)S(1)} %all_to_all.5.mine, bf16[128,8,128]{2,1,0:T(8,128)(2,1)S(1)} %collective-permute-done.4.theirs, f32[8,128]{1,0:T(8,128)S(1)} %get-tuple-element.42.bias), custom_call_target="tpu_custom_call" | custom-call | tf_op jit(solution)/shard_map/sum_patches/pallas_call | solution.py:510
Async XLA Ops:
  1.8 14.0 %collective-permute-start = (bf16[19,16,384]{2,1,0:T(8,128)(2,1)S(1)}, bf16[19,16,384]{2,1,0:T(8,128)(2,1)S(1)}, u32[]{:S(2)}, u32[]{:S(2)}) collective-permute-start(bf16[19,16,384]{2,1,0:T(8,128)(2,1)S(1)} %get-tuple-element.25), channel_id=1, source_target_pairs={{0,8},{8,16},{16,24},{24,32},{32,40},{40,48},{48,56},{56,64},{64,7... | collective-permute-start | bytes 700424 | tf_op jit(solution)/shard_map/ppermute | solution.py:464
  4.0 11.8 %collective-permute-start.1 = (bf16[19,16,384]{2,1,0:T(8,128)(2,1)S(1)}, bf16[19,16,384]{2,1,0:T(8,128)(2,1)S(1)}, u32[]{:S(2)}, u32[]{:S(2)}) collective-permute-start(bf16[19,16,384]{2,1,0:T(8,128)(2,1)S(1)} %get-tuple-element.26), channel_id=1, source_target_pairs={{0,120},{8,0},{16,8},{24,16},{32,24},{40,32},{48,40},{56,48},{64,5... | collective-permute-start | bytes 700424 | tf_op jit(solution)/shard_map/ppermute | solution.py:465
  15.9 6.6 %collective-permute-start.2 = (bf16[19,16,384]{2,1,0:T(8,128)(2,1)S(1)}, bf16[19,16,384]{2,1,0:T(8,128)(2,1)S(1)}, u32[]{:S(2)}, u32[]{:S(2)}) collective-permute-start(bf16[19,16,384]{2,1,0:T(8,128)(2,1)S(1)} %get-tuple-element.30), channel_id=1, source_target_pairs={{0,1},{1,2},{2,3},{3,4},{4,5},{5,6},{6,7},{7,0},{8,9},{9,10},{10,1... | collective-permute-start | bytes 700424 | tf_op jit(solution)/shard_map/ppermute | solution.py:481
  18.5 5.5 %collective-permute-start.3 = (bf16[19,16,384]{2,1,0:T(8,128)(2,1)S(1)}, bf16[19,16,384]{2,1,0:T(8,128)(2,1)S(1)}, u32[]{:S(2)}, u32[]{:S(2)}) collective-permute-start(bf16[19,16,384]{2,1,0:T(8,128)(2,1)S(1)} %get-tuple-element.31), channel_id=1, source_target_pairs={{0,7},{1,0},{2,1},{3,2},{4,3},{5,4},{6,5},{7,6},{8,15},{9,8},{10,9... | collective-permute-start | bytes 700424 | tf_op jit(solution)/shard_map/ppermute | solution.py:482
  50.9 2.3 %collective-permute-start.4 = (bf16[128,8,128]{2,1,0:T(8,128)(2,1)S(1)}, bf16[128,8,128]{2,1,0:T(8,128)(2,1)S(1)}, u32[]{:S(2)}, u32[]{:S(2)}) collective-permute-start(bf16[128,8,128]{2,1,0:T(8,128)(2,1)S(1)} %all_to_all.5.mine), channel_id=1, source_target_pairs={{0,1},{1,0},{2,3},{3,2},{4,5},{5,4},{6,7},{7,6},{8,9},{9,8},{10,11... | collective-permute-start | bytes 786440 | tf_op jit(solution)/shard_map/ppermute | solution.py:509

commit v14 on v13

--- a/solution.py
+++ b/solution.py
@@ -9,7 +9,7 @@
 F32 = jnp.float32
 F, R, Q, C = 16, 4, 8, 384
 MSG = 19
-PITCH = 40
+PITCH = 36
 VM = pl.BlockSpec(memory_space=pltpu.VMEM)
 ANY = pl.BlockSpec(memory_space=pl.ANY)
 
@@ -176,12 +176,9 @@
             copy.start()
     acc[...] = jnp.zeros_like(acc)
 
-    def cells(h, _):
+    for h in range(R):
         c0, c1 = cached_row(cfw, h * 16, 0, Q)
         put(s1, (pl.ds(h * Q, Q),), own[pl.ds(h * Q, Q)].reshape(Q * F, C).astype(F32), c0, c1)
-        return 0
-
-    lax.fori_loop(0, R, cells, 0)
     for a in range(3):
         for copy in first[a]:
             copy.wait()

time: 54 us -> 53.9 us (level)
  transfers between devices with their start and end apart: 5 -> 5, of which waited for: 2 -> 2; matrix products, arithmetic and copies ran while one was open for 0% -> 0% of each run, Pallas kernels for 23% -> 22%
where the time goes in v14:
time: 53.9 us; the launch traced here: 53.8 us
  Pallas kernels  24.2 us (45%)
  blocking collectives  17.3 us (32%)
  starting transfers between devices  9.55 us (18%)
  waiting for transfers between devices  2.68 us (5%)
    all_to_all x1, blocking collectives, local(): lax.all_to_all(slots.reshape(F * 8, 8, 128), ('ha', 'wa'), 0, 0, tiled=True)  17.3 us
    pallas_call x1, Pallas kernels, local(): kernel(finish_kernel, [shape(F, 8, 8, 128)], [VM] * 13, [pltpu.VMEM((8, 4...  9.59 us
    pallas_call x1, Pallas kernels, local(): kernel(inner_kernel, [near(R + 2, Q + 2, F, C, dtype=F32), near(3, 9, C,...  8.09 us
    pallas_call x1, Pallas kernels, local(): kernel(rows_kernel, [near(R + 2, 4, F, C, dtype=F32), near(R + 2, 6, F, 3...  3.96 us
    ppermute x1, starting transfers between devices, local(): bot = lax.ppermute(lo, 'ha', around('ha', -1))  3.71 us
    ppermute x1, starting transfers between devices, local(): left = lax.ppermute(to_right, 'wa', around('wa', 1))  2.55 us
    ppermute x1, starting transfers between devices, local(): top = lax.ppermute(hi, 'ha', around('ha', 1))  2.19 us
    pallas_call x1, Pallas kernels, local(): kernel(first_kernel, [near(32, F, C), near(3, (F + 1) * PITCH, 128, dtype...  1.73 us
  transfers between devices with their start and end apart: 5, of which 2 were waited for; matrix products, arithmetic and copies ran while one was open for 0% of the time, Pallas kernels for 22%

profile of v14, /device:TPU:1, one launch (start us, length us, event | category | flops | bytes accessed | tf_op | source)
XLA Modules:
  0.0 53.8 jit_solution(8717796057287167559)
XLA Ops:
  0.0 1.7 %act_first.1 = (bf16[32,16,384]{2,1,0:T(8,128)(2,1)S(1)}, f32[3,612,128]{2,1,0:T(8,128)S(1)}, bf16[19,16,384]{2,1,0:T(8,128)(2,1)S(1)}, bf16[19,16,384]{2,1,0:T(...) custom-call(bf16[16,4,8,384]{3,2,1,0:T(8,128)(2,1)} %feat_h.1, ...), custom_call_target="tpu_custom_call" | custom-call | tf_op jit(solution)/shard_map/act_first/pallas_call | solution.py:443
  1.7 2.2 %collective-permute-start = (bf16[19,16,384]{2,1,0:T(8,128)(2,1)S(1)}, bf16[19,16,384]{2,1,0:T(8,128)(2,1)S(1)}, u32[]{:S(2)}, u32[]{:S(2)}) collective-permute-start(bf16[19,16,384]{2,1,0:T(8,128)(2,1)S(1)} %get-tuple-element.25), channel_id=1, source_target_pairs={{0,8},{8,16},{16,24},{24,32},{32,40},{40,48},{48,56},{56,64},{64,7... | collective-permute-start | bytes 700424 | tf_op jit(solution)/shard_map/ppermute | solution.py:461
  3.9 3.7 %collective-permute-start.1 = (bf16[19,16,384]{2,1,0:T(8,128)(2,1)S(1)}, bf16[19,16,384]{2,1,0:T(8,128)(2,1)S(1)}, u32[]{:S(2)}, u32[]{:S(2)}) collective-permute-start(bf16[19,16,384]{2,1,0:T(8,128)(2,1)S(1)} %get-tuple-element.26), channel_id=1, source_target_pairs={{0,120},{8,0},{16,8},{24,16},{32,24},{40,32},{48,40},{56,48},{64,5... | collective-permute-start | bytes 700424 | tf_op jit(solution)/shard_map/ppermute | solution.py:462
  7.6 8.1 %inner.1 = (f32[6,10,16,384]{3,2,1,0:T(8,128)S(1)}, bf16[3,9,384,384]{3,2,1,0:T(8,128)(2,1)S(1)}, bf16[3,9,384,384]{3,2,1,0:T(8,128)(2,1)S(1)}, bf16[288,1152]{1,0:T(8,128)(2,1)S(1)}) custom-call(bf16[32,16,384]{2,1,0:T(8,128)(2,1)S(1)} %get-tuple-element.24.own, f32[3,64,128]{2,1,0:T(8,128)S(1)} %get-tuple-element.27.cfw, bf16[3,3,3,384,384]{4,3,2,1,0:T(8,128)(2,1)} %w1.1, ...), custom_call_target="tpu_custom_call" | custom-call | flops 4076863488 | bytes 17825792 | tf_op jit(solution)/shard_map/inner/pallas_call | solution.py:464
  15.7 0.0 collective-permute-done.top
  15.8 0.0 collective-permute-done.1.bot
  15.8 0.1 pack_columns.1
  15.9 2.6 %collective-permute-start.2 = (bf16[19,16,384]{2,1,0:T(8,128)(2,1)S(1)}, bf16[19,16,384]{2,1,0:T(8,128)(2,1)S(1)}, u32[]{:S(2)}, u32[]{:S(2)}) collective-permute-start(bf16[19,16,384]{2,1,0:T(8,128)(2,1)S(1)} %get-tuple-element.30), channel_id=1, source_target_pairs={{0,1},{1,2},{2,3},{3,4},{4,5},{5,6},{6,7},{7,0},{8,9},{9,10},{10,1... | collective-permute-start | bytes 700424 | tf_op jit(solution)/shard_map/ppermute | solution.py:478
  18.4 0.0 collective-permute-start.3
  18.4 4.0 %rows.1 = (f32[6,4,16,384]{3,2,1,0:T(8,128)S(1)}, bf16[6,6,16,1152]{3,2,1,0:T(8,128)(2,1)S(1)}, bf16[32,16,384]{2,1,0:T(8,128)(2,1)S(1)}, bf16[4,1152,512]{2,1,0:T(8,128)(2,1)S(1)}) custom-call(bf16[19,16,384]{2,1,0:T(8,128)(2,1)S(1)} %collective-permute-done.top, bf16[19,16,384]{2,1,0:T(8,128)(2,1)S(1)} %collective-permute-done.1.bot, ...), custom_call_target="tpu_custom_call" | custom-call | flops 2038431744 | bytes 10485760 | tf_op jit(solution)/shard_map/rows/pallas_call | solution.py:480
  22.4 0.0 collective-permute-done.2.left
  22.4 1.5 %collective-permute-done.3.right = bf16[19,16,384]{2,1,0:T(8,128)(2,1)S(1)} collective-permute-done((bf16[19,16,384]{2,1,0:T(8,128)(2,1)S(1)}, bf16[19,16,384]{2,1,0:T(8,128)(2,1)S(1)}, u32[]{:S(2)}, u32[]{:S(2)}) %collective-permute-start.3) | collective-permute-done | bytes 233504 | tf_op jit(solution)/shard_map/ppermute | solution.py:479
  23.9 9.6 %finish.1 = bf16[16,8,8,128]{3,2,1,0:T(8,128)(2,1)S(1)} custom-call(bf16[19,16,384]{2,1,0:T(8,128)(2,1)S(1)} %collective-permute-done.2.left, bf16[19,16,384]{2,1,0:T(8,128)(2,1)S(1)} %collective-permute-done.3.right, bf16[19,16,384]{2,1,0:T(8,128)(2,1)S(1)} %collective-permute-done.top, bf16[19,16,384]{2,1,0:T(8,128)(2,1)S(1)} %collective-permute-done.1.bot, ...), custom_call_target="tpu_custom_call" | custom-call | flops 6115295232 | bytes 20971520 | tf_op jit(solution)/shard_map/finish/pallas_call | solution.py:488
  33.5 17.3 %all_to_all.5.mine = bf16[128,8,128]{2,1,0:T(8,128)(2,1)S(1)} all-to-all(bf16[128,8,128]{2,1,0:T(8,128)(2,1)S(1)} %bitcast.2), channel_id=1, replica_groups=mesh['ha'=16,'wa'=8] {'ha','wa'}, dimensions={0} | all-to-all | bytes 524288 | tf_op jit(solution)/shard_map/all_to_all | solution.py:504
  50.8 1.1 %collective-permute-start.4 = (bf16[128,8,128]{2,1,0:T(8,128)(2,1)S(1)}, bf16[128,8,128]{2,1,0:T(8,128)(2,1)S(1)}, u32[]{:S(2)}, u32[]{:S(2)}) collective-permute-start(bf16[128,8,128]{2,1,0:T(8,128)(2,1)S(1)} %all_to_all.5.mine), channel_id=1, source_target_pairs={{0,1},{1,0},{2,3},{3,2},{4,5},{5,4},{6,7},{7,6},{8,9},{9,8},{10,11... | collective-permute-start | bytes 786440 | tf_op jit(solution)/shard_map/ppermute | solution.py:506
  51.9 1.2 %collective-permute-done.4.theirs = bf16[128,8,128]{2,1,0:T(8,128)(2,1)S(1)} collective-permute-done((bf16[128,8,128]{2,1,0:T(8,128)(2,1)S(1)}, bf16[128,8,128]{2,1,0:T(8,128)(2,1)S(1)}, u32[]{:S(2)}, u32[]{:S(2)}) %collective-permute-start.4) | collective-permute-done | bytes 262176 | tf_op jit(solution)/shard_map/ppermute | solution.py:506
  53.1 0.7 %sum_patches.1 = bf16[128,128]{1,0:T(8,128)(2,1)} custom-call(bf16[128,8,128]{2,1,0:T(8,128)(2,1)S(1)} %all_to_all.5.mine, bf16[128,8,128]{2,1,0:T(8,128)(2,1)S(1)} %collective-permute-done.4.theirs, f32[8,128]{1,0:T(8,128)S(1)} %get-tuple-element.42.bias), custom_call_target="tpu_custom_call" | custom-call | tf_op jit(solution)/shard_map/sum_patches/pallas_call | solution.py:507
Async XLA Ops:
  1.7 14.0 %collective-permute-start = (bf16[19,16,384]{2,1,0:T(8,128)(2,1)S(1)}, bf16[19,16,384]{2,1,0:T(8,128)(2,1)S(1)}, u32[]{:S(2)}, u32[]{:S(2)}) collective-permute-start(bf16[19,16,384]{2,1,0:T(8,128)(2,1)S(1)} %get-tuple-element.25), channel_id=1, source_target_pairs={{0,8},{8,16},{16,24},{24,32},{32,40},{40,48},{48,56},{56,64},{64,7... | collective-permute-start | bytes 700424 | tf_op jit(solution)/shard_map/ppermute | solution.py:461
  3.9 11.8 %collective-permute-start.1 = (bf16[19,16,384]{2,1,0:T(8,128)(2,1)S(1)}, bf16[19,16,384]{2,1,0:T(8,128)(2,1)S(1)}, u32[]{:S(2)}, u32[]{:S(2)}) collective-permute-start(bf16[19,16,384]{2,1,0:T(8,128)(2,1)S(1)} %get-tuple-element.26), channel_id=1, source_target_pairs={{0,120},{8,0},{16,8},{24,16},{32,24},{40,32},{48,40},{56,48},{64,5... | collective-permute-start | bytes 700424 | tf_op jit(solution)/shard_map/ppermute | solution.py:462
  15.9 6.5 %collective-permute-start.2 = (bf16[19,16,384]{2,1,0:T(8,128)(2,1)S(1)}, bf16[19,16,384]{2,1,0:T(8,128)(2,1)S(1)}, u32[]{:S(2)}, u32[]{:S(2)}) collective-permute-start(bf16[19,16,384]{2,1,0:T(8,128)(2,1)S(1)} %get-tuple-element.30), channel_id=1, source_target_pairs={{0,1},{1,2},{2,3},{3,4},{4,5},{5,6},{6,7},{7,0},{8,9},{9,10},{10,1... | collective-permute-start | bytes 700424 | tf_op jit(solution)/shard_map/ppermute | solution.py:478
  18.4 5.5 %collective-permute-start.3 = (bf16[19,16,384]{2,1,0:T(8,128)(2,1)S(1)}, bf16[19,16,384]{2,1,0:T(8,128)(2,1)S(1)}, u32[]{:S(2)}, u32[]{:S(2)}) collective-permute-start(bf16[19,16,384]{2,1,0:T(8,128)(2,1)S(1)} %get-tuple-element.31), channel_id=1, source_target_pairs={{0,7},{1,0},{2,1},{3,2},{4,3},{5,4},{6,5},{7,6},{8,15},{9,8},{10,9... | collective-permute-start | bytes 700424 | tf_op jit(solution)/shard_map/ppermute | solution.py:479
  50.8 2.3 %collective-permute-start.4 = (bf16[128,8,128]{2,1,0:T(8,128)(2,1)S(1)}, bf16[128,8,128]{2,1,0:T(8,128)(2,1)S(1)}, u32[]{:S(2)}, u32[]{:S(2)}) collective-permute-start(bf16[128,8,128]{2,1,0:T(8,128)(2,1)S(1)} %all_to_all.5.mine), channel_id=1, source_target_pairs={{0,1},{1,0},{2,3},{3,2},{4,5},{5,4},{6,7},{7,6},{8,9},{9,8},{10,11... | collective-permute-start | bytes 786440 | tf_op jit(solution)/shard_map/ppermute | solution.py:506

commit v15 on v13

--- a/solution.py
+++ b/solution.py
@@ -313,7 +313,7 @@
     def one(b):
         return w2v[2, 3 * b : 3 * b + 3, :, 256:384].reshape(3 * C, 128)
 
-    half = R // 2
+    half = R
     size = half * Q * F
     side = [w2v[a, :, :, 256:384].reshape(9 * C, 128) for a in range(2)]
     for top_row in range(0, R, half):

time: 54 us -> 54.5 us (level)
  transfers between devices with their start and end apart: 5 -> 5, of which waited for: 2 -> 2; matrix products, arithmetic and copies ran while one was open for 0% -> 0% of each run, Pallas kernels for 23% -> 22%
where the time goes in v15:
time: 54.5 us; the launch traced here: 54.4 us
  Pallas kernels  24.8 us (46%)
  blocking collectives  17.3 us (32%)
  starting transfers between devices  9.54 us (18%)
  waiting for transfers between devices  2.61 us (5%)
    all_to_all x1, blocking collectives, local(): lax.all_to_all(slots.reshape(F * 8, 8, 128), ('ha', 'wa'), 0, 0, tiled=True)  17.3 us
    pallas_call x1, Pallas kernels, local(): kernel(finish_kernel, [shape(F, 8, 8, 128)], [VM] * 13, [pltpu.VMEM((8, 4...  10.1 us
    pallas_call x1, Pallas kernels, local(): kernel(inner_kernel, [near(R + 2, Q + 2, F, C, dtype=F32), near(3, 9, C,...  8.1 us
    pallas_call x1, Pallas kernels, local(): kernel(rows_kernel, [near(R + 2, 4, F, C, dtype=F32), near(R + 2, 6, F, 3...  4.03 us
    ppermute x1, starting transfers between devices, local(): bot = lax.ppermute(lo, 'ha', around('ha', -1))  3.71 us
    ppermute x1, starting transfers between devices, local(): left = lax.ppermute(to_right, 'wa', around('wa', 1))  2.54 us
    ppermute x1, starting transfers between devices, local(): top = lax.ppermute(hi, 'ha', around('ha', 1))  2.19 us
    pallas_call x1, Pallas kernels, local(): kernel(first_kernel, [near(32, F, C), near(3, (F + 1) * PITCH, 128, dtype...  1.79 us
  transfers between devices with their start and end apart: 5, of which 2 were waited for; matrix products, arithmetic and copies ran while one was open for 0% of the time, Pallas kernels for 22%

profile of v15, /device:TPU:1, one launch (start us, length us, event | category | flops | bytes accessed | tf_op | source)
XLA Modules:
  0.0 54.4 jit_solution(10929446310738851118)
XLA Ops:
  0.0 1.8 %act_first.1 = (bf16[32,16,384]{2,1,0:T(8,128)(2,1)S(1)}, f32[3,680,128]{2,1,0:T(8,128)S(1)}, bf16[19,16,384]{2,1,0:T(8,128)(2,1)S(1)}, bf16[19,16,384]{2,1,0:T(...) custom-call(bf16[16,4,8,384]{3,2,1,0:T(8,128)(2,1)} %feat_h.1, ...), custom_call_target="tpu_custom_call" | custom-call | tf_op jit(solution)/shard_map/act_first/pallas_call | solution.py:446
  1.8 2.2 %collective-permute-start = (bf16[19,16,384]{2,1,0:T(8,128)(2,1)S(1)}, bf16[19,16,384]{2,1,0:T(8,128)(2,1)S(1)}, u32[]{:S(2)}, u32[]{:S(2)}) collective-permute-start(bf16[19,16,384]{2,1,0:T(8,128)(2,1)S(1)} %get-tuple-element.25), channel_id=1, source_target_pairs={{0,8},{8,16},{16,24},{24,32},{32,40},{40,48},{48,56},{56,64},{64,7... | collective-permute-start | bytes 700424 | tf_op jit(solution)/shard_map/ppermute | solution.py:464
  4.0 3.7 %collective-permute-start.1 = (bf16[19,16,384]{2,1,0:T(8,128)(2,1)S(1)}, bf16[19,16,384]{2,1,0:T(8,128)(2,1)S(1)}, u32[]{:S(2)}, u32[]{:S(2)}) collective-permute-start(bf16[19,16,384]{2,1,0:T(8,128)(2,1)S(1)} %get-tuple-element.26), channel_id=1, source_target_pairs={{0,120},{8,0},{16,8},{24,16},{32,24},{40,32},{48,40},{56,48},{64,5... | collective-permute-start | bytes 700424 | tf_op jit(solution)/shard_map/ppermute | solution.py:465
  7.7 8.1 %inner.1 = (f32[6,10,16,384]{3,2,1,0:T(8,128)S(1)}, bf16[3,9,384,384]{3,2,1,0:T(8,128)(2,1)S(1)}, bf16[3,9,384,384]{3,2,1,0:T(8,128)(2,1)S(1)}, bf16[288,1152]{1,0:T(8,128)(2,1)S(1)}) custom-call(bf16[32,16,384]{2,1,0:T(8,128)(2,1)S(1)} %get-tuple-element.24.own, f32[3,64,128]{2,1,0:T(8,128)S(1)} %get-tuple-element.27.cfw, bf16[3,3,3,384,384]{4,3,2,1,0:T(8,128)(2,1)} %w1.1, ...), custom_call_target="tpu_custom_call" | custom-call | flops 4076863488 | bytes 17825792 | tf_op jit(solution)/shard_map/inner/pallas_call | solution.py:467
  15.8 0.0 collective-permute-done.top
  15.8 0.0 collective-permute-done.1.bot
  15.8 0.1 pack_columns.1
  15.9 2.5 %collective-permute-start.2 = (bf16[19,16,384]{2,1,0:T(8,128)(2,1)S(1)}, bf16[19,16,384]{2,1,0:T(8,128)(2,1)S(1)}, u32[]{:S(2)}, u32[]{:S(2)}) collective-permute-start(bf16[19,16,384]{2,1,0:T(8,128)(2,1)S(1)} %get-tuple-element.30), channel_id=1, source_target_pairs={{0,1},{1,2},{2,3},{3,4},{4,5},{5,6},{6,7},{7,0},{8,9},{9,10},{10,1... | collective-permute-start | bytes 700424 | tf_op jit(solution)/shard_map/ppermute | solution.py:481
  18.5 0.0 collective-permute-start.3
  18.5 4.0 %rows.1 = (f32[6,4,16,384]{3,2,1,0:T(8,128)S(1)}, bf16[6,6,16,1152]{3,2,1,0:T(8,128)(2,1)S(1)}, bf16[32,16,384]{2,1,0:T(8,128)(2,1)S(1)}, bf16[4,1152,512]{2,1,0:T(8,128)(2,1)S(1)}) custom-call(bf16[19,16,384]{2,1,0:T(8,128)(2,1)S(1)} %collective-permute-done.top, bf16[19,16,384]{2,1,0:T(8,128)(2,1)S(1)} %collective-permute-done.1.bot, ...), custom_call_target="tpu_custom_call" | custom-call | flops 2038431744 | bytes 10485760 | tf_op jit(solution)/shard_map/rows/pallas_call | solution.py:483
  22.5 0.0 collective-permute-done.2.left
  22.5 1.4 %collective-permute-done.3.right = bf16[19,16,384]{2,1,0:T(8,128)(2,1)S(1)} collective-permute-done((bf16[19,16,384]{2,1,0:T(8,128)(2,1)S(1)}, bf16[19,16,384]{2,1,0:T(8,128)(2,1)S(1)}, u32[]{:S(2)}, u32[]{:S(2)}) %collective-permute-start.3) | collective-permute-done | bytes 233504 | tf_op jit(solution)/shard_map/ppermute | solution.py:482
  24.0 10.1 %finish.1 = bf16[16,8,8,128]{3,2,1,0:T(8,128)(2,1)S(1)} custom-call(bf16[19,16,384]{2,1,0:T(8,128)(2,1)S(1)} %collective-permute-done.2.left, bf16[19,16,384]{2,1,0:T(8,128)(2,1)S(1)} %collective-permute-done.3.right, bf16[19,16,384]{2,1,0:T(8,128)(2,1)S(1)} %collective-permute-done.top, bf16[19,16,384]{2,1,0:T(8,128)(2,1)S(1)} %collective-permute-done.1.bot, ...), custom_call_target="tpu_custom_call" | custom-call | flops 6115295232 | bytes 20971520 | tf_op jit(solution)/shard_map/finish/pallas_call | solution.py:491
  34.1 17.3 %all_to_all.5.mine = bf16[128,8,128]{2,1,0:T(8,128)(2,1)S(1)} all-to-all(bf16[128,8,128]{2,1,0:T(8,128)(2,1)S(1)} %bitcast.2), channel_id=1, replica_groups=mesh['ha'=16,'wa'=8] {'ha','wa'}, dimensions={0} | all-to-all | bytes 524288 | tf_op jit(solution)/shard_map/all_to_all | solution.py:507
  51.4 1.1 %collective-permute-start.4 = (bf16[128,8,128]{2,1,0:T(8,128)(2,1)S(1)}, bf16[128,8,128]{2,1,0:T(8,128)(2,1)S(1)}, u32[]{:S(2)}, u32[]{:S(2)}) collective-permute-start(bf16[128,8,128]{2,1,0:T(8,128)(2,1)S(1)} %all_to_all.5.mine), channel_id=1, source_target_pairs={{0,1},{1,0},{2,3},{3,2},{4,5},{5,4},{6,7},{7,6},{8,9},{9,8},{10,11... | collective-permute-start | bytes 786440 | tf_op jit(solution)/shard_map/ppermute | solution.py:509
  52.5 1.2 %collective-permute-done.4.theirs = bf16[128,8,128]{2,1,0:T(8,128)(2,1)S(1)} collective-permute-done((bf16[128,8,128]{2,1,0:T(8,128)(2,1)S(1)}, bf16[128,8,128]{2,1,0:T(8,128)(2,1)S(1)}, u32[]{:S(2)}, u32[]{:S(2)}) %collective-permute-start.4) | collective-permute-done | bytes 262176 | tf_op jit(solution)/shard_map/ppermute | solution.py:509
  53.7 0.7 %sum_patches.1 = bf16[128,128]{1,0:T(8,128)(2,1)} custom-call(bf16[128,8,128]{2,1,0:T(8,128)(2,1)S(1)} %all_to_all.5.mine, bf16[128,8,128]{2,1,0:T(8,128)(2,1)S(1)} %collective-permute-done.4.theirs, f32[8,128]{1,0:T(8,128)S(1)} %get-tuple-element.42.bias), custom_call_target="tpu_custom_call" | custom-call | tf_op jit(solution)/shard_map/sum_patches/pallas_call | solution.py:510
Async XLA Ops:
  1.8 14.0 %collective-permute-start = (bf16[19,16,384]{2,1,0:T(8,128)(2,1)S(1)}, bf16[19,16,384]{2,1,0:T(8,128)(2,1)S(1)}, u32[]{:S(2)}, u32[]{:S(2)}) collective-permute-start(bf16[19,16,384]{2,1,0:T(8,128)(2,1)S(1)} %get-tuple-element.25), channel_id=1, source_target_pairs={{0,8},{8,16},{16,24},{24,32},{32,40},{40,48},{48,56},{56,64},{64,7... | collective-permute-start | bytes 700424 | tf_op jit(solution)/shard_map/ppermute | solution.py:464
  4.0 11.8 %collective-permute-start.1 = (bf16[19,16,384]{2,1,0:T(8,128)(2,1)S(1)}, bf16[19,16,384]{2,1,0:T(8,128)(2,1)S(1)}, u32[]{:S(2)}, u32[]{:S(2)}) collective-permute-start(bf16[19,16,384]{2,1,0:T(8,128)(2,1)S(1)} %get-tuple-element.26), channel_id=1, source_target_pairs={{0,120},{8,0},{16,8},{24,16},{32,24},{40,32},{48,40},{56,48},{64,5... | collective-permute-start | bytes 700424 | tf_op jit(solution)/shard_map/ppermute | solution.py:465
  15.9 6.6 %collective-permute-start.2 = (bf16[19,16,384]{2,1,0:T(8,128)(2,1)S(1)}, bf16[19,16,384]{2,1,0:T(8,128)(2,1)S(1)}, u32[]{:S(2)}, u32[]{:S(2)}) collective-permute-start(bf16[19,16,384]{2,1,0:T(8,128)(2,1)S(1)} %get-tuple-element.30), channel_id=1, source_target_pairs={{0,1},{1,2},{2,3},{3,4},{4,5},{5,6},{6,7},{7,0},{8,9},{9,10},{10,1... | collective-permute-start | bytes 700424 | tf_op jit(solution)/shard_map/ppermute | solution.py:481
  18.5 5.5 %collective-permute-start.3 = (bf16[19,16,384]{2,1,0:T(8,128)(2,1)S(1)}, bf16[19,16,384]{2,1,0:T(8,128)(2,1)S(1)}, u32[]{:S(2)}, u32[]{:S(2)}) collective-permute-start(bf16[19,16,384]{2,1,0:T(8,128)(2,1)S(1)} %get-tuple-element.31), channel_id=1, source_target_pairs={{0,7},{1,0},{2,1},{3,2},{4,3},{5,4},{6,5},{7,6},{8,15},{9,8},{10,9... | collective-permute-start | bytes 700424 | tf_op jit(solution)/shard_map/ppermute | solution.py:482
  51.4 2.3 %collective-permute-start.4 = (bf16[128,8,128]{2,1,0:T(8,128)(2,1)S(1)}, bf16[128,8,128]{2,1,0:T(8,128)(2,1)S(1)}, u32[]{:S(2)}, u32[]{:S(2)}) collective-permute-start(bf16[128,8,128]{2,1,0:T(8,128)(2,1)S(1)} %all_to_all.5.mine), channel_id=1, source_target_pairs={{0,1},{1,0},{2,3},{3,2},{4,5},{5,4},{6,7},{7,6},{8,9},{9,8},{10,11... | collective-permute-start | bytes 786440 | tf_op jit(solution)/shard_map/ppermute | solution.py:509
